TPU v7x, 32 devices: a whole 2x2x4 slice. The times are simulated.
32 devices in a mesh: groups: 2 (over y), seq: 4 (over z), tile: 4 (over x, core).
Axes of the slice: x: 2, y: 2, z: 4, core: 2. Of those that a mesh axis runs over, the one named last changes fastest.
Arguments:
- queries: bfloat16 [2048, 8192], P(('groups', 'tile', 'seq')), parts along dimension 0, may hold values from -5 to 5
- keys: bfloat16 [2048, 1024], P(('groups', 'tile', 'seq')), parts along dimension 0, may hold values from -5 to 5
- values: bfloat16 [2048, 1024], P(('groups', 'tile', 'seq')), parts along dimension 0, may hold values from -5 to 5
- block_lists: int32 [128, 8, 16], P(('groups', 'seq'), 'tile'), parts along dimension 0, may hold values from 0 to 7, as said below
- block_counts: int32 [128, 8], P(('groups', 'seq'), 'tile'), parts along dimension 0, may hold values from 1 to 8, as said below
Outputs:
- attended: bfloat16 [2048, 8192], P(('groups', 'tile', 'seq')), parts along dimension 0
There are 2 independent parts, one for each index of `groups`. A program takes and returns all parts, laid end to end along the dimension named above; each array names one. Nothing has to cross between parts.
Inputs may be any that keep to these rules, and one draw needn't show every extreme that they name: `block_lists`: slot 0 of tile q's list is q; slots 1 to block_counts - 1 hold distinct blocks below q; the later slots hold q and are unused. block_counts[h, q] is at most q + 1; some head reads every block in its last tile.
All inputs are finite; a program needn't handle non-finite values.
Results may differ from a plain program's by a relative error of at most 0.0038.
Values may be sent and summed in bfloat16 or wider, within the bound.
No kernel may reach another device: no remote copies, remote signals or barrier semaphores. Data moves between devices by JAX's collectives and lax.ppermute only.
A program may use at most 128 MiB of HBM per device.

v0:
```python
import jax
import jax.numpy as jnp
from jax import lax
from jax.sharding import PartitionSpec as P

HEAD_DIMENSION = 128
TILE_ROWS = 128
GROUP = 8


def attend(q_rows, block_table, block_total, sel_lists_all, sel_counts_all, tile_anchor):
    own_rows, heads_here, head_size = q_rows.shape
    tile_count = sel_lists_all.shape[1]
    slot_total = sel_lists_all.shape[2]
    score_scale = head_size ** (-0.5)
    group_size = 1
    while group_size * TILE_ROWS * heads_here < 512 and tile_count % (2 * group_size) == 0:
        group_size = group_size * 2
    heads_local = jnp.arange(heads_here) // GROUP
    slot_ids = jnp.arange(slot_total)
    key_pos = jnp.arange(TILE_ROWS)

    def one_group(group_id):
        tile_start = group_id * group_size
        q_block = lax.dynamic_slice_in_dim(
            q_rows, tile_start * TILE_ROWS, group_size * TILE_ROWS, 0
        )
        q_block = q_block.reshape(group_size, TILE_ROWS, heads_here, head_size)
        sel_lists = lax.dynamic_slice_in_dim(sel_lists_all, tile_start, group_size, 1)
        sel_counts = lax.dynamic_slice_in_dim(sel_counts_all, tile_start, group_size, 1)
        flat_ids = (heads_local[:, None, None] * block_total + sel_lists).reshape(-1)
        sel_blocks = jnp.take(block_table, flat_ids, axis=0)
        sel_blocks = sel_blocks.reshape(heads_here, group_size, slot_total, TILE_ROWS, 2, head_size)
        scores = (
            jnp.einsum(
                "gqhd,hgjkd->hgqjk",
                q_block,
                sel_blocks[..., 0, :],
                preferred_element_type=jnp.float32,
            )
            * score_scale
        )
        tile_ids = tile_anchor + tile_start + jnp.arange(group_size)
        slot_ok = (slot_ids[None, None, :] < sel_counts[:, :, None])[:, :, None, :, None]
        causal = (sel_lists != tile_ids[None, :, None])[:, :, None, :, None] | (
            key_pos[None, None, None, None, :] <= key_pos[None, None, :, None, None]
        )
        kept_mask = slot_ok & causal
        scores = jnp.where(kept_mask, scores, -1e30)
        row_max = jnp.max(scores, axis=(3, 4), keepdims=True)
        probs = jnp.where(kept_mask, jnp.exp(scores - row_max), 0.0)
        totals = jnp.sum(probs, axis=(3, 4))
        probs_low = probs.astype(jnp.bfloat16)
        mixed = jnp.einsum(
            "hgqjk,hgjkd->gqhd",
            probs_low,
            sel_blocks[..., 1, :],
            preferred_element_type=jnp.float32,
        )
        mixed = mixed / jnp.transpose(totals, (1, 2, 0))[..., None]
        return mixed.astype(jnp.bfloat16)

    attended = lax.map(one_group, jnp.arange(tile_count // group_size, dtype=jnp.int32))
    return attended.reshape(own_rows, heads_here * head_size)


def owner_copies(kv_pairs, owners, heads_here, kv_dev):
    tok_rows, kv_heads_all, pair_width = kv_pairs.shape
    if heads_here >= GROUP:
        return kv_pairs.reshape(tok_rows, owners, kv_dev * pair_width)
    repeats = GROUP // heads_here
    spread = jnp.broadcast_to(
        kv_pairs[:, :, None, :], (tok_rows, kv_heads_all, repeats, pair_width)
    )
    return spread.reshape(tok_rows, owners, kv_dev * pair_width)


def per_device(queries, keys, values, block_lists, block_counts):
    tok_rows = queries.shape[0]
    owners = lax.axis_size("seq")
    heads_here = block_lists.shape[0]
    kv_heads_all = keys.shape[1] // HEAD_DIMENSION
    kv_dev = max(1, heads_here // GROUP)
    q_send = queries.reshape(tok_rows, owners, heads_here * HEAD_DIMENSION)
    kv_pairs = jnp.concatenate(
        [
            keys.reshape(tok_rows, kv_heads_all, HEAD_DIMENSION),
            values.reshape(tok_rows, kv_heads_all, HEAD_DIMENSION),
        ],
        axis=2,
    )
    kv_send = owner_copies(kv_pairs, owners, heads_here, kv_dev)
    q_owned, kv_owned = (
        lax.all_to_all(q_send, "seq", split_axis=1, concat_axis=0, tiled=True),
        lax.all_to_all(kv_send, "seq", split_axis=1, concat_axis=0, tiled=True),
    )
    kv_whole = lax.all_gather(kv_owned, "tile", axis=0, tiled=True)
    key_value_blocks = kv_whole.reshape(-1, TILE_ROWS, kv_dev, 2 * HEAD_DIMENSION)
    block_total = key_value_blocks.shape[0]
    block_table = jnp.transpose(key_value_blocks, (2, 0, 1, 3)).reshape(
        kv_dev * block_total, TILE_ROWS * 2 * HEAD_DIMENSION
    )
    own_rows = q_owned.shape[0]
    q_rows = q_owned.reshape(own_rows, heads_here, HEAD_DIMENSION)
    tile_anchor = lax.axis_index("tile") * block_lists.shape[1]
    attended = attend(q_rows, block_table, block_total, block_lists, block_counts, tile_anchor)
    returned = lax.all_to_all(
        attended.reshape(own_rows, 1, heads_here * HEAD_DIMENSION),
        "seq",
        split_axis=0,
        concat_axis=1,
        tiled=True,
    )
    return returned.reshape(tok_rows, owners * heads_here * HEAD_DIMENSION)


def solution(mesh):
    in_specs = (
        P(("groups", "tile", "seq"), None),
        P(("groups", "tile", "seq"), None),
        P(("groups", "tile", "seq"), None),
        P(("groups", "seq"), "tile", None),
        P(("groups", "seq"), "tile"),
    )
    out_specs = P(("groups", "tile", "seq"), None)
    return jax.shard_map(
        per_device, mesh=mesh, in_specs=in_specs, out_specs=out_specs, check_vma=False
    )
```

profile of v0, /device:TPU:1, one launch (start us, length us, event | category | flops | bytes accessed | tf_op | source)
XLA Modules:
  0.0 302.6 jit_solution(9113288122064490250)
XLA Ops:
  6.5 0.9 copy.52
  7.5 0.9 copy.53
  8.6 0.7 copy.31
  9.4 5.4 %all-to-all-start = ((bf16[64,4,512]{2,0,1:T(8,128)(2,1)}), bf16[64,4,512]{2,0,1:T(8,128)(2,1)S(1)}, u32[]{:S(2)}, u32[]{:S(2)}) async-start(bf16[64,4,512]{2,0,1:T(8,128)(2,1)} %copy.31), calls=%async_computation | async-start | bytes 524288 | tf_op jit(solution)/shard_map/all_to_all | solution.py:95
  14.8 2.3 copy.64
  17.1 5.2 %all-to-all-done = bf16[64,4,512]{2,0,1:T(8,128)(2,1)S(1)} async-done(((bf16[64,4,512]{2,0,1:T(8,128)(2,1)}), bf16[64,4,512]{2,0,1:T(8,128)(2,1)S(1)}, u32[]{:S(2)}, u32[]{:S(2)}) %all-to-all-start) | async-done | bytes 262176 | tf_op jit(solution)/shard_map/all_to_all | solution.py:95
  22.3 3.5 %all-to-all-start.1 = ((bf16[64,4,2048]{2,0,1:T(8,128)(2,1)}), bf16[64,4,2048]{2,0,1:T(8,128)(2,1)S(1)}, u32[]{:S(2)}, u32[]{:S(2)}) async-start(bf16[64,4,2048]{2,0,1:T(8,128)(2,1)} %bitcast.90), calls=%async_computation.1 | async-start | bytes 2097152 | tf_op jit(solution)/shard_map/all_to_all | solution.py:94
  26.6 24.4 %all-to-all-done.1 = bf16[64,4,2048]{2,0,1:T(8,128)(2,1)S(1)} async-done(((bf16[64,4,2048]{2,0,1:T(8,128)(2,1)}), bf16[64,4,2048]{2,0,1:T(8,128)(2,1)S(1)}, u32[]{:S(2)}, u32[]{:S(2)}) %all-to-all-start.1) | async-done | bytes 1048608 | tf_op jit(solution)/shard_map/all_to_all | solution.py:94
  51.3 1.3 reshape.217
  53.4 197.2 %while.11 = (s32[]{:T(128)}, bf16[2,1,128,16,128]{4,3,2,0,1:T(8,128)(2,1)}, s32[2]{0:T(128)S(1)}, s32[16,2,16]{2,1,0:T(2,128)}, bf16[16,32768]{1,0:T(8,128)(2,1)...) while((s32[]{:T(128)}, ...), condition=%wide.region_3.4_spmd.clone, body=%wide.region_0.3_spmd.clone.sunk | while | flops 2236104704 | bytes 172092496 | solution.py:63
  56.0 0.7 constant_dynamic-slice_fusion.5
  56.9 17.2 %gather_fusion = bf16[256,32768]{1,0:T(8,128)(2,1)} fusion(bf16[16,32768]{1,0:T(8,128)(2,1)S(1)} %get-tuple-element.222, s32[1024]{0:T(1024)S(1)} %pad_clamp_fusion.2), kind=kCustom, calls=%fused_computation.clone.clone.1 | custom fusion | bytes 33555456 | tf_op jit(solution)/shard_map/while/body/eval_jaxpr/jit(_take)/gather | solution.py:32
  74.1 27.4 %gather.13 = bf16[16,1,16,128,2,128]{5,4,3,2,0,1:T(2,128)(2,1)} reshape(bf16[256,32768]{1,0:T(8,128)(2,1)} %gather_fusion) | data formatting | bytes 33554432 | tf_op jit(solution)/shard_map/while/body/eval_jaxpr/jit(_take)/gather | solution.py:32
  101.5 16.6 %copy_select_fusion.2 = bf16[16,1,16,128,2,128]{5,3,2,0,4,1:T(8,128)(2,1)} fusion(bf16[16,1,16,128,2,128]{5,4,3,2,0,1:T(2,128)(2,1)} %gather.13, pred[16,16]{1,0:T(8,128)(4,1)S(1)} %get-tuple-element.189), kind=kLoop, calls=%fused_computation.4.clone.1 | loop fusion | flops 8388608 | bytes 33554688 | tf_op jit(solution)/shard_map/while/body/eval_jaxpr/jit(_take)/select_n | solution.py:32
  119.5 9.8 %fusion.33 = (f32[16,128]{1,0:T(8,128)S(1)}, f32[16,128,16,128]{1,3,2,0:T(8,128)}) fusion(pred[128,128]{0,1:T(8,128)(4,1)S(1)} %iota_compare_fusion.4, pred[16,16]{1,0:T(8,128)(4,1)S(1)} %compare_bitcast_fusion.2, pred[16,16]{1,0:T(8,128)(4,1)S(1)} %iota_compare_fusion.5, bf16[16,1,16,128,2,128]{5,3,2,0,4,1:T(8,128)(2,1)} %copy_select_fusion.2, ...), kind=kOutput, calls=%fused_computation.8.clone.1 | convolution fusion | flops 1094711296 | bytes 25715200 | tf_op jit(solution)/shard_map/while/body/eval_jaxpr/gqhd,hgjkd->hgqjk/dot_general | solution.py:35
  129.4 9.3 %fusion.34 = f32[16,128]{1,0:T(8,128)S(1)} fusion(f32[16,128]{1,0:T(8,128)S(1)} %get-tuple-element.190, f32[16,128,16,128]{1,3,2,0:T(8,128)} %get-tuple-element.191, pred[128,128]{0,1:T(8,128)(4,1)S(1)} %iota_compare_fusion.4, pred[16,16]{1,0:T(8,128)(4,1)S(1)} %compare_bitcast_fusion.2, pred[16,16]{1,0:T(8,128)(4,1)S(1)} %iota_compare_fusion.5), kind=kLoop, calls=%fused_computation.14.clone.1 | loop fusion | flops 29358080 | bytes 16810496 | tf_op jit(solution)/shard_map/while/body/eval_jaxpr/reduce_sum | solution.py:52
  138.7 12.1 %fusion.35 = bf16[1,1,128,16,128]{2,4,3,1,0:T(8,128)(2,1)S(1)} fusion(f32[16,128]{1,0:T(8,128)S(1)} %get-tuple-element.190, f32[16,128,16,128]{1,3,2,0:T(8,128)} %get-tuple-element.191, pred[128,128]{0,1:T(8,128)(4,1)S(1)} %iota_compare_fusion.4, pred[16,16]{1,0:T(8,128)(4,1)S(1)} %compare_bitcast_fusion.2, ...), kind=kOutput, calls=%fused_computation.17.clone.1 | convolution fusion | flops 1103626240 | bytes 25723392 | tf_op jit(solution)/shard_map/while/body/eval_jaxpr/hgqjk,hgjkd->gqhd/dot_general | solution.py:54
  151.2 0.8 constant_dynamic-update-slice_fusion.2
  155.5 17.2 %gather_fusion = bf16[256,32768]{1,0:T(8,128)(2,1)} fusion(bf16[16,32768]{1,0:T(8,128)(2,1)S(1)} %get-tuple-element.222, s32[1024]{0:T(1024)S(1)} %pad_clamp_fusion.2), kind=kCustom, calls=%fused_computation.clone.clone.1 | custom fusion | bytes 33555456 | tf_op jit(solution)/shard_map/while/body/eval_jaxpr/jit(_take)/gather | solution.py:32
  172.7 27.4 %gather.13 = bf16[16,1,16,128,2,128]{5,4,3,2,0,1:T(2,128)(2,1)} reshape(bf16[256,32768]{1,0:T(8,128)(2,1)} %gather_fusion) | data formatting | bytes 33554432 | tf_op jit(solution)/shard_map/while/body/eval_jaxpr/jit(_take)/gather | solution.py:32
  200.1 16.6 %copy_select_fusion.2 = bf16[16,1,16,128,2,128]{5,3,2,0,4,1:T(8,128)(2,1)} fusion(bf16[16,1,16,128,2,128]{5,4,3,2,0,1:T(2,128)(2,1)} %gather.13, pred[16,16]{1,0:T(8,128)(4,1)S(1)} %get-tuple-element.189), kind=kLoop, calls=%fused_computation.4.clone.1 | loop fusion | flops 8388608 | bytes 33554688 | tf_op jit(solution)/shard_map/while/body/eval_jaxpr/jit(_take)/select_n | solution.py:32
  218.1 9.8 %fusion.33 = (f32[16,128]{1,0:T(8,128)S(1)}, f32[16,128,16,128]{1,3,2,0:T(8,128)}) fusion(pred[128,128]{0,1:T(8,128)(4,1)S(1)} %iota_compare_fusion.4, pred[16,16]{1,0:T(8,128)(4,1)S(1)} %compare_bitcast_fusion.2, pred[16,16]{1,0:T(8,128)(4,1)S(1)} %iota_compare_fusion.5, bf16[16,1,16,128,2,128]{5,3,2,0,4,1:T(8,128)(2,1)} %copy_select_fusion.2, ...), kind=kOutput, calls=%fused_computation.8.clone.1 | convolution fusion | flops 1094711296 | bytes 25715200 | tf_op jit(solution)/shard_map/while/body/eval_jaxpr/gqhd,hgjkd->hgqjk/dot_general | solution.py:35
  227.9 9.3 %fusion.34 = f32[16,128]{1,0:T(8,128)S(1)} fusion(f32[16,128]{1,0:T(8,128)S(1)} %get-tuple-element.190, f32[16,128,16,128]{1,3,2,0:T(8,128)} %get-tuple-element.191, pred[128,128]{0,1:T(8,128)(4,1)S(1)} %iota_compare_fusion.4, pred[16,16]{1,0:T(8,128)(4,1)S(1)} %compare_bitcast_fusion.2, pred[16,16]{1,0:T(8,128)(4,1)S(1)} %iota_compare_fusion.5), kind=kLoop, calls=%fused_computation.14.clone.1 | loop fusion | flops 29358080 | bytes 16810496 | tf_op jit(solution)/shard_map/while/body/eval_jaxpr/reduce_sum | solution.py:52
  237.3 12.1 %fusion.35 = bf16[1,1,128,16,128]{2,4,3,1,0:T(8,128)(2,1)S(1)} fusion(f32[16,128]{1,0:T(8,128)S(1)} %get-tuple-element.190, f32[16,128,16,128]{1,3,2,0:T(8,128)} %get-tuple-element.191, pred[128,128]{0,1:T(8,128)(4,1)S(1)} %iota_compare_fusion.4, pred[16,16]{1,0:T(8,128)(4,1)S(1)} %compare_bitcast_fusion.2, ...), kind=kOutput, calls=%fused_computation.17.clone.1 | convolution fusion | flops 1103626240 | bytes 25723392 | tf_op jit(solution)/shard_map/while/body/eval_jaxpr/hgqjk,hgjkd->gqhd/dot_general | solution.py:54
  249.8 0.8 constant_dynamic-update-slice_fusion.2
  250.6 5.8 %reshape_reshape.4 = bf16[256,1,2048]{2,1,0:T(2,128)(2,1)S(1)} reshape(bf16[2,1,128,16,128]{4,3,2,0,1:T(8,128)(2,1)} %get-tuple-element.62) | data formatting | bytes 2097152 | tf_op jit(solution)/shard_map/reshape;reshape | solution.py:108
  256.9 6.8 %reduce.4 = bf16[256,2048]{1,0:T(8,128)(2,1)S(1)} reduce(bf16[256,1,2048]{2,1,0:T(2,128)(2,1)S(1)} %reshape_reshape.4, bf16[]{:T(256)} %broadcast.146), dimensions={1}, to_apply=%reshape_reshape.4.reduce_sub_computation | reduce | bytes 2097154 | tf_op jit(solution)/shard_map/reshape;reshape | solution.py:108
  263.7 0.8 reshape.218
  264.5 27.3 %all_to_all.48 = bf16[4,2,65536]{2,1,0:T(2,128)(2,1)S(1)} all-to-all(bf16[4,2,65536]{2,1,0:T(2,128)(2,1)S(1)} %reshape.218), channel_id=1, replica_groups=mesh['groups'=2,'seq'=4,'tile'=4] {'seq'}, dimensions={0} | all-to-all | bytes 2097152 | tf_op jit(solution)/shard_map/all_to_all | solution.py:107
  291.8 0.9 reshape.219
  293.4 0.8 copy.39
  294.2 1.6 copy.56
  (43 shorter events, 6.5 us)
Async XLA Ops:
  9.4 13.0 %all-to-all-start = ((bf16[64,4,512]{2,0,1:T(8,128)(2,1)}), bf16[64,4,512]{2,0,1:T(8,128)(2,1)S(1)}, u32[]{:S(2)}, u32[]{:S(2)}) async-start(bf16[64,4,512]{2,0,1:T(8,128)(2,1)} %copy.31), calls=%async_computation | async-start | bytes 524288 | tf_op jit(solution)/shard_map/all_to_all | solution.py:95
  22.3 3.6 %copy-start = (bf16[64,4,512]{2,0,1:T(8,128)(2,1)}, bf16[64,4,512]{2,0,1:T(8,128)(2,1)S(1)}, u32[]{:S(2)}) copy-start(bf16[64,4,512]{2,0,1:T(8,128)(2,1)S(1)} %all-to-all-done) | copy-start | bytes 786436
  22.3 28.7 %all-to-all-start.1 = ((bf16[64,4,2048]{2,0,1:T(8,128)(2,1)}), bf16[64,4,2048]{2,0,1:T(8,128)(2,1)S(1)}, u32[]{:S(2)}, u32[]{:S(2)}) async-start(bf16[64,4,2048]{2,0,1:T(8,128)(2,1)} %bitcast.90), calls=%async_computation.1 | async-start | bytes 2097152 | tf_op jit(solution)/shard_map/all_to_all | solution.py:94
  25.9 25.4 %all-gather.2.cloned.1.call-start = ((), (), s32[]{:S(2)}) async-start(), calls=%async_computation.3 | async-start | bytes 1310720 | tf_op jit(solution)/shard_map/all_gather | solution.py:97
  101.5 17.9 %copy-start.1 = (s32[16,2]{0,1:T(2,128)S(1)}, s32[16,2]{0,1:T(2,128)}, u32[]{:S(2)}) copy-start(s32[16,2]{0,1:T(2,128)} %get-tuple-element.223) | copy-start | bytes 388 | tf_op jit(solution)/shard_map/while
  200.1 17.9 %copy-start.1 = (s32[16,2]{0,1:T(2,128)S(1)}, s32[16,2]{0,1:T(2,128)}, u32[]{:S(2)}) copy-start(s32[16,2]{0,1:T(2,128)} %get-tuple-element.223) | copy-start | bytes 388 | tf_op jit(solution)/shard_map/while
Sparse Core Ops, SparseCore 0:
  28.3 20.1 all-gather.1
where the time goes:
time: 307 us; the launch traced here: 303 us
  local copies, waits for them, and re-layouts  113 us (37%)
  other arithmetic  59 us (19%)
  matrix products  43.8 us (14%)
  waiting for transfers between devices  30.3 us (10%)
  blocking collectives  27.3 us (9%)
  between operations  13.5 us (4%)
  starting transfers between devices  8.98 us (3%)
  loops' own time  6.51 us (2%)
    gather x4, local copies, waits for them, and re-layouts, one_group(): sel_blocks = jnp.take(block_table, flat_ids, axis=0)  89.2 us
    select_n x4, other arithmetic, one_group(): sel_blocks = jnp.take(block_table, flat_ids, axis=0)  33.2 us
    all_to_all x1, blocking collectives, per_device(): lax.all_to_all(attended.reshape(own_rows, 1, heads_here * HEAD_DIMENSION)...  27.3 us
    all_to_all x1, waiting for transfers between devices, per_device(): lax.all_to_all(q_send, 'seq', split_axis=1, concat_axis=0, tiled=True)  24.4 us
    dot_general x2, matrix products, one_group(): jnp.einsum('hgqjk,hgjkd->gqhd', probs_low, sel_blocks[..., 1, :], preferr...  24.2 us
    dot_general x2, matrix products, one_group(): jnp.einsum('gqhd,hgjkd->hgqjk', q_block, sel_blocks[..., 0, :], preferred...  19.6 us
    reduce_sum x2, other arithmetic, one_group(): totals = jnp.sum(probs, axis=(3, 4))  18.7 us
    another operation x1, other arithmetic, per_device(): attended.reshape(own_rows, 1, heads_here * HEAD_DIMENSION)  6.79 us
  transfers between devices with their start and end apart: 3, of which 2 were waited for; matrix products, arithmetic and copies ran while one was open for 1% of the time, Pallas kernels for 0%

commit v1 on v0

--- a/solution.py
+++ b/solution.py
@@ -1,7 +1,11 @@
+import functools
+
 import jax
 import jax.numpy as jnp
 from jax import lax
-from jax.sharding import PartitionSpec as P
+from jax.experimental import pallas as pl
+from jax.experimental.pallas import tpu as pltpu
+from jax.sharding import Mesh, PartitionSpec as P
 
 HEAD_DIMENSION = 128
 TILE_ROWS = 128
@@ -114,15 +118,200 @@
     return returned.reshape(tok_rows, owners * heads_here * HEAD_DIMENSION)
 
 
+DROP = -1e30
+LOG2E = 1.4426950408889634
+
+
+def ring_steps(z_size):
+    chips = 2 * z_size
+    places = [(0, p) if p < z_size else (1, chips - 1 - p) for p in range(chips)]
+
+    def device(place, core):
+        x, z = places[place % chips]
+        return (z * 2 + x) * 2 + core
+
+    ahead = [(device(p, 0), device(p + 1, 0)) for p in range(chips)]
+    ahead += [(device(p, 1), device(p - 1, 1)) for p in range(chips)]
+    back = [(device(p, 0), device(p - 1, 0)) for p in range(chips)]
+    back += [(device(p, 1), device(p + 1, 1)) for p in range(chips)]
+    return ahead, back
+
+
+def ring_kernel(z_size, heads, *refs):
+    chips = 2 * z_size
+    reach = z_size - 1
+    units = refs[2 : 3 + 2 * reach]
+    q_own, q_other = refs[0], refs[1]
+    k_far, v_far, out_own, out_other, k_aug, v_aug, q_aug, picks = refs[3 + 2 * reach :]
+    rows = q_own.shape[0]
+    kv_heads = heads // GROUP
+    width = HEAD_DIMENSION
+    unit_rows = 2 * rows
+    x, z, core = lax.axis_index("x"), lax.axis_index("seq"), lax.axis_index("core")
+    place = jnp.where(x == 0, z, chips - 1 - z)
+    turn = 1 - 2 * core
+
+    def chunk_of(place_from, core_from):
+        place_from = lax.rem(place_from + 2 * chips, chips)
+        x_from = jnp.where(place_from < z_size, 0, 1)
+        z_from = jnp.where(place_from < z_size, place_from, chips - 1 - place_from)
+        return (2 * x_from + core_from) * z_size + z_from
+
+    sources = [place]
+    sources += [place - step * turn for step in range(1, reach + 1)]
+    sources += [place + step * turn for step in range(1, reach + 1)]
+    sources += [place + z_size]
+    lane = lax.broadcasted_iota(jnp.int32, (rows, width), 1)
+    for slot in range(chips):
+        for half in range(2):
+            mark = jnp.where(lane == chunk_of(sources[slot], jnp.where(half == 0, core, 1 - core)), 1.0, 0.0)
+            mark = mark.astype(jnp.bfloat16)
+            at = slot * unit_rows + half * rows
+            for head in range(kv_heads):
+                k_aug[head, at : at + rows, width:] = mark
+    ones = jnp.ones((chips * unit_rows, width), jnp.bfloat16)
+    for head in range(kv_heads):
+        v_aug[head, :, width:] = ones
+        columns = slice(head * width, (head + 1) * width)
+        for slot in range(chips):
+            at = slice(slot * unit_rows, (slot + 1) * unit_rows)
+            if slot < chips - 1:
+                k_aug[head, at, :width] = units[slot][:unit_rows, columns]
+                v_aug[head, at, :width] = units[slot][unit_rows : 2 * unit_rows, columns]
+            else:
+                k_aug[head, at, :width] = k_far[:, columns]
+                v_aug[head, at, :width] = v_far[:, columns]
+    for slot in range(chips - 1):
+        picks[slot * 16 : slot * 16 + 16, :] = units[slot][2 * unit_rows :, :]
+
+    def slot_of(z_from):
+        place_from = jnp.where(x == 0, z_from, chips - 1 - z_from)
+        away = lax.rem((place - place_from) * turn + 2 * chips, chips)
+        return jnp.where(away < z_size, away, reach + chips - away)
+
+    key_at = lax.broadcasted_iota(jnp.int32, (rows, unit_rows), 1)
+    row_at = lax.broadcasted_iota(jnp.int32, (rows, unit_rows), 0)
+    lane_row = lax.broadcasted_iota(jnp.int32, (1, width), 1)
+    lists_from = heads // 16
+    factor = jnp.float32(width**-0.5 * LOG2E)
+    for side in (1, 0):
+        here = jnp.where(side == 0, core, 1 - core)
+        causal = jnp.where(lane_row > chunk_of(place, here), DROP, 0.0)
+        key_off = key_at - side * rows
+        corner = jnp.where((key_off >= 0) & (key_off < rows) & (key_off > row_at), DROP, 0.0)
+        corner = jnp.concatenate([corner] * GROUP, axis=0)
+        out = out_own if side == 0 else out_other
+        column = pl.multiple_of((side * 2 + z // 2) * width, width)
+        for head in range(kv_heads):
+            for member in range(GROUP):
+                local = head * GROUP + member
+                slot = slot_of(core * lists_from + local // 16)
+                tile = picks[pl.ds(pl.multiple_of(slot * 16, 16), 16), pl.ds(column, width)]
+                bias = tile.astype(jnp.float32)[local % 16 : local % 16 + 1, :] + causal
+                at = slice(member * rows, (member + 1) * rows)
+                if side == 0:
+                    q_from = pl.multiple_of((core * heads + local) * width, width)
+                    q_aug[at, :width] = q_own[:, pl.ds(q_from, width)]
+                else:
+                    q_aug[at, :width] = q_other[:, local * width : (local + 1) * width]
+                q_aug[at, width:] = jnp.broadcast_to(bias, (rows, width)).astype(jnp.bfloat16)
+            scores = lax.dot_general(
+                q_aug[...], k_aug[head], (((1,), (1,)), ((), ())), preferred_element_type=jnp.float32
+            )
+            scores = jnp.concatenate([scores[:, :unit_rows] + corner, scores[:, unit_rows:]], axis=1)
+            row_max = jnp.max(scores, axis=1, keepdims=True)
+            probs = jnp.exp2((scores - row_max) * factor).astype(jnp.bfloat16)
+            mixed = jnp.dot(probs, v_aug[head], preferred_element_type=jnp.float32)
+            result = (mixed[:, :width] / mixed[:, width:]).astype(jnp.bfloat16)
+            for member in range(GROUP):
+                local = head * GROUP + member
+                out[:, local * width : (local + 1) * width] = result[member * rows : (member + 1) * rows]
+
+
+def per_device_ring(z_size, queries, keys, values, block_lists, block_counts):
+    rows = queries.shape[0]
+    core = lax.axis_index("core")
+    half = keys.shape[1] // 2
+    heads = queries.shape[1] // HEAD_DIMENSION // 2
+    swap = [(0, 1), (1, 0)]
+    ahead, back = ring_steps(z_size)
+    axes = ("seq", "x", "core")
+
+    own = core * half
+    other = half - own
+    lane = jnp.arange(HEAD_DIMENSION) // 2
+    slots = jnp.arange(block_lists.shape[2])
+    used = (block_lists[..., None] == lane) & (slots < block_counts[..., None])[..., None]
+    picks = jnp.where(jnp.any(used, axis=2), 0.0, DROP).astype(jnp.bfloat16)
+    picks = picks.reshape(picks.shape[0], 2 * HEAD_DIMENSION)
+    sent = jnp.concatenate(
+        [
+            lax.dynamic_slice_in_dim(keys, other, half, 1),
+            lax.dynamic_slice_in_dim(values, other, half, 1),
+            jnp.concatenate([picks, picks], axis=1),
+        ],
+        axis=0,
+    )
+    got = lax.ppermute(sent, "core", swap)
+    unit = jnp.concatenate(
+        [
+            lax.dynamic_slice_in_dim(keys, own, half, 1),
+            got[:rows],
+            lax.dynamic_slice_in_dim(values, own, half, 1),
+            got[rows : 2 * rows],
+            jnp.concatenate([picks, got[2 * rows :, : 2 * HEAD_DIMENSION]], axis=1),
+        ],
+        axis=0,
+    )
+    q_width = heads * HEAD_DIMENSION
+    q_other = lax.ppermute(
+        lax.dynamic_slice_in_dim(queries, q_width - core * q_width, q_width, 1), "core", swap
+    )
+    one, two, first, second = unit, unit, [], []
+    for _ in range(z_size - 1):
+        one = lax.ppermute(one, axes, ahead)
+        two = lax.ppermute(two, axes, back)
+        first.append(one)
+        second.append(two)
+    unit_rows = 2 * rows
+    k_far = lax.ppermute(one[:unit_rows], axes, ahead)
+    v_far = lax.ppermute(two[unit_rows : 2 * unit_rows], axes, back)
+    chips = 2 * z_size
+    kv_heads = heads // GROUP
+    out_shape = jax.ShapeDtypeStruct((rows, q_width), jnp.bfloat16)
+    kept, away = pl.pallas_call(
+        functools.partial(ring_kernel, z_size, heads),
+        out_shape=(out_shape, out_shape),
+        scratch_shapes=[
+            pltpu.VMEM((kv_heads, chips * unit_rows, 2 * HEAD_DIMENSION), jnp.bfloat16),
+            pltpu.VMEM((kv_heads, chips * unit_rows, 2 * HEAD_DIMENSION), jnp.bfloat16),
+            pltpu.VMEM((GROUP * rows, 2 * HEAD_DIMENSION), jnp.bfloat16),
+            pltpu.VMEM((chips * 16, half), jnp.bfloat16),
+        ],
+        compiler_params=pltpu.CompilerParams(vmem_limit_bytes=40 * 2**20),
+        name="attend",
+    )(queries, q_other, unit, *first, *second, k_far, v_far)
+    back_home = lax.ppermute(away, "core", swap)
+    return jnp.where(
+        core == 0,
+        jnp.concatenate([kept, back_home], axis=1),
+        jnp.concatenate([back_home, kept], axis=1),
+    )
+
+
 def solution(mesh):
+    groups, z_size, tiles = (mesh.shape[a] for a in ("groups", "seq", "tile"))
+    if tiles == 4 and z_size == 4:
+        fine = Mesh(mesh.devices.reshape(groups, z_size, 2, 2), ("groups", "seq", "x", "core"))
+        step, tile, on = functools.partial(per_device_ring, z_size), ("x", "core"), fine
+    else:
+        step, tile, on = per_device, ("tile",), mesh
+    rows = P(("groups",) + tile + ("seq",), None)
     in_specs = (
-        P(("groups", "tile", "seq"), None),
-        P(("groups", "tile", "seq"), None),
-        P(("groups", "tile", "seq"), None),
-        P(("groups", "seq"), "tile", None),
-        P(("groups", "seq"), "tile"),
-    )
-    out_specs = P(("groups", "tile", "seq"), None)
-    return jax.shard_map(
-        per_device, mesh=mesh, in_specs=in_specs, out_specs=out_specs, check_vma=False
-    )
+        rows,
+        rows,
+        rows,
+        P(("groups", "seq"), tile, None),
+        P(("groups", "seq"), tile),
+    )
+    return jax.shard_map(step, mesh=on, in_specs=in_specs, out_specs=rows, check_vma=False)

time: 307 us -> 48.2 us (0.16); the launches traced: 303 us -> 47.6 us
  local copies, waits for them, and re-layouts: 113 us -> 2.69 us
  other arithmetic: 59 us -> 2.27 us
  matrix products: 43.8 us -> 0 us
  blocking collectives: 27.3 us -> 0 us
  between operations: 13.5 us -> 0.1 us
  waiting for transfers between devices: 30.3 us -> 22.3 us
  loops' own time: 6.51 us -> 0 us
  Pallas kernels: 0 us -> 6.29 us
  starting transfers between devices: 8.98 us -> 14 us
    gather x4 -> x0, local copies, waits for them, and re-layouts: 89.2 us -> none  [one_group(): sel_blocks = jnp.take(block_table, flat_ids, axis=0)]
    dot_general x4 -> x0, matrix products: 43.8 us -> none  [the longest x2 24.2 us: one_group(): jnp.einsum('hgqjk,hgjkd->gqhd', probs_low, sel_blocks[..., 1, :], preferr...]
    select_n x4 -> x2, other arithmetic: 33.2 us -> 1.21 us  [the longest x1 1.21 us: per_device_ring(): jnp.where(core == 0, jnp.concatenate([kept, back_home], axis=1), jnp.conc...]
    all_to_all x2 -> x0, waiting for transfers between devices: 29.6 us -> none  [the longest x1 24.4 us: per_device(): lax.all_to_all(q_send, 'seq', split_axis=1, concat_axis=0, tiled=True)]
    all_to_all x1 -> x0, blocking collectives: 27.3 us -> none  [per_device(): lax.all_to_all(attended.reshape(own_rows, 1, heads_here * HEAD_DIMENSION)...]
    ppermute x0 -> x11, waiting for transfers between devices: none -> 22.3 us  [the longest x3 9.8 us: per_device_ring(): two = lax.ppermute(two, axes, back)]
    reduce_sum x2 -> x0, other arithmetic: 18.7 us -> none  [one_group(): totals = jnp.sum(probs, axis=(3, 4))]
    ppermute x0 -> x11, starting transfers between devices: none -> 14 us  [the longest x3 6.89 us: per_device_ring(): two = lax.ppermute(two, axes, back)]
  transfers between devices with their start and end apart: 3 -> 11, of which waited for: 2 -> 8; matrix products, arithmetic and copies ran while one was open for 1% -> 0% of each run, Pallas kernels for 0% -> 0%
where the time goes in v1:
time: 48.2 us; the launch traced here: 47.6 us
  waiting for transfers between devices  22.3 us (46%)
  starting transfers between devices  14 us (29%)
  Pallas kernels  6.29 us (13%)
  local copies, waits for them, and re-layouts  2.69 us (6%)
  other arithmetic  2.27 us (5%)
    ppermute x3, waiting for transfers between devices, per_device_ring(): two = lax.ppermute(two, axes, back)  9.8 us
    ppermute x3, starting transfers between devices, per_device_ring(): two = lax.ppermute(two, axes, back)  6.89 us
    pallas_call x1, Pallas kernels, per_device_ring(): pl.pallas_call(functools.partial(ring_kernel, z_size, heads), out_shape=(...  6.29 us
    ppermute x3, waiting for transfers between devices, per_device_ring(): one = lax.ppermute(one, axes, ahead)  5.82 us
    ppermute x1, waiting for transfers between devices, per_device_ring(): k_far = lax.ppermute(one[:unit_rows], axes, ahead)  3.78 us
    ppermute x1, starting transfers between devices, per_device_ring(): back_home = lax.ppermute(away, 'core', swap)  3.35 us
    ppermute x1, starting transfers between devices, per_device_ring(): lax.ppermute(lax.dynamic_slice_in_dim(queries, q_width - core * q_width,...  1.87 us
    unnamed x7, local copies, waits for them, and re-layouts  1.71 us
  transfers between devices with their start and end apart: 11, of which 8 were waited for; matrix products, arithmetic and copies ran while one was open for 0% of the time, Pallas kernels for 0%

profile of v1, /device:TPU:1, one launch (start us, length us, event | category | flops | bytes accessed | tf_op | source)
XLA Modules:
  0.0 47.6 jit_solution(6256305441916183115)
XLA Ops:
  0.0 0.0 copy-start
  0.0 0.8 %copy.7 = s32[16,2]{1,0:T(8,128)S(1)} copy(s32[16,2]{0,1:T(2,128)} %param.9) | data formatting | bytes 256 | tf_op args[4]
  0.8 0.1 iota_compare_fusion
  0.9 0.9 %and_reduce_fusion = pred[16,2,128]{2,1,0:T(4,128)(4,1)S(1)} fusion(s32[128]{0:T(128)S(1)} %and_select_fusion, s32[16,2,16]{2,1,0:T(2,128)} %param.8, pred[16,2,16]{2,1,0:T(4,128)(4,1)S(1)} %iota_compare_fusion), kind=kLoop, calls=%fused_computation.1 | loop fusion | flops 192512 | bytes 7168 | tf_op jit(solution)/shard_map/reduce_or | solution.py:245
  1.9 0.9 %constant_dynamic-slice_fusion.1 = (bf16[64,512]{1,0:T(8,128)(2,1)S(1)}, bf16[272,512]{1,0:T(8,128)(2,1)S(1)}, bf16[64,512]{1,0:T(8,128)(2,1)S(1)}) fusion(bf16[64,1024]{1,0:T(8,128)(2,1)} %param.6, s32[]{:T(128)S(6)} %select_n.37, s32[]{:T(128)S(6)} %select_n.36, bf16[64,1024]{1,0:T(8,128)(2,1)} %param.7), kind=kLoop, calls=%fused_computation.13 | loop fusion | bytes 393224 | tf_op jit(solution)/shard_map/dynamic_slice | solution.py:249
  2.9 0.1 collective-permute-start.1
  3.0 1.3 %collective-permute-done.1 = bf16[144,512]{1,0:T(8,128)(2,1)S(1)} collective-permute-done((bf16[144,512]{1,0:T(8,128)(2,1)S(1)}, bf16[144,512]{1,0:T(8,128)(2,1)S(1)}, u32[]{:S(2)}, u32[]{:S(2)}) %collective-permute-start.1) | collective-permute-done | bytes 147488 | tf_op jit(solution)/shard_map/ppermute | solution.py:255
  4.3 0.8 %dynamic-slice_dynamic-update-slice_fusion = bf16[272,512]{1,0:T(8,128)(2,1)S(1)} fusion(bf16[272,512]{1,0:T(8,128)(2,1)S(1)} %slice_dynamic-update-slice_fusion.1, bf16[64,1024]{1,0:T(8,128)(2,1)} %param.7, s32[]{:T(128)S(6)} %select_n.36), kind=kLoop, calls=%fused_computation.5 | loop fusion | bytes 131076
  5.2 2.5 %collective-permute-start.5 = (bf16[272,512]{1,0:T(8,128)(2,1)S(1)}, bf16[272,512]{1,0:T(8,128)(2,1)S(1)}, u32[]{:S(2)}, u32[]{:S(2)}) collective-permute-start(bf16[272,512]{1,0:T(8,128)(2,1)S(1)} %maximum_dynamic-update-slice_fusion.refs_2_), channel_id=1, source_target_pairs={{0,2},{4,0},{8,4},{12,8},{14,12},{10,14},{6,10},{2,6},{1,5},{5,9},... | collective-permute-start | bytes 835592 | tf_op jit(solution)/shard_map/ppermute | solution.py:273
  7.7 0.0 collective-permute-start.2
  7.7 5.6 %collective-permute-done.5.refs_6_ = bf16[272,512]{1,0:T(8,128)(2,1)S(1)} collective-permute-done((bf16[272,512]{1,0:T(8,128)(2,1)S(1)}, bf16[272,512]{1,0:T(8,128)(2,1)S(1)}, u32[]{:S(2)}, u32[]{:S(2)}) %collective-permute-start.5) | collective-permute-done | bytes 278560 | tf_op jit(solution)/shard_map/ppermute | solution.py:273
  13.3 2.2 %collective-permute-start.6 = (bf16[272,512]{1,0:T(8,128)(2,1)S(1)}, bf16[272,512]{1,0:T(8,128)(2,1)S(1)}, u32[]{:S(2)}, u32[]{:S(2)}) collective-permute-start(bf16[272,512]{1,0:T(8,128)(2,1)S(1)} %collective-permute-done.5.refs_6_), channel_id=1, source_target_pairs={{0,2},{4,0},{8,4},{12,8},{14,12},{10,14},{6,10},{2,6},{1,5},{5,9},... | collective-permute-start | bytes 835592 | tf_op jit(solution)/shard_map/ppermute | solution.py:273
  15.5 0.0 collective-permute-done.2.refs_3_
  15.5 0.2 collective-permute-start.3
  15.7 0.0 copy-done
  15.7 1.9 %collective-permute-start = (bf16[64,4096]{1,0:T(8,128)(2,1)S(1)}, bf16[64,4096]{1,0:T(8,128)(2,1)S(1)}, u32[]{:S(2)}, u32[]{:S(2)}) collective-permute-start(bf16[64,4096]{1,0:T(8,128)(2,1)S(1)} %constant_dynamic-slice_fusion.2), channel_id=1, source_target_pairs={{0,1},{1,0},{2,3},{3,2},{4,5},{5,4},{6,7},{7,6},{8,9},{9,8},{10,11... | collective-permute-start | bytes 1572872 | tf_op jit(solution)/shard_map/ppermute | solution.py:267
  17.6 2.2 %collective-permute-done.6.refs_7_ = bf16[272,512]{1,0:T(8,128)(2,1)S(1)} collective-permute-done((bf16[272,512]{1,0:T(8,128)(2,1)S(1)}, bf16[272,512]{1,0:T(8,128)(2,1)S(1)}, u32[]{:S(2)}, u32[]{:S(2)}) %collective-permute-start.6) | collective-permute-done | bytes 278560 | tf_op jit(solution)/shard_map/ppermute | solution.py:273
  19.7 2.2 %collective-permute-start.7 = (bf16[272,512]{1,0:T(8,128)(2,1)S(1)}, bf16[272,512]{1,0:T(8,128)(2,1)S(1)}, u32[]{:S(2)}, u32[]{:S(2)}) collective-permute-start(bf16[272,512]{1,0:T(8,128)(2,1)S(1)} %collective-permute-done.6.refs_7_), channel_id=1, source_target_pairs={{0,2},{4,0},{8,4},{12,8},{14,12},{10,14},{6,10},{2,6},{1,5},{5,9},... | collective-permute-start | bytes 835592 | tf_op jit(solution)/shard_map/ppermute | solution.py:273
  21.9 1.9 %collective-permute-done.3.refs_4_ = bf16[272,512]{1,0:T(8,128)(2,1)S(1)} collective-permute-done((bf16[272,512]{1,0:T(8,128)(2,1)S(1)}, bf16[272,512]{1,0:T(8,128)(2,1)S(1)}, u32[]{:S(2)}, u32[]{:S(2)}) %collective-permute-start.3) | collective-permute-done | bytes 278560 | tf_op jit(solution)/shard_map/ppermute | solution.py:272
  23.8 0.0 collective-permute-start.4
  23.8 2.0 %collective-permute-done.7.refs_8_ = bf16[272,512]{1,0:T(8,128)(2,1)S(1)} collective-permute-done((bf16[272,512]{1,0:T(8,128)(2,1)S(1)}, bf16[272,512]{1,0:T(8,128)(2,1)S(1)}, u32[]{:S(2)}, u32[]{:S(2)}) %collective-permute-start.7) | collective-permute-done | bytes 278560 | tf_op jit(solution)/shard_map/ppermute | solution.py:273
  25.9 1.5 %collective-permute-start.9 = (bf16[128,512]{1,0:T(8,128)(2,1)S(1)}, bf16[128,512]{1,0:T(8,128)(2,1)S(1)}, u32[]{:S(2)}, u32[]{:S(2)}) collective-permute-start(bf16[128,512]{1,0:T(8,128)(2,1)S(1)} %slice.24), channel_id=1, source_target_pairs={{0,2},{4,0},{8,4},{12,8},{14,12},{10,14},{6,10},{2,6},{1,5},{5,9},... | collective-permute-start | bytes 393224 | tf_op jit(solution)/shard_map/ppermute | solution.py:278
  27.4 3.9 %collective-permute-done.4.refs_5_ = bf16[272,512]{1,0:T(8,128)(2,1)S(1)} collective-permute-done((bf16[272,512]{1,0:T(8,128)(2,1)S(1)}, bf16[272,512]{1,0:T(8,128)(2,1)S(1)}, u32[]{:S(2)}, u32[]{:S(2)}) %collective-permute-start.4) | collective-permute-done | bytes 278560 | tf_op jit(solution)/shard_map/ppermute | solution.py:272
  31.3 0.1 collective-permute-start.8
  31.4 0.0 collective-permute-done.refs_1_
  31.4 0.0 collective-permute-done.9.refs_10_
  31.4 3.8 %collective-permute-done.8.refs_9_ = bf16[128,512]{1,0:T(8,128)(2,1)S(1)} collective-permute-done((bf16[128,512]{1,0:T(8,128)(2,1)S(1)}, bf16[128,512]{1,0:T(8,128)(2,1)S(1)}, u32[]{:S(2)}, u32[]{:S(2)}) %collective-permute-start.8) | collective-permute-done | bytes 131104 | tf_op jit(solution)/shard_map/ppermute | solution.py:277
  35.2 6.3 %attend.1 = (bf16[64,4096]{1,0:T(8,128)(2,1)S(1)}, bf16[64,4096]{1,0:T(8,128)(2,1)S(1)}) custom-call(bf16[64,8192]{1,0:T(8,128)(2,1)S(1)} %copy-done, bf16[64,4096]{1,0:T(8,128)(2,1)S(1)} %collective-permute-done.refs_1_, bf16[272,512]{1,0:T(8,128)(2,1)S(1)} %maximum_dynamic-update-slice_fusion.refs_2_, bf16[272,512]{1,0:T(8,128)(2,1)S(1)} %collective-permute-done.2.refs_3_, ...), custom_call_target="tpu_custom_call" | custom-call | tf_op jit(solution)/shard_map/attend/pallas_call | solution.py:282
  41.5 3.4 %collective-permute-start.10 = (bf16[64,4096]{1,0:T(8,128)(2,1)S(1)}, bf16[64,4096]{1,0:T(8,128)(2,1)S(1)}, u32[]{:S(2)}, u32[]{:S(2)}) collective-permute-start(bf16[64,4096]{1,0:T(8,128)(2,1)S(1)} %get-tuple-element.8), channel_id=1, source_target_pairs={{0,1},{1,0},{2,3},{3,2},{4,5},{5,4},{6,7},{7,6},{8,9},{9,8},{10,11... | collective-permute-start | bytes 1572872 | tf_op jit(solution)/shard_map/ppermute | solution.py:294
  44.8 1.5 %collective-permute-done.10 = bf16[64,4096]{1,0:T(8,128)(2,1)S(1)} collective-permute-done((bf16[64,4096]{1,0:T(8,128)(2,1)S(1)}, bf16[64,4096]{1,0:T(8,128)(2,1)S(1)}, u32[]{:S(2)}, u32[]{:S(2)}) %collective-permute-start.10) | collective-permute-done | bytes 524320 | tf_op jit(solution)/shard_map/ppermute | solution.py:294
  46.4 1.2 %maximum_select_fusion = bf16[64,8192]{1,0:T(8,128)(2,1)} fusion(bf16[64,4096]{1,0:T(8,128)(2,1)S(1)} %collective-permute-done.10, bf16[64,4096]{1,0:T(8,128)(2,1)S(1)} %get-tuple-element.7, pred[]{:T(512)S(6)} %eq.16), kind=kLoop, calls=%fused_computation | loop fusion | flops 4718592 | bytes 2097153 | tf_op jit(solution)/shard_map/jit(_where)/select_n | solution.py:295
  (11 shorter events, 0.1 us)
Async XLA Ops:
  0.0 15.7 %copy-start = (bf16[64,8192]{1,0:T(8,128)(2,1)S(1)}, bf16[64,8192]{1,0:T(8,128)(2,1)}, u32[]{:S(2)}) copy-start(bf16[64,8192]{1,0:T(8,128)(2,1)} %refs_0_.1) | copy-start | bytes 3145732
  2.9 1.4 %collective-permute-start.1 = (bf16[144,512]{1,0:T(8,128)(2,1)S(1)}, bf16[144,512]{1,0:T(8,128)(2,1)S(1)}, u32[]{:S(2)}, u32[]{:S(2)}) collective-permute-start(bf16[144,512]{1,0:T(8,128)(2,1)S(1)} %maximum_maximum_fusion), channel_id=1, source_target_pairs={{0,1},{1,0},{2,3},{3,2},{4,5},{5,4},{6,7},{7,6},{8,9},{9,8},{10,11... | collective-permute-start | bytes 442376 | tf_op jit(solution)/shard_map/ppermute | solution.py:255
  5.2 8.1 %collective-permute-start.5 = (bf16[272,512]{1,0:T(8,128)(2,1)S(1)}, bf16[272,512]{1,0:T(8,128)(2,1)S(1)}, u32[]{:S(2)}, u32[]{:S(2)}) collective-permute-start(bf16[272,512]{1,0:T(8,128)(2,1)S(1)} %maximum_dynamic-update-slice_fusion.refs_2_), channel_id=1, source_target_pairs={{0,2},{4,0},{8,4},{12,8},{14,12},{10,14},{6,10},{2,6},{1,5},{5,9},... | collective-permute-start | bytes 835592 | tf_op jit(solution)/shard_map/ppermute | solution.py:273
  7.7 7.8 %collective-permute-start.2 = (bf16[272,512]{1,0:T(8,128)(2,1)S(1)}, bf16[272,512]{1,0:T(8,128)(2,1)S(1)}, u32[]{:S(2)}, u32[]{:S(2)}) collective-permute-start(bf16[272,512]{1,0:T(8,128)(2,1)S(1)} %maximum_dynamic-update-slice_fusion.refs_2_), channel_id=1, source_target_pairs={{0,4},{4,8},{8,12},{12,14},{14,10},{10,6},{6,2},{2,0},{1,3},{5,1},... | collective-permute-start | bytes 835592 | tf_op jit(solution)/shard_map/ppermute | solution.py:272
  13.3 6.4 %collective-permute-start.6 = (bf16[272,512]{1,0:T(8,128)(2,1)S(1)}, bf16[272,512]{1,0:T(8,128)(2,1)S(1)}, u32[]{:S(2)}, u32[]{:S(2)}) collective-permute-start(bf16[272,512]{1,0:T(8,128)(2,1)S(1)} %collective-permute-done.5.refs_6_), channel_id=1, source_target_pairs={{0,2},{4,0},{8,4},{12,8},{14,12},{10,14},{6,10},{2,6},{1,5},{5,9},... | collective-permute-start | bytes 835592 | tf_op jit(solution)/shard_map/ppermute | solution.py:273
  15.5 8.3 %collective-permute-start.3 = (bf16[272,512]{1,0:T(8,128)(2,1)S(1)}, bf16[272,512]{1,0:T(8,128)(2,1)S(1)}, u32[]{:S(2)}, u32[]{:S(2)}) collective-permute-start(bf16[272,512]{1,0:T(8,128)(2,1)S(1)} %collective-permute-done.2.refs_3_), channel_id=1, source_target_pairs={{0,4},{4,8},{8,12},{12,14},{14,10},{10,6},{6,2},{2,0},{1,3},{5,1},... | collective-permute-start | bytes 835592 | tf_op jit(solution)/shard_map/ppermute | solution.py:272
  15.7 15.7 %collective-permute-start = (bf16[64,4096]{1,0:T(8,128)(2,1)S(1)}, bf16[64,4096]{1,0:T(8,128)(2,1)S(1)}, u32[]{:S(2)}, u32[]{:S(2)}) collective-permute-start(bf16[64,4096]{1,0:T(8,128)(2,1)S(1)} %constant_dynamic-slice_fusion.2), channel_id=1, source_target_pairs={{0,1},{1,0},{2,3},{3,2},{4,5},{5,4},{6,7},{7,6},{8,9},{9,8},{10,11... | collective-permute-start | bytes 1572872 | tf_op jit(solution)/shard_map/ppermute | solution.py:267
  19.7 6.2 %collective-permute-start.7 = (bf16[272,512]{1,0:T(8,128)(2,1)S(1)}, bf16[272,512]{1,0:T(8,128)(2,1)S(1)}, u32[]{:S(2)}, u32[]{:S(2)}) collective-permute-start(bf16[272,512]{1,0:T(8,128)(2,1)S(1)} %collective-permute-done.6.refs_7_), channel_id=1, source_target_pairs={{0,2},{4,0},{8,4},{12,8},{14,12},{10,14},{6,10},{2,6},{1,5},{5,9},... | collective-permute-start | bytes 835592 | tf_op jit(solution)/shard_map/ppermute | solution.py:273
  23.8 7.5 %collective-permute-start.4 = (bf16[272,512]{1,0:T(8,128)(2,1)S(1)}, bf16[272,512]{1,0:T(8,128)(2,1)S(1)}, u32[]{:S(2)}, u32[]{:S(2)}) collective-permute-start(bf16[272,512]{1,0:T(8,128)(2,1)S(1)} %collective-permute-done.3.refs_4_), channel_id=1, source_target_pairs={{0,4},{4,8},{8,12},{12,14},{14,10},{10,6},{6,2},{2,0},{1,3},{5,1},... | collective-permute-start | bytes 835592 | tf_op jit(solution)/shard_map/ppermute | solution.py:272
  25.9 5.5 %collective-permute-start.9 = (bf16[128,512]{1,0:T(8,128)(2,1)S(1)}, bf16[128,512]{1,0:T(8,128)(2,1)S(1)}, u32[]{:S(2)}, u32[]{:S(2)}) collective-permute-start(bf16[128,512]{1,0:T(8,128)(2,1)S(1)} %slice.24), channel_id=1, source_target_pairs={{0,2},{4,0},{8,4},{12,8},{14,12},{10,14},{6,10},{2,6},{1,5},{5,9},... | collective-permute-start | bytes 393224 | tf_op jit(solution)/shard_map/ppermute | solution.py:278
  31.3 3.9 %collective-permute-start.8 = (bf16[128,512]{1,0:T(8,128)(2,1)S(1)}, bf16[128,512]{1,0:T(8,128)(2,1)S(1)}, u32[]{:S(2)}, u32[]{:S(2)}) collective-permute-start(bf16[128,512]{1,0:T(8,128)(2,1)S(1)} %slice.23), channel_id=1, source_target_pairs={{0,4},{4,8},{8,12},{12,14},{14,10},{10,6},{6,2},{2,0},{1,3},{5,1},... | collective-permute-start | bytes 393224 | tf_op jit(solution)/shard_map/ppermute | solution.py:277
  41.5 4.9 %collective-permute-start.10 = (bf16[64,4096]{1,0:T(8,128)(2,1)S(1)}, bf16[64,4096]{1,0:T(8,128)(2,1)S(1)}, u32[]{:S(2)}, u32[]{:S(2)}) collective-permute-start(bf16[64,4096]{1,0:T(8,128)(2,1)S(1)} %get-tuple-element.8), channel_id=1, source_target_pairs={{0,1},{1,0},{2,3},{3,2},{4,5},{5,4},{6,7},{7,6},{8,9},{9,8},{10,11... | collective-permute-start | bytes 1572872 | tf_op jit(solution)/shard_map/ppermute | solution.py:294

commit v2 on v1

--- a/solution.py
+++ b/solution.py
@@ -137,52 +137,63 @@
     return ahead, back
 
 
-def ring_kernel(z_size, heads, *refs):
+def chip_place(z_size):
+    x, z = lax.axis_index("x"), lax.axis_index("seq")
+    return jnp.where(x == 0, z, 2 * z_size - 1 - z)
+
+
+def chunk_of(z_size, place, core):
+    chips = 2 * z_size
+    place = lax.rem(place + 2 * chips, chips)
+    x = jnp.where(place < z_size, 0, 1)
+    z = jnp.where(place < z_size, place, chips - 1 - place)
+    return (2 * x + core) * z_size + z
+
+
+def fill_keys(z_size, rows, k_aug, v_aug, at, place, keys, values):
+    width = HEAD_DIMENSION
+    core = lax.axis_index("core")
+    lane = lax.broadcasted_iota(jnp.int32, (rows, width), 1)
+    for half in range(2):
+        chunk = chunk_of(z_size, place, core if half == 0 else 1 - core)
+        mark = jnp.where(lane == chunk, 1.0, 0.0).astype(jnp.bfloat16)
+        for head in range(k_aug.shape[0]):
+            k_aug[head, at + half * rows : at + (half + 1) * rows, width:] = mark
+    ones = jnp.ones((2 * rows, width), jnp.bfloat16)
+    for head in range(k_aug.shape[0]):
+        columns = slice(head * width, (head + 1) * width)
+        k_aug[head, at : at + 2 * rows, :width] = keys[:, columns]
+        v_aug[head, at : at + 2 * rows, :width] = values[:, columns]
+        v_aug[head, at : at + 2 * rows, width:] = ones
+
+
+def factor():
+    return jnp.float32(HEAD_DIMENSION**-0.5 * LOG2E)
+
+
+def near_kernel(z_size, heads, *refs):
     chips = 2 * z_size
     reach = z_size - 1
+    q_own, q_other = refs[:2]
     units = refs[2 : 3 + 2 * reach]
-    q_own, q_other = refs[0], refs[1]
-    k_far, v_far, out_own, out_other, k_aug, v_aug, q_aug, picks = refs[3 + 2 * reach :]
+    q_aug, total, top, k_aug, v_aug, lists = refs[3 + 2 * reach :]
     rows = q_own.shape[0]
-    kv_heads = heads // GROUP
     width = HEAD_DIMENSION
     unit_rows = 2 * rows
+    list_rows = units[0].shape[0] - 2 * unit_rows
+    slot_total = 16
     x, z, core = lax.axis_index("x"), lax.axis_index("seq"), lax.axis_index("core")
-    place = jnp.where(x == 0, z, chips - 1 - z)
+    place = chip_place(z_size)
     turn = 1 - 2 * core
-
-    def chunk_of(place_from, core_from):
-        place_from = lax.rem(place_from + 2 * chips, chips)
-        x_from = jnp.where(place_from < z_size, 0, 1)
-        z_from = jnp.where(place_from < z_size, place_from, chips - 1 - place_from)
-        return (2 * x_from + core_from) * z_size + z_from
 
     sources = [place]
     sources += [place - step * turn for step in range(1, reach + 1)]
     sources += [place + step * turn for step in range(1, reach + 1)]
-    sources += [place + z_size]
-    lane = lax.broadcasted_iota(jnp.int32, (rows, width), 1)
-    for slot in range(chips):
-        for half in range(2):
-            mark = jnp.where(lane == chunk_of(sources[slot], jnp.where(half == 0, core, 1 - core)), 1.0, 0.0)
-            mark = mark.astype(jnp.bfloat16)
-            at = slot * unit_rows + half * rows
-            for head in range(kv_heads):
-                k_aug[head, at : at + rows, width:] = mark
-    ones = jnp.ones((chips * unit_rows, width), jnp.bfloat16)
-    for head in range(kv_heads):
-        v_aug[head, :, width:] = ones
-        columns = slice(head * width, (head + 1) * width)
-        for slot in range(chips):
-            at = slice(slot * unit_rows, (slot + 1) * unit_rows)
-            if slot < chips - 1:
-                k_aug[head, at, :width] = units[slot][:unit_rows, columns]
-                v_aug[head, at, :width] = units[slot][unit_rows : 2 * unit_rows, columns]
-            else:
-                k_aug[head, at, :width] = k_far[:, columns]
-                v_aug[head, at, :width] = v_far[:, columns]
-    for slot in range(chips - 1):
-        picks[slot * 16 : slot * 16 + 16, :] = units[slot][2 * unit_rows :, :]
+    for slot, unit in enumerate(units):
+        keys, values = unit[:unit_rows, :], unit[unit_rows : 2 * unit_rows, :]
+        fill_keys(z_size, rows, k_aug, v_aug, slot * unit_rows, sources[slot], keys, values)
+        at = slice(slot * list_rows, (slot + 1) * list_rows)
+        lists[at, :] = unit[2 * unit_rows :, :width].astype(jnp.float32)
 
     def slot_of(z_from):
         place_from = jnp.where(x == 0, z_from, chips - 1 - z_from)
@@ -191,44 +202,79 @@
 
     key_at = lax.broadcasted_iota(jnp.int32, (rows, unit_rows), 1)
     row_at = lax.broadcasted_iota(jnp.int32, (rows, unit_rows), 0)
-    lane_row = lax.broadcasted_iota(jnp.int32, (1, width), 1)
-    lists_from = heads // 16
-    factor = jnp.float32(width**-0.5 * LOG2E)
+    lane = lax.broadcasted_iota(jnp.int32, (list_rows, width), 1)
+    block = (lane // 2).astype(jnp.float32)
+    spans = heads // list_rows
     for side in (1, 0):
-        here = jnp.where(side == 0, core, 1 - core)
-        causal = jnp.where(lane_row > chunk_of(place, here), DROP, 0.0)
+        here = core if side == 0 else 1 - core
+        causal = jnp.where(lane > chunk_of(z_size, place, here), DROP, 0.0)
+        biases = []
+        for span in range(spans):
+            slot = slot_of(core * spans + span)
+            tile = lists[pl.ds(pl.multiple_of(slot * list_rows, list_rows), list_rows), :]
+            hit = jnp.zeros((list_rows, width), jnp.float32)
+            for entry in range(slot_total):
+                base = side * 2 * slot_total + entry
+                picked = jnp.where(
+                    z < z_size // 2,
+                    tile[:, base : base + 1],
+                    tile[:, base + slot_total : base + slot_total + 1],
+                )
+                hit = jnp.maximum(hit, jnp.where(picked == block, 1.0, 0.0))
+            biases.append(jnp.where(hit > 0.0, 0.0, DROP) + causal)
         key_off = key_at - side * rows
         corner = jnp.where((key_off >= 0) & (key_off < rows) & (key_off > row_at), DROP, 0.0)
         corner = jnp.concatenate([corner] * GROUP, axis=0)
-        out = out_own if side == 0 else out_other
-        column = pl.multiple_of((side * 2 + z // 2) * width, width)
-        for head in range(kv_heads):
+        for head in range(heads // GROUP):
             for member in range(GROUP):
                 local = head * GROUP + member
-                slot = slot_of(core * lists_from + local // 16)
-                tile = picks[pl.ds(pl.multiple_of(slot * 16, 16), 16), pl.ds(column, width)]
-                bias = tile.astype(jnp.float32)[local % 16 : local % 16 + 1, :] + causal
+                line = local % list_rows
+                bias = biases[local // list_rows][line : line + 1, :]
                 at = slice(member * rows, (member + 1) * rows)
                 if side == 0:
                     q_from = pl.multiple_of((core * heads + local) * width, width)
-                    q_aug[at, :width] = q_own[:, pl.ds(q_from, width)]
+                    q_aug[side, head, at, :width] = q_own[:, pl.ds(q_from, width)]
                 else:
-                    q_aug[at, :width] = q_other[:, local * width : (local + 1) * width]
-                q_aug[at, width:] = jnp.broadcast_to(bias, (rows, width)).astype(jnp.bfloat16)
+                    q_aug[side, head, at, :width] = q_other[:, local * width : (local + 1) * width]
+                q_aug[side, head, at, width:] = jnp.broadcast_to(bias, (rows, width)).astype(jnp.bfloat16)
             scores = lax.dot_general(
-                q_aug[...], k_aug[head], (((1,), (1,)), ((), ())), preferred_element_type=jnp.float32
+                q_aug[side, head], k_aug[head], (((1,), (1,)), ((), ())), preferred_element_type=jnp.float32
             )
             scores = jnp.concatenate([scores[:, :unit_rows] + corner, scores[:, unit_rows:]], axis=1)
             row_max = jnp.max(scores, axis=1, keepdims=True)
-            probs = jnp.exp2((scores - row_max) * factor).astype(jnp.bfloat16)
-            mixed = jnp.dot(probs, v_aug[head], preferred_element_type=jnp.float32)
-            result = (mixed[:, :width] / mixed[:, width:]).astype(jnp.bfloat16)
-            for member in range(GROUP):
-                local = head * GROUP + member
-                out[:, local * width : (local + 1) * width] = result[member * rows : (member + 1) * rows]
+            probs = jnp.exp2((scores - row_max) * factor()).astype(jnp.bfloat16)
+            total[side, head] = jnp.dot(probs, v_aug[head], preferred_element_type=jnp.float32)
+            top[side, head] = jnp.broadcast_to(row_max, (GROUP * rows, width))
+
+
+def far_kernel(z_size, side, whole, q_aug, total, top, k_far, v_far, out, k_aug, v_aug):
+    width = HEAD_DIMENSION
+    rows = out.shape[0]
+    kv_heads = k_aug.shape[0]
+    place = chip_place(z_size) + z_size
+    fill_keys(z_size, rows, k_aug, v_aug, 0, place, k_far[...], v_far[...])
+    start = lax.axis_index("core") * kv_heads * GROUP * width if whole else 0
+    for head in range(kv_heads):
+        scores = lax.dot_general(
+            q_aug[side, head], k_aug[head], (((1,), (1,)), ((), ())), preferred_element_type=jnp.float32
+        )
+        near_max = top[side, head]
+        row_max = jnp.maximum(near_max, jnp.max(scores, axis=1, keepdims=True))
+        shrink = jnp.exp2((near_max - row_max) * factor())
+        probs = jnp.exp2((scores - row_max) * factor()).astype(jnp.bfloat16)
+        added = jnp.dot(probs, v_aug[head], preferred_element_type=jnp.float32)
+        mixed = total[side, head, :, :width] * shrink + added[:, :width]
+        sums = total[side, head, :, width:] * shrink + added[:, width:]
+        result = (mixed / sums).astype(jnp.bfloat16)
+        for member in range(GROUP):
+            column = start + (head * GROUP + member) * width
+            if whole:
+                column = pl.multiple_of(column, width)
+            out[:, pl.ds(column, width)] = result[member * rows : (member + 1) * rows]
 
 
 def per_device_ring(z_size, queries, keys, values, block_lists, block_counts):
+    del block_counts
     rows = queries.shape[0]
     core = lax.axis_index("core")
     half = keys.shape[1] // 2
@@ -238,35 +284,20 @@
     axes = ("seq", "x", "core")
 
     own = core * half
-    other = half - own
-    lane = jnp.arange(HEAD_DIMENSION) // 2
-    slots = jnp.arange(block_lists.shape[2])
-    used = (block_lists[..., None] == lane) & (slots < block_counts[..., None])[..., None]
-    picks = jnp.where(jnp.any(used, axis=2), 0.0, DROP).astype(jnp.bfloat16)
-    picks = picks.reshape(picks.shape[0], 2 * HEAD_DIMENSION)
-    sent = jnp.concatenate(
-        [
-            lax.dynamic_slice_in_dim(keys, other, half, 1),
-            lax.dynamic_slice_in_dim(values, other, half, 1),
-            jnp.concatenate([picks, picks], axis=1),
-        ],
+    k_got = lax.ppermute(keys, "core", swap)
+    v_got = lax.ppermute(values, "core", swap)
+    l_got = lax.ppermute(block_lists, "core", swap)
+    lists = jnp.concatenate([block_lists, l_got], axis=1).astype(jnp.bfloat16)
+    lists = lists.reshape(lists.shape[0], lists.shape[1] * lists.shape[2])
+    lists = jnp.pad(lists, ((0, 0), (0, half - lists.shape[1])))
+    unit = jnp.concatenate(
+        [lax.dynamic_slice_in_dim(part, own, half, 1) for part in (keys, k_got, values, v_got)] + [lists],
         axis=0,
     )
-    got = lax.ppermute(sent, "core", swap)
-    unit = jnp.concatenate(
-        [
-            lax.dynamic_slice_in_dim(keys, own, half, 1),
-            got[:rows],
-            lax.dynamic_slice_in_dim(values, own, half, 1),
-            got[rows : 2 * rows],
-            jnp.concatenate([picks, got[2 * rows :, : 2 * HEAD_DIMENSION]], axis=1),
-        ],
-        axis=0,
-    )
     q_width = heads * HEAD_DIMENSION
-    q_other = lax.ppermute(
-        lax.dynamic_slice_in_dim(queries, q_width - core * q_width, q_width, 1), "core", swap
-    )
+    late = lax.optimization_barrier((queries, unit))[0]
+    q_sent = lax.dynamic_slice_in_dim(late, q_width - core * q_width, q_width, 1)
+    q_other = lax.ppermute(q_sent, "core", swap)
     one, two, first, second = unit, unit, [], []
     for _ in range(z_size - 1):
         one = lax.ppermute(one, axes, ahead)
@@ -278,25 +309,49 @@
     v_far = lax.ppermute(two[unit_rows : 2 * unit_rows], axes, back)
     chips = 2 * z_size
     kv_heads = heads // GROUP
-    out_shape = jax.ShapeDtypeStruct((rows, q_width), jnp.bfloat16)
-    kept, away = pl.pallas_call(
-        functools.partial(ring_kernel, z_size, heads),
-        out_shape=(out_shape, out_shape),
+    near_rows = (chips - 1) * unit_rows
+    group_rows = GROUP * rows
+    wide = 2 * HEAD_DIMENSION
+    state = pl.pallas_call(
+        functools.partial(near_kernel, z_size, heads),
+        out_shape=(
+            jax.ShapeDtypeStruct((2, kv_heads, group_rows, wide), jnp.bfloat16),
+            jax.ShapeDtypeStruct((2, kv_heads, group_rows, wide), jnp.float32),
+            jax.ShapeDtypeStruct((2, kv_heads, group_rows, HEAD_DIMENSION), jnp.float32),
+        ),
         scratch_shapes=[
-            pltpu.VMEM((kv_heads, chips * unit_rows, 2 * HEAD_DIMENSION), jnp.bfloat16),
-            pltpu.VMEM((kv_heads, chips * unit_rows, 2 * HEAD_DIMENSION), jnp.bfloat16),
-            pltpu.VMEM((GROUP * rows, 2 * HEAD_DIMENSION), jnp.bfloat16),
-            pltpu.VMEM((chips * 16, half), jnp.bfloat16),
+            pltpu.VMEM((kv_heads, near_rows, wide), jnp.bfloat16),
+            pltpu.VMEM((kv_heads, near_rows, wide), jnp.bfloat16),
+            pltpu.VMEM(((chips - 1) * block_lists.shape[0], HEAD_DIMENSION), jnp.float32),
         ],
         compiler_params=pltpu.CompilerParams(vmem_limit_bytes=40 * 2**20),
-        name="attend",
-    )(queries, q_other, unit, *first, *second, k_far, v_far)
-    back_home = lax.ppermute(away, "core", swap)
-    return jnp.where(
-        core == 0,
-        jnp.concatenate([kept, back_home], axis=1),
-        jnp.concatenate([back_home, kept], axis=1),
-    )
+        cost_estimate=pl.CostEstimate(
+            flops=4 * 2 * kv_heads * group_rows * near_rows * wide,
+            bytes_accessed=8 * 2**20,
+            transcendentals=2 * kv_heads * group_rows * near_rows,
+        ),
+        name="near",
+    )(queries, q_other, unit, *first, *second)
+
+    def finish(side, whole):
+        return pl.pallas_call(
+            functools.partial(far_kernel, z_size, side, whole),
+            out_shape=jax.ShapeDtypeStruct((rows, q_width * (2 if whole else 1)), jnp.bfloat16),
+            scratch_shapes=[
+                pltpu.VMEM((kv_heads, unit_rows, wide), jnp.bfloat16),
+                pltpu.VMEM((kv_heads, unit_rows, wide), jnp.bfloat16),
+            ],
+            compiler_params=pltpu.CompilerParams(vmem_limit_bytes=40 * 2**20),
+            cost_estimate=pl.CostEstimate(
+                flops=4 * kv_heads * group_rows * unit_rows * wide,
+                bytes_accessed=8 * 2**20,
+                transcendentals=2 * kv_heads * group_rows * unit_rows,
+            ),
+            name="far_own" if whole else "far_other",
+        )(*state, k_far, v_far)
+
+    back_home = lax.ppermute(finish(1, False), "core", swap)
+    return lax.dynamic_update_slice_in_dim(finish(0, True), back_home, q_width - core * q_width, 1)
 
 
 def solution(mesh):

time: 48.2 us -> 43.7 us (0.907)
  waiting for transfers between devices: 22.3 us -> 14.8 us
  Pallas kernels: 6.29 us -> 9.45 us
  other arithmetic: 2.27 us -> 0.76 us
  local copies, waits for them, and re-layouts: 2.69 us -> 3.73 us
  starting transfers between devices: 14 us -> 14.6 us
    ppermute x3, starting transfers between devices: 0.18 us -> 7.1 us  [per_device_ring(): one = lax.ppermute(one, axes, ahead)]
    ppermute x3, starting transfers between devices: 6.89 us -> 0.48 us  [per_device_ring(): two = lax.ppermute(two, axes, back)]
    ppermute x3, waiting for transfers between devices: 9.8 us -> 3.97 us  [per_device_ring(): two = lax.ppermute(two, axes, back)]
    ppermute x3, waiting for transfers between devices: 5.82 us -> 10.8 us  [per_device_ring(): one = lax.ppermute(one, axes, ahead)]
    ppermute x1, waiting for transfers between devices: 3.78 us -> 0.01 us  [per_device_ring(): k_far = lax.ppermute(one[:unit_rows], axes, ahead)]
    pallas_call x1 -> x3, Pallas kernels: 6.29 us -> 9.45 us  [the longest x1 6.14 us: per_device_ring(): pl.pallas_call(functools.partial(near_kernel, z_size, heads), out_shape=(...]
    ppermute x3 -> x5, waiting for transfers between devices: 2.85 us -> 0.01 us  [the longest x1 0.01 us: per_device_ring(): v_got = lax.ppermute(values, 'core', swap)]
    ppermute x1, starting transfers between devices: 0.06 us -> 1.96 us  [per_device_ring(): k_far = lax.ppermute(one[:unit_rows], axes, ahead)]
  transfers between devices with their start and end apart: 11 -> 13, of which waited for: 8 -> 5; matrix products, arithmetic and copies ran while one was open for 0% -> 8% of each run, Pallas kernels for 0% -> 19%
where the time goes in v2:
time: 43.7 us; the launch traced here: 43.4 us
  waiting for transfers between devices  14.8 us (34%)
  starting transfers between devices  14.6 us (33%)
  Pallas kernels  9.45 us (22%)
  local copies, waits for them, and re-layouts  3.73 us (9%)
  other arithmetic  0.76 us (2%)
    ppermute x3, waiting for transfers between devices, per_device_ring(): one = lax.ppermute(one, axes, ahead)  10.8 us
    ppermute x3, starting transfers between devices, per_device_ring(): one = lax.ppermute(one, axes, ahead)  7.1 us
    pallas_call x1, Pallas kernels, per_device_ring(): pl.pallas_call(functools.partial(near_kernel, z_size, heads), out_shape=(...  6.14 us
    ppermute x3, waiting for transfers between devices, per_device_ring(): two = lax.ppermute(two, axes, back)  3.97 us
    ppermute x1, starting transfers between devices, per_device_ring(): back_home = lax.ppermute(finish(1, False), 'core', swap)  3.35 us
    pallas_call x2, Pallas kernels, finish(): pl.pallas_call(functools.partial(far_kernel, z_size, side, whole), out_sh...  3.3 us
    ppermute x1, starting transfers between devices, per_device_ring(): k_far = lax.ppermute(one[:unit_rows], axes, ahead)  1.96 us
    unnamed x6, local copies, waits for them, and re-layouts  1.71 us
  transfers between devices with their start and end apart: 13, of which 5 were waited for; matrix products, arithmetic and copies ran while one was open for 8% of the time, Pallas kernels for 19%

profile of v2, /device:TPU:1, one launch (start us, length us, event | category | flops | bytes accessed | tf_op | source)
XLA Modules:
  0.0 43.4 jit_solution(1750150804873700361)
XLA Ops:
  0.0 0.1 collective-permute-start
  0.1 0.5 %collective-permute-start.1 = (bf16[64,1024]{1,0:T(8,128)(2,1)}, bf16[64,1024]{1,0:T(8,128)(2,1)S(1)}, u32[]{:S(2)}, u32[]{:S(2)}) collective-permute-start(bf16[64,1024]{1,0:T(8,128)(2,1)} %param.7), channel_id=1, source_target_pairs={{0,1},{1,0},{2,3},{3,2},{4,5},{5,4},{6,7},{7,6},{8,9},{9,8},{10,11... | collective-permute-start | bytes 393224 | tf_op jit(solution)/shard_map/ppermute | solution.py:288
  0.5 0.1 collective-permute-start.2
  0.6 0.8 %dynamic-slice_dynamic-update-slice_fusion.3 = bf16[272,512]{1,0:T(8,128)(2,1)S(1)} fusion(bf16[64,1024]{1,0:T(8,128)(2,1)} %param.6, s32[]{:T(128)S(6)} %select_n.4), kind=kLoop, calls=%fused_computation.3 | loop fusion | bytes 131076
  1.4 0.7 %convert.6 = bf16[16,2,16]{2,1,0:T(2,128)(2,1)S(1)} convert(s32[16,2,16]{2,1,0:T(2,128)} %param.8) | non-fusion elementwise | flops 512 | bytes 3072 | tf_op jit(solution)/shard_map/convert
  2.1 0.0 collective-permute-done.2
  2.2 0.1 convert_element_type.7
  2.3 0.9 %dynamic-slice_dynamic-update-slice_fusion.1 = bf16[272,512]{1,0:T(8,128)(2,1)S(1)} fusion(bf16[272,512]{1,0:T(8,128)(2,1)S(1)} %dynamic-slice_dynamic-update-slice_fusion.2, bf16[64,1024]{1,0:T(8,128)(2,1)} %param.7, s32[]{:T(128)S(6)} %select_n.4), kind=kLoop, calls=%fused_computation.1 | loop fusion | bytes 131076
  3.2 0.0 collective-permute-done.1
  3.2 2.7 %collective-permute-start.4 = (bf16[272,512]{1,0:T(8,128)(2,1)S(1)}, bf16[272,512]{1,0:T(8,128)(2,1)S(1)}, u32[]{:S(2)}, u32[]{:S(2)}) collective-permute-start(bf16[272,512]{1,0:T(8,128)(2,1)S(1)} %pad_dynamic-update-slice_fusion.refs_2_), channel_id=1, source_target_pairs={{0,4},{4,8},{8,12},{12,14},{14,10},{10,6},{6,2},{2,0},{1,3},{5,1},... | collective-permute-start | bytes 835592 | tf_op jit(solution)/shard_map/ppermute | solution.py:303
  5.9 0.2 collective-permute-start.7
  6.0 5.8 %collective-permute-done.4.refs_3_ = bf16[272,512]{1,0:T(8,128)(2,1)S(1)} collective-permute-done((bf16[272,512]{1,0:T(8,128)(2,1)S(1)}, bf16[272,512]{1,0:T(8,128)(2,1)S(1)}, u32[]{:S(2)}, u32[]{:S(2)}) %collective-permute-start.4) | collective-permute-done | bytes 278560 | tf_op jit(solution)/shard_map/ppermute | solution.py:303
  11.8 2.2 %collective-permute-start.5 = (bf16[272,512]{1,0:T(8,128)(2,1)S(1)}, bf16[272,512]{1,0:T(8,128)(2,1)S(1)}, u32[]{:S(2)}, u32[]{:S(2)}) collective-permute-start(bf16[272,512]{1,0:T(8,128)(2,1)S(1)} %collective-permute-done.4.refs_3_), channel_id=1, source_target_pairs={{0,4},{4,8},{8,12},{12,14},{14,10},{10,6},{6,2},{2,0},{1,3},{5,1},... | collective-permute-start | bytes 835592 | tf_op jit(solution)/shard_map/ppermute | solution.py:303
  14.0 0.0 collective-permute-done.7.refs_6_
  14.0 0.3 collective-permute-start.8
  14.3 1.1 %constant_dynamic-slice_fusion = bf16[64,4096]{1,0:T(8,128)(2,1)S(1)} fusion(bf16[64,8192]{1,0:T(8,128)(2,1)} %refs_0_.1, s32[]{:T(128)S(6)} %select_n.5), kind=kLoop, calls=%fused_computation.7 | loop fusion | bytes 1048580 | tf_op jit(solution)/shard_map/dynamic_slice | solution.py:299
  15.4 1.1 %collective-permute-start.3 = (bf16[64,4096]{1,0:T(8,128)(2,1)S(1)}, bf16[64,4096]{1,0:T(8,128)(2,1)S(1)}, u32[]{:S(2)}, u32[]{:S(2)}) collective-permute-start(bf16[64,4096]{1,0:T(8,128)(2,1)S(1)} %constant_dynamic-slice_fusion), channel_id=1, source_target_pairs={{0,1},{1,0},{2,3},{3,2},{4,5},{5,4},{6,7},{7,6},{8,9},{9,8},{10,11... | collective-permute-start | bytes 1572872 | tf_op jit(solution)/shard_map/ppermute | solution.py:300
  16.5 2.3 %collective-permute-done.5.refs_4_ = bf16[272,512]{1,0:T(8,128)(2,1)S(1)} collective-permute-done((bf16[272,512]{1,0:T(8,128)(2,1)S(1)}, bf16[272,512]{1,0:T(8,128)(2,1)S(1)}, u32[]{:S(2)}, u32[]{:S(2)}) %collective-permute-start.5) | collective-permute-done | bytes 278560 | tf_op jit(solution)/shard_map/ppermute | solution.py:303
  18.8 2.2 %collective-permute-start.6 = (bf16[272,512]{1,0:T(8,128)(2,1)S(1)}, bf16[272,512]{1,0:T(8,128)(2,1)S(1)}, u32[]{:S(2)}, u32[]{:S(2)}) collective-permute-start(bf16[272,512]{1,0:T(8,128)(2,1)S(1)} %collective-permute-done.5.refs_4_), channel_id=1, source_target_pairs={{0,4},{4,8},{8,12},{12,14},{14,10},{10,6},{6,2},{2,0},{1,3},{5,1},... | collective-permute-start | bytes 835592 | tf_op jit(solution)/shard_map/ppermute | solution.py:303
  21.0 0.8 %collective-permute-done.8.refs_7_ = bf16[272,512]{1,0:T(8,128)(2,1)S(1)} collective-permute-done((bf16[272,512]{1,0:T(8,128)(2,1)S(1)}, bf16[272,512]{1,0:T(8,128)(2,1)S(1)}, u32[]{:S(2)}, u32[]{:S(2)}) %collective-permute-start.8) | collective-permute-done | bytes 278560 | tf_op jit(solution)/shard_map/ppermute | solution.py:304
  21.8 0.0 collective-permute-start.9
  21.8 2.7 %collective-permute-done.6.refs_5_ = bf16[272,512]{1,0:T(8,128)(2,1)S(1)} collective-permute-done((bf16[272,512]{1,0:T(8,128)(2,1)S(1)}, bf16[272,512]{1,0:T(8,128)(2,1)S(1)}, u32[]{:S(2)}, u32[]{:S(2)}) %collective-permute-start.6) | collective-permute-done | bytes 278560 | tf_op jit(solution)/shard_map/ppermute | solution.py:303
  24.6 2.0 %collective-permute-start.10 = (bf16[128,512]{1,0:T(8,128)(2,1)S(1)}, bf16[128,512]{1,0:T(8,128)(2,1)S(1)}, u32[]{:S(2)}, u32[]{:S(2)}) collective-permute-start(bf16[128,512]{1,0:T(8,128)(2,1)S(1)} %slice.8), channel_id=1, source_target_pairs={{0,4},{4,8},{8,12},{12,14},{14,10},{10,6},{6,2},{2,0},{1,3},{5,1},... | collective-permute-start | bytes 393224 | tf_op jit(solution)/shard_map/ppermute | solution.py:308
  26.5 3.2 %collective-permute-done.9.refs_8_ = bf16[272,512]{1,0:T(8,128)(2,1)S(1)} collective-permute-done((bf16[272,512]{1,0:T(8,128)(2,1)S(1)}, bf16[272,512]{1,0:T(8,128)(2,1)S(1)}, u32[]{:S(2)}, u32[]{:S(2)}) %collective-permute-start.9) | collective-permute-done | bytes 278560 | tf_op jit(solution)/shard_map/ppermute | solution.py:304
  29.7 0.1 collective-permute-start.11
  29.8 0.0 collective-permute-done.3.refs_1_
  29.8 6.1 %near.1 = (bf16[2,4,512,256]{3,2,1,0:T(8,128)(2,1)S(1)}, f32[2,4,512,256]{3,2,1,0:T(8,128)S(1)}, f32[2,4,512,128]{3,2,1,0:T(8,128)S(1)}) custom-call(bf16[64,8192]{1,0:T(8,128)(2,1)S(1)} %copy-done, bf16[64,4096]{1,0:T(8,128)(2,1)S(1)} %collective-permute-done.3.refs_1_, bf16[272,512]{1,0:T(8,128)(2,1)S(1)} %pad_dynamic-update-slice_fusion.refs_2_, ...), custom_call_target="tpu_custom_call" | custom-call | flops 3758096384 | bytes 8388608 | tf_op jit(solution)/shard_map/near/pallas_call | solution.py:315
  35.9 0.0 collective-permute-done.11.v_far
  36.0 1.2 %far_other.1 = bf16[64,4096]{1,0:T(8,128)(2,1)S(1)} custom-call(bf16[2,4,512,256]{3,2,1,0:T(8,128)(2,1)S(1)} %get-tuple-element.10.q_aug, f32[2,4,512,256]{3,2,1,0:T(8,128)S(1)} %get-tuple-element.11.total, f32[2,4,512,128]{3,2,1,0:T(8,128)S(1)} %get-tuple-element.12.top, bf16[128,512]{1,0:T(8,128)(2,1)S(1)} %collective-permute-done.10.k_far, ...), custom_call_target="tpu_custom_call" | custom-call | flops 268435456 | bytes 8388608 | tf_op jit(solution)/shard_map/far_other/pallas_call | solution.py:337
  37.1 3.3 %collective-permute-start.12 = (bf16[64,4096]{1,0:T(8,128)(2,1)S(1)}, bf16[64,4096]{1,0:T(8,128)(2,1)S(1)}, u32[]{:S(2)}, u32[]{:S(2)}) collective-permute-start(bf16[64,4096]{1,0:T(8,128)(2,1)S(1)} %far_other.1), channel_id=1, source_target_pairs={{0,1},{1,0},{2,3},{3,2},{4,5},{5,4},{6,7},{7,6},{8,9},{9,8},{10,11... | collective-permute-start | bytes 1572872 | tf_op jit(solution)/shard_map/ppermute | solution.py:353
  40.5 2.1 %far_own.1 = bf16[64,8192]{1,0:T(8,128)(2,1)} custom-call(bf16[2,4,512,256]{3,2,1,0:T(8,128)(2,1)S(1)} %get-tuple-element.10.q_aug, f32[2,4,512,256]{3,2,1,0:T(8,128)S(1)} %get-tuple-element.11.total, f32[2,4,512,128]{3,2,1,0:T(8,128)S(1)} %get-tuple-element.12.top, bf16[128,512]{1,0:T(8,128)(2,1)S(1)} %collective-permute-done.10.k_far, ...), custom_call_target="tpu_custom_call" | custom-call | flops 268435456 | bytes 8388608 | tf_op jit(solution)/shard_map/far_own/pallas_call | solution.py:337
  42.6 0.8 %constant_dynamic-update-slice_fusion = bf16[64,8192]{1,0:T(8,128)(2,1)} fusion(bf16[64,8192]{1,0:T(8,128)(2,1)} %far_own.1, bf16[64,4096]{1,0:T(8,128)(2,1)S(1)} %collective-permute-done.12, s32[]{:T(128)S(6)} %select_n.5), kind=kLoop, calls=%fused_computation.6 | loop fusion | bytes 1048580 | tf_op jit(solution)/shard_map/dynamic_update_slice | solution.py:354
  (12 shorter events, 0.1 us)
Async XLA Ops:
  0.0 29.8 %copy-start = (bf16[64,8192]{1,0:T(8,128)(2,1)S(1)}, bf16[64,8192]{1,0:T(8,128)(2,1)}, u32[]{:S(2)}) copy-start(bf16[64,8192]{1,0:T(8,128)(2,1)} %refs_0_.1) | copy-start | bytes 3145732
  0.0 2.3 %collective-permute-start = (bf16[64,1024]{1,0:T(8,128)(2,1)}, bf16[64,1024]{1,0:T(8,128)(2,1)S(1)}, u32[]{:S(2)}, u32[]{:S(2)}) collective-permute-start(bf16[64,1024]{1,0:T(8,128)(2,1)} %param.6), channel_id=1, source_target_pairs={{0,1},{1,0},{2,3},{3,2},{4,5},{5,4},{6,7},{7,6},{8,9},{9,8},{10,11... | collective-permute-start | bytes 393224 | tf_op jit(solution)/shard_map/ppermute | solution.py:287
  0.1 3.1 %collective-permute-start.1 = (bf16[64,1024]{1,0:T(8,128)(2,1)}, bf16[64,1024]{1,0:T(8,128)(2,1)S(1)}, u32[]{:S(2)}, u32[]{:S(2)}) collective-permute-start(bf16[64,1024]{1,0:T(8,128)(2,1)} %param.7), channel_id=1, source_target_pairs={{0,1},{1,0},{2,3},{3,2},{4,5},{5,4},{6,7},{7,6},{8,9},{9,8},{10,11... | collective-permute-start | bytes 393224 | tf_op jit(solution)/shard_map/ppermute | solution.py:288
  0.5 1.6 %collective-permute-start.2 = (s32[16,2,16]{2,1,0:T(2,128)}, s32[16,2,16]{2,1,0:T(2,128)S(1)}, u32[]{:S(2)}, u32[]{:S(2)}) collective-permute-start(s32[16,2,16]{2,1,0:T(2,128)} %param.8), channel_id=1, source_target_pairs={{0,1},{1,0},{2,3},{3,2},{4,5},{5,4},{6,7},{7,6},{8,9},{9,8},{10,11... | collective-permute-start | bytes 6152 | tf_op jit(solution)/shard_map/ppermute | solution.py:289
  3.2 8.6 %collective-permute-start.4 = (bf16[272,512]{1,0:T(8,128)(2,1)S(1)}, bf16[272,512]{1,0:T(8,128)(2,1)S(1)}, u32[]{:S(2)}, u32[]{:S(2)}) collective-permute-start(bf16[272,512]{1,0:T(8,128)(2,1)S(1)} %pad_dynamic-update-slice_fusion.refs_2_), channel_id=1, source_target_pairs={{0,4},{4,8},{8,12},{12,14},{14,10},{10,6},{6,2},{2,0},{1,3},{5,1},... | collective-permute-start | bytes 835592 | tf_op jit(solution)/shard_map/ppermute | solution.py:303
  5.9 8.1 %collective-permute-start.7 = (bf16[272,512]{1,0:T(8,128)(2,1)S(1)}, bf16[272,512]{1,0:T(8,128)(2,1)S(1)}, u32[]{:S(2)}, u32[]{:S(2)}) collective-permute-start(bf16[272,512]{1,0:T(8,128)(2,1)S(1)} %pad_dynamic-update-slice_fusion.refs_2_), channel_id=1, source_target_pairs={{0,2},{4,0},{8,4},{12,8},{14,12},{10,14},{6,10},{2,6},{1,5},{5,9},... | collective-permute-start | bytes 835592 | tf_op jit(solution)/shard_map/ppermute | solution.py:304
  11.8 7.0 %collective-permute-start.5 = (bf16[272,512]{1,0:T(8,128)(2,1)S(1)}, bf16[272,512]{1,0:T(8,128)(2,1)S(1)}, u32[]{:S(2)}, u32[]{:S(2)}) collective-permute-start(bf16[272,512]{1,0:T(8,128)(2,1)S(1)} %collective-permute-done.4.refs_3_), channel_id=1, source_target_pairs={{0,4},{4,8},{8,12},{12,14},{14,10},{10,6},{6,2},{2,0},{1,3},{5,1},... | collective-permute-start | bytes 835592 | tf_op jit(solution)/shard_map/ppermute | solution.py:303
  14.0 7.8 %collective-permute-start.8 = (bf16[272,512]{1,0:T(8,128)(2,1)S(1)}, bf16[272,512]{1,0:T(8,128)(2,1)S(1)}, u32[]{:S(2)}, u32[]{:S(2)}) collective-permute-start(bf16[272,512]{1,0:T(8,128)(2,1)S(1)} %collective-permute-done.7.refs_6_), channel_id=1, source_target_pairs={{0,2},{4,0},{8,4},{12,8},{14,12},{10,14},{6,10},{2,6},{1,5},{5,9},... | collective-permute-start | bytes 835592 | tf_op jit(solution)/shard_map/ppermute | solution.py:304
  15.4 14.4 %collective-permute-start.3 = (bf16[64,4096]{1,0:T(8,128)(2,1)S(1)}, bf16[64,4096]{1,0:T(8,128)(2,1)S(1)}, u32[]{:S(2)}, u32[]{:S(2)}) collective-permute-start(bf16[64,4096]{1,0:T(8,128)(2,1)S(1)} %constant_dynamic-slice_fusion), channel_id=1, source_target_pairs={{0,1},{1,0},{2,3},{3,2},{4,5},{5,4},{6,7},{7,6},{8,9},{9,8},{10,11... | collective-permute-start | bytes 1572872 | tf_op jit(solution)/shard_map/ppermute | solution.py:300
  18.8 5.7 %collective-permute-start.6 = (bf16[272,512]{1,0:T(8,128)(2,1)S(1)}, bf16[272,512]{1,0:T(8,128)(2,1)S(1)}, u32[]{:S(2)}, u32[]{:S(2)}) collective-permute-start(bf16[272,512]{1,0:T(8,128)(2,1)S(1)} %collective-permute-done.5.refs_4_), channel_id=1, source_target_pairs={{0,4},{4,8},{8,12},{12,14},{14,10},{10,6},{6,2},{2,0},{1,3},{5,1},... | collective-permute-start | bytes 835592 | tf_op jit(solution)/shard_map/ppermute | solution.py:303
  21.8 7.8 %collective-permute-start.9 = (bf16[272,512]{1,0:T(8,128)(2,1)S(1)}, bf16[272,512]{1,0:T(8,128)(2,1)S(1)}, u32[]{:S(2)}, u32[]{:S(2)}) collective-permute-start(bf16[272,512]{1,0:T(8,128)(2,1)S(1)} %collective-permute-done.8.refs_7_), channel_id=1, source_target_pairs={{0,2},{4,0},{8,4},{12,8},{14,12},{10,14},{6,10},{2,6},{1,5},{5,9},... | collective-permute-start | bytes 835592 | tf_op jit(solution)/shard_map/ppermute | solution.py:304
  24.6 11.4 %collective-permute-start.10 = (bf16[128,512]{1,0:T(8,128)(2,1)S(1)}, bf16[128,512]{1,0:T(8,128)(2,1)S(1)}, u32[]{:S(2)}, u32[]{:S(2)}) collective-permute-start(bf16[128,512]{1,0:T(8,128)(2,1)S(1)} %slice.8), channel_id=1, source_target_pairs={{0,4},{4,8},{8,12},{12,14},{14,10},{10,6},{6,2},{2,0},{1,3},{5,1},... | collective-permute-start | bytes 393224 | tf_op jit(solution)/shard_map/ppermute | solution.py:308
  29.7 6.2 %collective-permute-start.11 = (bf16[128,512]{1,0:T(8,128)(2,1)S(1)}, bf16[128,512]{1,0:T(8,128)(2,1)S(1)}, u32[]{:S(2)}, u32[]{:S(2)}) collective-permute-start(bf16[128,512]{1,0:T(8,128)(2,1)S(1)} %slice.9), channel_id=1, source_target_pairs={{0,2},{4,0},{8,4},{12,8},{14,12},{10,14},{6,10},{2,6},{1,5},{5,9},... | collective-permute-start | bytes 393224 | tf_op jit(solution)/shard_map/ppermute | solution.py:309
  37.1 5.5 %collective-permute-start.12 = (bf16[64,4096]{1,0:T(8,128)(2,1)S(1)}, bf16[64,4096]{1,0:T(8,128)(2,1)S(1)}, u32[]{:S(2)}, u32[]{:S(2)}) collective-permute-start(bf16[64,4096]{1,0:T(8,128)(2,1)S(1)} %far_other.1), channel_id=1, source_target_pairs={{0,1},{1,0},{2,3},{3,2},{4,5},{5,4},{6,7},{7,6},{8,9},{9,8},{10,11... | collective-permute-start | bytes 1572872 | tf_op jit(solution)/shard_map/ppermute | solution.py:353

commit v3 on v2

--- a/solution.py
+++ b/solution.py
@@ -130,10 +130,9 @@
         x, z = places[place % chips]
         return (z * 2 + x) * 2 + core
 
-    ahead = [(device(p, 0), device(p + 1, 0)) for p in range(chips)]
-    ahead += [(device(p, 1), device(p - 1, 1)) for p in range(chips)]
-    back = [(device(p, 0), device(p - 1, 0)) for p in range(chips)]
-    back += [(device(p, 1), device(p + 1, 1)) for p in range(chips)]
+    pairs = [(p, core) for p in range(chips) for core in range(2)]
+    ahead = [(device(p, core), device(p + 1, core)) for p, core in pairs]
+    back = [(device(p, core), device(p - 1, core)) for p, core in pairs]
     return ahead, back
 
 
@@ -174,30 +173,30 @@
 def near_kernel(z_size, heads, *refs):
     chips = 2 * z_size
     reach = z_size - 1
+    near = 1 + 2 * reach
     q_own, q_other = refs[:2]
-    units = refs[2 : 3 + 2 * reach]
-    q_aug, total, top, k_aug, v_aug, lists = refs[3 + 2 * reach :]
+    k_units, v_units = refs[2 : 2 + near], refs[2 + near : 2 + 2 * near]
+    q_aug, total, top, k_aug, v_aug, lists = refs[2 + 2 * near :]
     rows = q_own.shape[0]
     width = HEAD_DIMENSION
     unit_rows = 2 * rows
-    list_rows = units[0].shape[0] - 2 * unit_rows
+    list_rows = v_units[0].shape[0] - unit_rows
     slot_total = 16
     x, z, core = lax.axis_index("x"), lax.axis_index("seq"), lax.axis_index("core")
     place = chip_place(z_size)
-    turn = 1 - 2 * core
 
     sources = [place]
-    sources += [place - step * turn for step in range(1, reach + 1)]
-    sources += [place + step * turn for step in range(1, reach + 1)]
-    for slot, unit in enumerate(units):
-        keys, values = unit[:unit_rows, :], unit[unit_rows : 2 * unit_rows, :]
+    sources += [place - step for step in range(1, reach + 1)]
+    sources += [place + step for step in range(1, reach + 1)]
+    for slot in range(near):
+        keys, values = k_units[slot][...], v_units[slot][:unit_rows, :]
         fill_keys(z_size, rows, k_aug, v_aug, slot * unit_rows, sources[slot], keys, values)
         at = slice(slot * list_rows, (slot + 1) * list_rows)
-        lists[at, :] = unit[2 * unit_rows :, :width].astype(jnp.float32)
+        lists[at, :] = v_units[slot][unit_rows:, :width].astype(jnp.float32)
 
     def slot_of(z_from):
         place_from = jnp.where(x == 0, z_from, chips - 1 - z_from)
-        away = lax.rem((place - place_from) * turn + 2 * chips, chips)
+        away = lax.rem(place - place_from + chips, chips)
         return jnp.where(away < z_size, away, reach + chips - away)
 
     key_at = lax.broadcasted_iota(jnp.int32, (rows, unit_rows), 1)
@@ -290,23 +289,24 @@
     lists = jnp.concatenate([block_lists, l_got], axis=1).astype(jnp.bfloat16)
     lists = lists.reshape(lists.shape[0], lists.shape[1] * lists.shape[2])
     lists = jnp.pad(lists, ((0, 0), (0, half - lists.shape[1])))
-    unit = jnp.concatenate(
-        [lax.dynamic_slice_in_dim(part, own, half, 1) for part in (keys, k_got, values, v_got)] + [lists],
-        axis=0,
-    )
+    def halves(part, got):
+        return [lax.dynamic_slice_in_dim(part, own, half, 1), lax.dynamic_slice_in_dim(got, own, half, 1)]
+
+    k_unit = jnp.concatenate(halves(keys, k_got), axis=0)
+    v_unit = jnp.concatenate(halves(values, v_got) + [lists], axis=0)
     q_width = heads * HEAD_DIMENSION
-    late = lax.optimization_barrier((queries, unit))[0]
-    q_sent = lax.dynamic_slice_in_dim(late, q_width - core * q_width, q_width, 1)
+    q_sent = lax.dynamic_slice_in_dim(queries, q_width - core * q_width, q_width, 1)
     q_other = lax.ppermute(q_sent, "core", swap)
-    one, two, first, second = unit, unit, [], []
+    k_unit, q_other = lax.optimization_barrier((k_unit, q_other))
+    k_ahead, k_back, v_ahead, v_back = [k_unit], [k_unit], [v_unit], [v_unit]
     for _ in range(z_size - 1):
-        one = lax.ppermute(one, axes, ahead)
-        two = lax.ppermute(two, axes, back)
-        first.append(one)
-        second.append(two)
+        k_ahead.append(lax.ppermute(k_ahead[-1], axes, ahead))
+        k_back.append(lax.ppermute(k_back[-1], axes, back))
+        v_ahead.append(lax.ppermute(v_ahead[-1], axes, ahead))
+        v_back.append(lax.ppermute(v_back[-1], axes, back))
     unit_rows = 2 * rows
-    k_far = lax.ppermute(one[:unit_rows], axes, ahead)
-    v_far = lax.ppermute(two[unit_rows : 2 * unit_rows], axes, back)
+    k_far = lax.ppermute(k_ahead[-1], axes, ahead)
+    v_far = lax.ppermute(v_back[-1][:unit_rows], axes, back)
     chips = 2 * z_size
     kv_heads = heads // GROUP
     near_rows = (chips - 1) * unit_rows
@@ -331,7 +331,7 @@
             transcendentals=2 * kv_heads * group_rows * near_rows,
         ),
         name="near",
-    )(queries, q_other, unit, *first, *second)
+    )(queries, q_other, *k_ahead, *k_back[1:], *v_ahead, *v_back[1:])
 
     def finish(side, whole):
         return pl.pallas_call(

time: 43.7 us -> 39.7 us (0.908)
  waiting for transfers between devices: 14.8 us -> 9.95 us
  starting transfers between devices: 14.6 us -> 15.4 us
    ppermute x8 -> x14, waiting for transfers between devices: 14.7 us -> 9.94 us  [the longest x3 6.2 us: per_device_ring(): k_ahead.append(lax.ppermute(k_ahead[-1], axes, ahead))]
    dynamic_slice x1 -> x5, local copies, waits for them, and re-layouts: 1.08 us -> 2.85 us  [the longest x2 1.69 us: halves(): lax.dynamic_slice_in_dim(part, own, half, 1)]
    unnamed x6 -> x2, local copies, waits for them, and re-layouts: 1.71 us -> 0.01 us
    ppermute x8 -> x14, starting transfers between devices: 9.6 us -> 11 us  [the longest x3 3.92 us: per_device_ring(): v_back.append(lax.ppermute(v_back[-1], axes, back))]
    ppermute x1, starting transfers between devices: 1.13 us -> 0.44 us  [per_device_ring(): q_other = lax.ppermute(q_sent, 'core', swap)]
  transfers between devices with their start and end apart: 13 -> 19, of which waited for: 5 -> 6; matrix products, arithmetic and copies ran while one was open for 8% -> 9% of each run, Pallas kernels for 19% -> 21%
where the time goes in v3:
time: 39.7 us; the launch traced here: 39.4 us
  starting transfers between devices  15.4 us (39%)
  waiting for transfers between devices  9.95 us (25%)
  Pallas kernels  9.46 us (24%)
  local copies, waits for them, and re-layouts  3.78 us (10%)
  other arithmetic  0.78 us (2%)
    ppermute x3, waiting for transfers between devices, per_device_ring(): k_ahead.append(lax.ppermute(k_ahead[-1], axes, ahead))  6.2 us
    pallas_call x1, Pallas kernels, per_device_ring(): pl.pallas_call(functools.partial(near_kernel, z_size, heads), out_shape=(...  6.15 us
    ppermute x3, starting transfers between devices, per_device_ring(): v_back.append(lax.ppermute(v_back[-1], axes, back))  3.92 us
    ppermute x3, waiting for transfers between devices, per_device_ring(): v_back.append(lax.ppermute(v_back[-1], axes, back))  3.71 us
    ppermute x1, starting transfers between devices, per_device_ring(): back_home = lax.ppermute(finish(1, False), 'core', swap)  3.35 us
    pallas_call x2, Pallas kernels, finish(): pl.pallas_call(functools.partial(far_kernel, z_size, side, whole), out_sh...  3.3 us
    ppermute x3, starting transfers between devices, per_device_ring(): k_ahead.append(lax.ppermute(k_ahead[-1], axes, ahead))  2.77 us
    dynamic_slice x2, local copies, waits for them, and re-layouts, halves(): lax.dynamic_slice_in_dim(part, own, half, 1)  1.69 us
  transfers between devices with their start and end apart: 19, of which 6 were waited for; matrix products, arithmetic and copies ran while one was open for 9% of the time, Pallas kernels for 21%

profile of v3, /device:TPU:1, one launch (start us, length us, event | category | flops | bytes accessed | tf_op | source)
XLA Modules:
  0.0 39.4 jit_solution(13648676043840992868)
XLA Ops:
  0.1 1.2 %constant_dynamic-slice_fusion.2 = bf16[64,4096]{1,0:T(8,128)(2,1)S(1)} fusion(bf16[64,8192]{1,0:T(8,128)(2,1)} %refs_0_.1, s32[]{:T(128)S(6)} %select_n.5), kind=kLoop, calls=%fused_computation.8 | loop fusion | bytes 1048580 | tf_op jit(solution)/shard_map/dynamic_slice | solution.py:298
  1.2 0.4 %collective-permute-start.1 = (bf16[64,4096]{1,0:T(8,128)(2,1)S(1)}, bf16[64,4096]{1,0:T(8,128)(2,1)S(1)}, u32[]{:S(2)}, u32[]{:S(2)}) collective-permute-start(bf16[64,4096]{1,0:T(8,128)(2,1)S(1)} %constant_dynamic-slice_fusion.2), channel_id=1, source_target_pairs={{0,1},{1,0},{2,3},{3,2},{4,5},{5,4},{6,7},{7,6},{8,9},{9,8},{10,11... | collective-permute-start | bytes 1572872 | tf_op jit(solution)/shard_map/ppermute | solution.py:299
  1.7 0.1 collective-permute-start.8
  1.8 0.4 collective-permute-start.9
  2.2 0.8 %constant_dynamic-slice_fusion.4 = bf16[64,512]{1,0:T(8,128)(2,1)S(1)} fusion(bf16[64,1024]{1,0:T(8,128)(2,1)} %param.6, s32[]{:T(128)S(6)} %select_n.4), kind=kLoop, calls=%fused_computation.10 | loop fusion | bytes 131076 | tf_op jit(solution)/shard_map/dynamic_slice | solution.py:293
  3.0 0.8 %constant_dynamic-slice_fusion.1 = bf16[64,512]{1,0:T(8,128)(2,1)S(1)} fusion(bf16[64,1024]{1,0:T(8,128)(2,1)} %param.7, s32[]{:T(128)S(6)} %select_n.4), kind=kLoop, calls=%fused_computation.7 | loop fusion | bytes 131076 | tf_op jit(solution)/shard_map/dynamic_slice | solution.py:293
  3.9 0.7 %convert.6 = bf16[16,2,16]{2,1,0:T(2,128)(2,1)S(1)} convert(s32[16,2,16]{2,1,0:T(2,128)} %param.8) | non-fusion elementwise | flops 512 | bytes 3072 | tf_op jit(solution)/shard_map/convert
  4.6 0.1 convert_element_type.7
  4.8 2.3 %collective-permute-start.13 = (bf16[144,512]{1,0:T(8,128)(2,1)S(1)}, bf16[144,512]{1,0:T(8,128)(2,1)S(1)}, u32[]{:S(2)}, u32[]{:S(2)}) collective-permute-start(bf16[144,512]{1,0:T(8,128)(2,1)S(1)} %fusion.1.refs_9_), channel_id=1, source_target_pairs={{0,2},{1,3},{4,0},{5,1},{8,4},{9,5},{12,8},{13,9},{14,12},{15,13},... | collective-permute-start | bytes 442376 | tf_op jit(solution)/shard_map/ppermute | solution.py:306
  7.1 0.2 collective-permute-start.10
  7.3 1.5 %collective-permute-start.2 = (bf16[128,512]{1,0:T(8,128)(2,1)S(1)}, bf16[128,512]{1,0:T(8,128)(2,1)S(1)}, u32[]{:S(2)}, u32[]{:S(2)}) collective-permute-start(bf16[128,512]{1,0:T(8,128)(2,1)S(1)} %pad_maximum_fusion.refs_2_), channel_id=1, source_target_pairs={{0,4},{1,5},{4,8},{5,9},{8,12},{9,13},{12,14},{13,15},{14,10},{15,... | collective-permute-start | bytes 393224 | tf_op jit(solution)/shard_map/ppermute | solution.py:303
  8.8 2.2 %collective-permute-done.13.refs_13_ = bf16[144,512]{1,0:T(8,128)(2,1)S(1)} collective-permute-done((bf16[144,512]{1,0:T(8,128)(2,1)S(1)}, bf16[144,512]{1,0:T(8,128)(2,1)S(1)}, u32[]{:S(2)}, u32[]{:S(2)}) %collective-permute-start.13) | collective-permute-done | bytes 147488 | tf_op jit(solution)/shard_map/ppermute | solution.py:306
  11.1 1.1 %collective-permute-start.14 = (bf16[144,512]{1,0:T(8,128)(2,1)S(1)}, bf16[144,512]{1,0:T(8,128)(2,1)S(1)}, u32[]{:S(2)}, u32[]{:S(2)}) collective-permute-start(bf16[144,512]{1,0:T(8,128)(2,1)S(1)} %collective-permute-done.13.refs_13_), channel_id=1, source_target_pairs={{0,2},{1,3},{4,0},{5,1},{8,4},{9,5},{12,8},{13,9},{14,12},{15,13},... | collective-permute-start | bytes 442376 | tf_op jit(solution)/shard_map/ppermute | solution.py:306
  12.1 0.4 %collective-permute-start.11 = (bf16[144,512]{1,0:T(8,128)(2,1)S(1)}, bf16[144,512]{1,0:T(8,128)(2,1)S(1)}, u32[]{:S(2)}, u32[]{:S(2)}) collective-permute-start(bf16[144,512]{1,0:T(8,128)(2,1)S(1)} %collective-permute-done.10.refs_10_), channel_id=1, source_target_pairs={{0,4},{1,5},{4,8},{5,9},{8,12},{9,13},{12,14},{13,15},{14,10},{15,... | collective-permute-start | bytes 442376 | tf_op jit(solution)/shard_map/ppermute | solution.py:305
  12.5 2.1 %collective-permute-done.2.refs_3_ = bf16[128,512]{1,0:T(8,128)(2,1)S(1)} collective-permute-done((bf16[128,512]{1,0:T(8,128)(2,1)S(1)}, bf16[128,512]{1,0:T(8,128)(2,1)S(1)}, u32[]{:S(2)}, u32[]{:S(2)}) %collective-permute-start.2) | collective-permute-done | bytes 131104 | tf_op jit(solution)/shard_map/ppermute | solution.py:303
  14.6 0.5 %collective-permute-start.3 = (bf16[128,512]{1,0:T(8,128)(2,1)S(1)}, bf16[128,512]{1,0:T(8,128)(2,1)S(1)}, u32[]{:S(2)}, u32[]{:S(2)}) collective-permute-start(bf16[128,512]{1,0:T(8,128)(2,1)S(1)} %collective-permute-done.2.refs_3_), channel_id=1, source_target_pairs={{0,4},{1,5},{4,8},{5,9},{8,12},{9,13},{12,14},{13,15},{14,10},{15,... | collective-permute-start | bytes 393224 | tf_op jit(solution)/shard_map/ppermute | solution.py:303
  15.1 1.0 %collective-permute-start.6 = (bf16[128,512]{1,0:T(8,128)(2,1)S(1)}, bf16[128,512]{1,0:T(8,128)(2,1)S(1)}, u32[]{:S(2)}, u32[]{:S(2)}) collective-permute-start(bf16[128,512]{1,0:T(8,128)(2,1)S(1)} %collective-permute-done.5.refs_6_), channel_id=1, source_target_pairs={{0,2},{1,3},{4,0},{5,1},{8,4},{9,5},{12,8},{13,9},{14,12},{15,13},... | collective-permute-start | bytes 393224 | tf_op jit(solution)/shard_map/ppermute | solution.py:304
  16.1 0.8 %collective-permute-done.14.refs_14_ = bf16[144,512]{1,0:T(8,128)(2,1)S(1)} collective-permute-done((bf16[144,512]{1,0:T(8,128)(2,1)S(1)}, bf16[144,512]{1,0:T(8,128)(2,1)S(1)}, u32[]{:S(2)}, u32[]{:S(2)}) %collective-permute-start.14) | collective-permute-done | bytes 147488 | tf_op jit(solution)/shard_map/ppermute | solution.py:306
  16.9 0.5 %collective-permute-start.15 = (bf16[144,512]{1,0:T(8,128)(2,1)S(1)}, bf16[144,512]{1,0:T(8,128)(2,1)S(1)}, u32[]{:S(2)}, u32[]{:S(2)}) collective-permute-start(bf16[144,512]{1,0:T(8,128)(2,1)S(1)} %collective-permute-done.14.refs_14_), channel_id=1, source_target_pairs={{0,2},{1,3},{4,0},{5,1},{8,4},{9,5},{12,8},{13,9},{14,12},{15,13},... | collective-permute-start | bytes 442376 | tf_op jit(solution)/shard_map/ppermute | solution.py:306
  17.4 1.0 %collective-permute-start.12 = (bf16[144,512]{1,0:T(8,128)(2,1)S(1)}, bf16[144,512]{1,0:T(8,128)(2,1)S(1)}, u32[]{:S(2)}, u32[]{:S(2)}) collective-permute-start(bf16[144,512]{1,0:T(8,128)(2,1)S(1)} %collective-permute-done.11.refs_11_), channel_id=1, source_target_pairs={{0,4},{1,5},{4,8},{5,9},{8,12},{9,13},{12,14},{13,15},{14,10},{15,... | collective-permute-start | bytes 442376 | tf_op jit(solution)/shard_map/ppermute | solution.py:305
  18.3 1.4 %collective-permute-done.3.refs_4_ = bf16[128,512]{1,0:T(8,128)(2,1)S(1)} collective-permute-done((bf16[128,512]{1,0:T(8,128)(2,1)S(1)}, bf16[128,512]{1,0:T(8,128)(2,1)S(1)}, u32[]{:S(2)}, u32[]{:S(2)}) %collective-permute-start.3) | collective-permute-done | bytes 131104 | tf_op jit(solution)/shard_map/ppermute | solution.py:303
  19.8 0.8 %collective-permute-start.4 = (bf16[128,512]{1,0:T(8,128)(2,1)S(1)}, bf16[128,512]{1,0:T(8,128)(2,1)S(1)}, u32[]{:S(2)}, u32[]{:S(2)}) collective-permute-start(bf16[128,512]{1,0:T(8,128)(2,1)S(1)} %collective-permute-done.3.refs_4_), channel_id=1, source_target_pairs={{0,4},{1,5},{4,8},{5,9},{8,12},{9,13},{12,14},{13,15},{14,10},{15,... | collective-permute-start | bytes 393224 | tf_op jit(solution)/shard_map/ppermute | solution.py:303
  20.6 0.6 %collective-permute-start.7 = (bf16[128,512]{1,0:T(8,128)(2,1)S(1)}, bf16[128,512]{1,0:T(8,128)(2,1)S(1)}, u32[]{:S(2)}, u32[]{:S(2)}) collective-permute-start(bf16[128,512]{1,0:T(8,128)(2,1)S(1)} %collective-permute-done.6.refs_7_), channel_id=1, source_target_pairs={{0,2},{1,3},{4,0},{5,1},{8,4},{9,5},{12,8},{13,9},{14,12},{15,13},... | collective-permute-start | bytes 393224 | tf_op jit(solution)/shard_map/ppermute | solution.py:304
  21.2 0.7 %collective-permute-done.15.refs_15_ = bf16[144,512]{1,0:T(8,128)(2,1)S(1)} collective-permute-done((bf16[144,512]{1,0:T(8,128)(2,1)S(1)}, bf16[144,512]{1,0:T(8,128)(2,1)S(1)}, u32[]{:S(2)}, u32[]{:S(2)}) %collective-permute-start.15) | collective-permute-done | bytes 147488 | tf_op jit(solution)/shard_map/ppermute | solution.py:306
  21.9 0.7 %collective-permute-start.17 = (bf16[128,512]{1,0:T(8,128)(2,1)S(1)}, bf16[128,512]{1,0:T(8,128)(2,1)S(1)}, u32[]{:S(2)}, u32[]{:S(2)}) collective-permute-start(bf16[128,512]{1,0:T(8,128)(2,1)S(1)} %slice.4), channel_id=1, source_target_pairs={{0,2},{1,3},{4,0},{5,1},{8,4},{9,5},{12,8},{13,9},{14,12},{15,13},... | collective-permute-start | bytes 393224 | tf_op jit(solution)/shard_map/ppermute | solution.py:309
  22.6 2.7 %collective-permute-done.4.refs_5_ = bf16[128,512]{1,0:T(8,128)(2,1)S(1)} collective-permute-done((bf16[128,512]{1,0:T(8,128)(2,1)S(1)}, bf16[128,512]{1,0:T(8,128)(2,1)S(1)}, u32[]{:S(2)}, u32[]{:S(2)}) %collective-permute-start.4) | collective-permute-done | bytes 131104 | tf_op jit(solution)/shard_map/ppermute | solution.py:303
  25.3 0.4 %collective-permute-start.16 = (bf16[128,512]{1,0:T(8,128)(2,1)S(1)}, bf16[128,512]{1,0:T(8,128)(2,1)S(1)}, u32[]{:S(2)}, u32[]{:S(2)}) collective-permute-start(bf16[128,512]{1,0:T(8,128)(2,1)S(1)} %collective-permute-done.4.refs_5_), channel_id=1, source_target_pairs={{0,4},{1,5},{4,8},{5,9},{8,12},{9,13},{12,14},{13,15},{14,10},{15,... | collective-permute-start | bytes 393224 | tf_op jit(solution)/shard_map/ppermute | solution.py:308
  25.8 6.2 %near.1 = (bf16[2,4,512,256]{3,2,1,0:T(8,128)(2,1)S(1)}, f32[2,4,512,256]{3,2,1,0:T(8,128)S(1)}, f32[2,4,512,128]{3,2,1,0:T(8,128)S(1)}) custom-call(bf16[64,8192]{1,0:T(8,128)(2,1)S(1)} %copy-done, bf16[64,4096]{1,0:T(8,128)(2,1)S(1)} %collective-permute-done.1.refs_1_, bf16[128,512]{1,0:T(8,128)(2,1)S(1)} %pad_maximum_fusion.refs_2_, ...), custom_call_target="tpu_custom_call" | custom-call | flops 3758096384 | bytes 8388608 | tf_op jit(solution)/shard_map/near/pallas_call | solution.py:315
  31.9 1.2 %far_other.1 = bf16[64,4096]{1,0:T(8,128)(2,1)S(1)} custom-call(bf16[2,4,512,256]{3,2,1,0:T(8,128)(2,1)S(1)} %get-tuple-element.12.q_aug, f32[2,4,512,256]{3,2,1,0:T(8,128)S(1)} %get-tuple-element.13.total, f32[2,4,512,128]{3,2,1,0:T(8,128)S(1)} %get-tuple-element.14.top, bf16[128,512]{1,0:T(8,128)(2,1)S(1)} %collective-permute-done.16.k_far, ...), custom_call_target="tpu_custom_call" | custom-call | flops 268435456 | bytes 8388608 | tf_op jit(solution)/shard_map/far_other/pallas_call | solution.py:337
  33.1 3.3 %collective-permute-start.18 = (bf16[64,4096]{1,0:T(8,128)(2,1)S(1)}, bf16[64,4096]{1,0:T(8,128)(2,1)S(1)}, u32[]{:S(2)}, u32[]{:S(2)}) collective-permute-start(bf16[64,4096]{1,0:T(8,128)(2,1)S(1)} %far_other.1), channel_id=1, source_target_pairs={{0,1},{1,0},{2,3},{3,2},{4,5},{5,4},{6,7},{7,6},{8,9},{9,8},{10,11... | collective-permute-start | bytes 1572872 | tf_op jit(solution)/shard_map/ppermute | solution.py:353
  36.5 2.1 %far_own.1 = bf16[64,8192]{1,0:T(8,128)(2,1)} custom-call(bf16[2,4,512,256]{3,2,1,0:T(8,128)(2,1)S(1)} %get-tuple-element.12.q_aug, f32[2,4,512,256]{3,2,1,0:T(8,128)S(1)} %get-tuple-element.13.total, f32[2,4,512,128]{3,2,1,0:T(8,128)S(1)} %get-tuple-element.14.top, bf16[128,512]{1,0:T(8,128)(2,1)S(1)} %collective-permute-done.16.k_far, ...), custom_call_target="tpu_custom_call" | custom-call | flops 268435456 | bytes 8388608 | tf_op jit(solution)/shard_map/far_own/pallas_call | solution.py:337
  38.6 0.8 %constant_dynamic-update-slice_fusion = bf16[64,8192]{1,0:T(8,128)(2,1)} fusion(bf16[64,8192]{1,0:T(8,128)(2,1)} %far_own.1, bf16[64,4096]{1,0:T(8,128)(2,1)S(1)} %collective-permute-done.18, s32[]{:T(128)S(6)} %select_n.5), kind=kLoop, calls=%fused_computation.5 | loop fusion | bytes 1048580 | tf_op jit(solution)/shard_map/dynamic_update_slice | solution.py:354
  (24 shorter events, 0.2 us)
Async XLA Ops:
  0.0 25.8 %copy-start = (bf16[64,8192]{1,0:T(8,128)(2,1)S(1)}, bf16[64,8192]{1,0:T(8,128)(2,1)}, u32[]{:S(2)}) copy-start(bf16[64,8192]{1,0:T(8,128)(2,1)} %refs_0_.1) | copy-start | bytes 3145732
  0.0 7.3 %collective-permute-start = (bf16[64,1024]{1,0:T(8,128)(2,1)}, bf16[64,1024]{1,0:T(8,128)(2,1)S(1)}, u32[]{:S(2)}, u32[]{:S(2)}) collective-permute-start(bf16[64,1024]{1,0:T(8,128)(2,1)} %param.6), channel_id=1, source_target_pairs={{0,1},{1,0},{2,3},{3,2},{4,5},{5,4},{6,7},{7,6},{8,9},{9,8},{10,11... | collective-permute-start | bytes 393224 | tf_op jit(solution)/shard_map/ppermute | solution.py:286
  1.2 6.1 %collective-permute-start.1 = (bf16[64,4096]{1,0:T(8,128)(2,1)S(1)}, bf16[64,4096]{1,0:T(8,128)(2,1)S(1)}, u32[]{:S(2)}, u32[]{:S(2)}) collective-permute-start(bf16[64,4096]{1,0:T(8,128)(2,1)S(1)} %constant_dynamic-slice_fusion.2), channel_id=1, source_target_pairs={{0,1},{1,0},{2,3},{3,2},{4,5},{5,4},{6,7},{7,6},{8,9},{9,8},{10,11... | collective-permute-start | bytes 1572872 | tf_op jit(solution)/shard_map/ppermute | solution.py:299
  1.7 3.1 %collective-permute-start.8 = (bf16[64,1024]{1,0:T(8,128)(2,1)}, bf16[64,1024]{1,0:T(8,128)(2,1)S(1)}, u32[]{:S(2)}, u32[]{:S(2)}) collective-permute-start(bf16[64,1024]{1,0:T(8,128)(2,1)} %param.7), channel_id=1, source_target_pairs={{0,1},{1,0},{2,3},{3,2},{4,5},{5,4},{6,7},{7,6},{8,9},{9,8},{10,11... | collective-permute-start | bytes 393224 | tf_op jit(solution)/shard_map/ppermute | solution.py:287
  1.8 2.8 %collective-permute-start.9 = (s32[16,2,16]{2,1,0:T(2,128)}, s32[16,2,16]{2,1,0:T(2,128)S(1)}, u32[]{:S(2)}, u32[]{:S(2)}) collective-permute-start(s32[16,2,16]{2,1,0:T(2,128)} %param.8), channel_id=1, source_target_pairs={{0,1},{1,0},{2,3},{3,2},{4,5},{5,4},{6,7},{7,6},{8,9},{9,8},{10,11... | collective-permute-start | bytes 6152 | tf_op jit(solution)/shard_map/ppermute | solution.py:288
  4.8 6.3 %collective-permute-start.13 = (bf16[144,512]{1,0:T(8,128)(2,1)S(1)}, bf16[144,512]{1,0:T(8,128)(2,1)S(1)}, u32[]{:S(2)}, u32[]{:S(2)}) collective-permute-start(bf16[144,512]{1,0:T(8,128)(2,1)S(1)} %fusion.1.refs_9_), channel_id=1, source_target_pairs={{0,2},{1,3},{4,0},{5,1},{8,4},{9,5},{12,8},{13,9},{14,12},{15,13},... | collective-permute-start | bytes 442376 | tf_op jit(solution)/shard_map/ppermute | solution.py:306
  7.1 5.0 %collective-permute-start.10 = (bf16[144,512]{1,0:T(8,128)(2,1)S(1)}, bf16[144,512]{1,0:T(8,128)(2,1)S(1)}, u32[]{:S(2)}, u32[]{:S(2)}) collective-permute-start(bf16[144,512]{1,0:T(8,128)(2,1)S(1)} %fusion.1.refs_9_), channel_id=1, source_target_pairs={{0,4},{1,5},{4,8},{5,9},{8,12},{9,13},{12,14},{13,15},{14,10},{15,... | collective-permute-start | bytes 442376 | tf_op jit(solution)/shard_map/ppermute | solution.py:305
  7.3 7.3 %collective-permute-start.2 = (bf16[128,512]{1,0:T(8,128)(2,1)S(1)}, bf16[128,512]{1,0:T(8,128)(2,1)S(1)}, u32[]{:S(2)}, u32[]{:S(2)}) collective-permute-start(bf16[128,512]{1,0:T(8,128)(2,1)S(1)} %pad_maximum_fusion.refs_2_), channel_id=1, source_target_pairs={{0,4},{1,5},{4,8},{5,9},{8,12},{9,13},{12,14},{13,15},{14,10},{15,... | collective-permute-start | bytes 393224 | tf_op jit(solution)/shard_map/ppermute | solution.py:303
  8.8 6.3 %collective-permute-start.5 = (bf16[128,512]{1,0:T(8,128)(2,1)S(1)}, bf16[128,512]{1,0:T(8,128)(2,1)S(1)}, u32[]{:S(2)}, u32[]{:S(2)}) collective-permute-start(bf16[128,512]{1,0:T(8,128)(2,1)S(1)} %pad_maximum_fusion.refs_2_), channel_id=1, source_target_pairs={{0,2},{1,3},{4,0},{5,1},{8,4},{9,5},{12,8},{13,9},{14,12},{15,13},... | collective-permute-start | bytes 393224 | tf_op jit(solution)/shard_map/ppermute | solution.py:304
  11.1 5.8 %collective-permute-start.14 = (bf16[144,512]{1,0:T(8,128)(2,1)S(1)}, bf16[144,512]{1,0:T(8,128)(2,1)S(1)}, u32[]{:S(2)}, u32[]{:S(2)}) collective-permute-start(bf16[144,512]{1,0:T(8,128)(2,1)S(1)} %collective-permute-done.13.refs_13_), channel_id=1, source_target_pairs={{0,2},{1,3},{4,0},{5,1},{8,4},{9,5},{12,8},{13,9},{14,12},{15,13},... | collective-permute-start | bytes 442376 | tf_op jit(solution)/shard_map/ppermute | solution.py:306
  12.1 5.3 %collective-permute-start.11 = (bf16[144,512]{1,0:T(8,128)(2,1)S(1)}, bf16[144,512]{1,0:T(8,128)(2,1)S(1)}, u32[]{:S(2)}, u32[]{:S(2)}) collective-permute-start(bf16[144,512]{1,0:T(8,128)(2,1)S(1)} %collective-permute-done.10.refs_10_), channel_id=1, source_target_pairs={{0,4},{1,5},{4,8},{5,9},{8,12},{9,13},{12,14},{13,15},{14,10},{15,... | collective-permute-start | bytes 442376 | tf_op jit(solution)/shard_map/ppermute | solution.py:305
  14.6 5.2 %collective-permute-start.3 = (bf16[128,512]{1,0:T(8,128)(2,1)S(1)}, bf16[128,512]{1,0:T(8,128)(2,1)S(1)}, u32[]{:S(2)}, u32[]{:S(2)}) collective-permute-start(bf16[128,512]{1,0:T(8,128)(2,1)S(1)} %collective-permute-done.2.refs_3_), channel_id=1, source_target_pairs={{0,4},{1,5},{4,8},{5,9},{8,12},{9,13},{12,14},{13,15},{14,10},{15,... | collective-permute-start | bytes 393224 | tf_op jit(solution)/shard_map/ppermute | solution.py:303
  15.1 5.5 %collective-permute-start.6 = (bf16[128,512]{1,0:T(8,128)(2,1)S(1)}, bf16[128,512]{1,0:T(8,128)(2,1)S(1)}, u32[]{:S(2)}, u32[]{:S(2)}) collective-permute-start(bf16[128,512]{1,0:T(8,128)(2,1)S(1)} %collective-permute-done.5.refs_6_), channel_id=1, source_target_pairs={{0,2},{1,3},{4,0},{5,1},{8,4},{9,5},{12,8},{13,9},{14,12},{15,13},... | collective-permute-start | bytes 393224 | tf_op jit(solution)/shard_map/ppermute | solution.py:304
  16.9 5.0 %collective-permute-start.15 = (bf16[144,512]{1,0:T(8,128)(2,1)S(1)}, bf16[144,512]{1,0:T(8,128)(2,1)S(1)}, u32[]{:S(2)}, u32[]{:S(2)}) collective-permute-start(bf16[144,512]{1,0:T(8,128)(2,1)S(1)} %collective-permute-done.14.refs_14_), channel_id=1, source_target_pairs={{0,2},{1,3},{4,0},{5,1},{8,4},{9,5},{12,8},{13,9},{14,12},{15,13},... | collective-permute-start | bytes 442376 | tf_op jit(solution)/shard_map/ppermute | solution.py:306
  17.4 8.4 %collective-permute-start.12 = (bf16[144,512]{1,0:T(8,128)(2,1)S(1)}, bf16[144,512]{1,0:T(8,128)(2,1)S(1)}, u32[]{:S(2)}, u32[]{:S(2)}) collective-permute-start(bf16[144,512]{1,0:T(8,128)(2,1)S(1)} %collective-permute-done.11.refs_11_), channel_id=1, source_target_pairs={{0,4},{1,5},{4,8},{5,9},{8,12},{9,13},{12,14},{13,15},{14,10},{15,... | collective-permute-start | bytes 442376 | tf_op jit(solution)/shard_map/ppermute | solution.py:305
  19.8 5.5 %collective-permute-start.4 = (bf16[128,512]{1,0:T(8,128)(2,1)S(1)}, bf16[128,512]{1,0:T(8,128)(2,1)S(1)}, u32[]{:S(2)}, u32[]{:S(2)}) collective-permute-start(bf16[128,512]{1,0:T(8,128)(2,1)S(1)} %collective-permute-done.3.refs_4_), channel_id=1, source_target_pairs={{0,4},{1,5},{4,8},{5,9},{8,12},{9,13},{12,14},{13,15},{14,10},{15,... | collective-permute-start | bytes 393224 | tf_op jit(solution)/shard_map/ppermute | solution.py:303
  20.6 5.2 %collective-permute-start.7 = (bf16[128,512]{1,0:T(8,128)(2,1)S(1)}, bf16[128,512]{1,0:T(8,128)(2,1)S(1)}, u32[]{:S(2)}, u32[]{:S(2)}) collective-permute-start(bf16[128,512]{1,0:T(8,128)(2,1)S(1)} %collective-permute-done.6.refs_7_), channel_id=1, source_target_pairs={{0,2},{1,3},{4,0},{5,1},{8,4},{9,5},{12,8},{13,9},{14,12},{15,13},... | collective-permute-start | bytes 393224 | tf_op jit(solution)/shard_map/ppermute | solution.py:304
  21.9 10.0 %collective-permute-start.17 = (bf16[128,512]{1,0:T(8,128)(2,1)S(1)}, bf16[128,512]{1,0:T(8,128)(2,1)S(1)}, u32[]{:S(2)}, u32[]{:S(2)}) collective-permute-start(bf16[128,512]{1,0:T(8,128)(2,1)S(1)} %slice.4), channel_id=1, source_target_pairs={{0,2},{1,3},{4,0},{5,1},{8,4},{9,5},{12,8},{13,9},{14,12},{15,13},... | collective-permute-start | bytes 393224 | tf_op jit(solution)/shard_map/ppermute | solution.py:309
  25.3 6.6 %collective-permute-start.16 = (bf16[128,512]{1,0:T(8,128)(2,1)S(1)}, bf16[128,512]{1,0:T(8,128)(2,1)S(1)}, u32[]{:S(2)}, u32[]{:S(2)}) collective-permute-start(bf16[128,512]{1,0:T(8,128)(2,1)S(1)} %collective-permute-done.4.refs_5_), channel_id=1, source_target_pairs={{0,4},{1,5},{4,8},{5,9},{8,12},{9,13},{12,14},{13,15},{14,10},{15,... | collective-permute-start | bytes 393224 | tf_op jit(solution)/shard_map/ppermute | solution.py:308
  33.1 5.5 %collective-permute-start.18 = (bf16[64,4096]{1,0:T(8,128)(2,1)S(1)}, bf16[64,4096]{1,0:T(8,128)(2,1)S(1)}, u32[]{:S(2)}, u32[]{:S(2)}) collective-permute-start(bf16[64,4096]{1,0:T(8,128)(2,1)S(1)} %far_other.1), channel_id=1, source_target_pairs={{0,1},{1,0},{2,3},{3,2},{4,5},{5,4},{6,7},{7,6},{8,9},{9,8},{10,11... | collective-permute-start | bytes 1572872 | tf_op jit(solution)/shard_map/ppermute | solution.py:353

commit v4 on v3

--- a/solution.py
+++ b/solution.py
@@ -176,7 +176,8 @@
     near = 1 + 2 * reach
     q_own, q_other = refs[:2]
     k_units, v_units = refs[2 : 2 + near], refs[2 + near : 2 + 2 * near]
-    q_aug, total, top, k_aug, v_aug, lists = refs[2 + 2 * near :]
+    states = refs[2 + 2 * near : 8 + 2 * near]
+    k_aug, v_aug, lists = refs[8 + 2 * near : 11 + 2 * near]
     rows = q_own.shape[0]
     width = HEAD_DIMENSION
     unit_rows = 2 * rows
@@ -204,8 +205,32 @@
     lane = lax.broadcasted_iota(jnp.int32, (list_rows, width), 1)
     block = (lane // 2).astype(jnp.float32)
     spans = heads // list_rows
+    def settle(side, head, scores, corner):
+        part_rows = GROUP * rows // 2
+        for part in range(2):
+            at = slice(part * part_rows, (part + 1) * part_rows)
+            first = scores[at, :unit_rows] + corner[at]
+            row_max = jnp.max(
+                jnp.maximum(first, best_of(scores[at, unit_rows:], unit_rows)), axis=1, keepdims=True
+            )
+            probs = [jnp.exp2((first - row_max) * factor()).astype(jnp.bfloat16)]
+            probs.append(jnp.exp2((scores[at, unit_rows:] - row_max) * factor()).astype(jnp.bfloat16))
+            probs = jnp.concatenate(probs, axis=1)
+            states[3 * side + 1][head, at] = jnp.dot(
+                probs, v_aug[head], preferred_element_type=jnp.float32
+            )
+            states[3 * side + 2][head, at] = jnp.broadcast_to(row_max, (part_rows, width))
+
+    def best_of(block, step):
+        best = block[:, :step]
+        for start in range(step, block.shape[1], step):
+            best = jnp.maximum(best, block[:, start : start + step])
+        return best
+
+    waiting = ()
     for side in (1, 0):
         here = core if side == 0 else 1 - core
+        q_aug = states[3 * side]
         causal = jnp.where(lane > chunk_of(z_size, place, here), DROP, 0.0)
         biases = []
         for span in range(spans):
@@ -232,44 +257,52 @@
                 at = slice(member * rows, (member + 1) * rows)
                 if side == 0:
                     q_from = pl.multiple_of((core * heads + local) * width, width)
-                    q_aug[side, head, at, :width] = q_own[:, pl.ds(q_from, width)]
+                    q_aug[head, at, :width] = q_own[:, pl.ds(q_from, width)]
                 else:
-                    q_aug[side, head, at, :width] = q_other[:, local * width : (local + 1) * width]
-                q_aug[side, head, at, width:] = jnp.broadcast_to(bias, (rows, width)).astype(jnp.bfloat16)
+                    q_aug[head, at, :width] = q_other[:, local * width : (local + 1) * width]
+                q_aug[head, at, width:] = jnp.broadcast_to(bias, (rows, width)).astype(jnp.bfloat16)
             scores = lax.dot_general(
-                q_aug[side, head], k_aug[head], (((1,), (1,)), ((), ())), preferred_element_type=jnp.float32
+                q_aug[head], k_aug[head], (((1,), (1,)), ((), ())), preferred_element_type=jnp.float32
             )
-            scores = jnp.concatenate([scores[:, :unit_rows] + corner, scores[:, unit_rows:]], axis=1)
-            row_max = jnp.max(scores, axis=1, keepdims=True)
-            probs = jnp.exp2((scores - row_max) * factor()).astype(jnp.bfloat16)
-            total[side, head] = jnp.dot(probs, v_aug[head], preferred_element_type=jnp.float32)
-            top[side, head] = jnp.broadcast_to(row_max, (GROUP * rows, width))
-
-
-def far_kernel(z_size, side, whole, q_aug, total, top, k_far, v_far, out, k_aug, v_aug):
+            if waiting:
+                settle(*waiting)
+            waiting = (side, head, scores, corner)
+    settle(*waiting)
+
+
+def far_kernel(z_size, whole, q_aug, total, top, k_far, v_far, target, k_aug, v_aug, *spare):
     width = HEAD_DIMENSION
-    rows = out.shape[0]
+    rows = target.shape[0]
+    out = spare[0] if whole else target
+    copies = []
     kv_heads = k_aug.shape[0]
     place = chip_place(z_size) + z_size
     fill_keys(z_size, rows, k_aug, v_aug, 0, place, k_far[...], v_far[...])
-    start = lax.axis_index("core") * kv_heads * GROUP * width if whole else 0
     for head in range(kv_heads):
         scores = lax.dot_general(
-            q_aug[side, head], k_aug[head], (((1,), (1,)), ((), ())), preferred_element_type=jnp.float32
-        )
-        near_max = top[side, head]
+            q_aug[head], k_aug[head], (((1,), (1,)), ((), ())), preferred_element_type=jnp.float32
+        )
+        near_max = top[head]
         row_max = jnp.maximum(near_max, jnp.max(scores, axis=1, keepdims=True))
         shrink = jnp.exp2((near_max - row_max) * factor())
         probs = jnp.exp2((scores - row_max) * factor()).astype(jnp.bfloat16)
         added = jnp.dot(probs, v_aug[head], preferred_element_type=jnp.float32)
-        mixed = total[side, head, :, :width] * shrink + added[:, :width]
-        sums = total[side, head, :, width:] * shrink + added[:, width:]
+        mixed = total[head, :, :width] * shrink + added[:, :width]
+        sums = total[head, :, width:] * shrink + added[:, width:]
         result = (mixed / sums).astype(jnp.bfloat16)
         for member in range(GROUP):
-            column = start + (head * GROUP + member) * width
-            if whole:
-                column = pl.multiple_of(column, width)
-            out[:, pl.ds(column, width)] = result[member * rows : (member + 1) * rows]
+            column = (head * GROUP + member) * width
+            out[:, column : column + width] = result[member * rows : (member + 1) * rows]
+        if whole:
+            span = GROUP * width
+            start = pl.multiple_of((lax.axis_index("core") * kv_heads + head) * span, span)
+            copy = pltpu.make_async_copy(
+                out.at[:, pl.ds(head * span, span)], target.at[:, pl.ds(start, span)], spare[1].at[head]
+            )
+            copy.start()
+            copies.append(copy)
+    for copy in copies:
+        copy.wait()
 
 
 def per_device_ring(z_size, queries, keys, values, block_lists, block_counts):
@@ -286,8 +319,8 @@
     k_got = lax.ppermute(keys, "core", swap)
     v_got = lax.ppermute(values, "core", swap)
     l_got = lax.ppermute(block_lists, "core", swap)
-    lists = jnp.concatenate([block_lists, l_got], axis=1).astype(jnp.bfloat16)
-    lists = lists.reshape(lists.shape[0], lists.shape[1] * lists.shape[2])
+    lines = [part[:, tile] for part in (block_lists, l_got) for tile in range(block_lists.shape[1])]
+    lists = jnp.concatenate(lines, axis=1).astype(jnp.bfloat16)
     lists = jnp.pad(lists, ((0, 0), (0, half - lists.shape[1])))
     def halves(part, got):
         return [lax.dynamic_slice_in_dim(part, own, half, 1), lax.dynamic_slice_in_dim(got, own, half, 1)]
@@ -315,10 +348,11 @@
     state = pl.pallas_call(
         functools.partial(near_kernel, z_size, heads),
         out_shape=(
-            jax.ShapeDtypeStruct((2, kv_heads, group_rows, wide), jnp.bfloat16),
-            jax.ShapeDtypeStruct((2, kv_heads, group_rows, wide), jnp.float32),
-            jax.ShapeDtypeStruct((2, kv_heads, group_rows, HEAD_DIMENSION), jnp.float32),
-        ),
+            jax.ShapeDtypeStruct((kv_heads, group_rows, wide), jnp.bfloat16),
+            jax.ShapeDtypeStruct((kv_heads, group_rows, wide), jnp.float32),
+            jax.ShapeDtypeStruct((kv_heads, group_rows, HEAD_DIMENSION), jnp.float32),
+        )
+        * 2,
         scratch_shapes=[
             pltpu.VMEM((kv_heads, near_rows, wide), jnp.bfloat16),
             pltpu.VMEM((kv_heads, near_rows, wide), jnp.bfloat16),
@@ -335,12 +369,14 @@
 
     def finish(side, whole):
         return pl.pallas_call(
-            functools.partial(far_kernel, z_size, side, whole),
+            functools.partial(far_kernel, z_size, whole),
             out_shape=jax.ShapeDtypeStruct((rows, q_width * (2 if whole else 1)), jnp.bfloat16),
+            out_specs=pl.BlockSpec(memory_space=pl.ANY if whole else pltpu.VMEM),
             scratch_shapes=[
                 pltpu.VMEM((kv_heads, unit_rows, wide), jnp.bfloat16),
                 pltpu.VMEM((kv_heads, unit_rows, wide), jnp.bfloat16),
-            ],
+            ]
+            + ([pltpu.VMEM((rows, q_width), jnp.bfloat16), pltpu.SemaphoreType.DMA((kv_heads,))] if whole else []),
             compiler_params=pltpu.CompilerParams(vmem_limit_bytes=40 * 2**20),
             cost_estimate=pl.CostEstimate(
                 flops=4 * kv_heads * group_rows * unit_rows * wide,
@@ -348,7 +384,7 @@
                 transcendentals=2 * kv_heads * group_rows * unit_rows,
             ),
             name="far_own" if whole else "far_other",
-        )(*state, k_far, v_far)
+        )(*state[3 * side : 3 * side + 3], k_far, v_far)
 
     back_home = lax.ppermute(finish(1, False), "core", swap)
     return lax.dynamic_update_slice_in_dim(finish(0, True), back_home, q_width - core * q_width, 1)

time: 39.7 us -> 39 us (0.982)
  Pallas kernels: 9.46 us -> 8.82 us
  transfers between devices with their start and end apart: 19 -> 19, of which waited for: 6 -> 6; matrix products, arithmetic and copies ran while one was open for 9% -> 10% of each run, Pallas kernels for 21% -> 20%
where the time goes in v4:
time: 39 us; the launch traced here: 38.8 us
  starting transfers between devices  15.4 us (39%)
  waiting for transfers between devices  9.95 us (26%)
  Pallas kernels  8.82 us (23%)
  local copies, waits for them, and re-layouts  3.7 us (9%)
  other arithmetic  0.83 us (2%)
    ppermute x3, waiting for transfers between devices, per_device_ring(): k_ahead.append(lax.ppermute(k_ahead[-1], axes, ahead))  6.2 us
    pallas_call x1, Pallas kernels, per_device_ring(): pl.pallas_call(functools.partial(near_kernel, z_size, heads), out_shape=(...  5.79 us
    ppermute x3, starting transfers between devices, per_device_ring(): v_back.append(lax.ppermute(v_back[-1], axes, back))  3.92 us
    ppermute x3, waiting for transfers between devices, per_device_ring(): v_back.append(lax.ppermute(v_back[-1], axes, back))  3.71 us
    ppermute x1, starting transfers between devices, per_device_ring(): back_home = lax.ppermute(finish(1, False), 'core', swap)  3.35 us
    pallas_call x2, Pallas kernels, finish(): pl.pallas_call(functools.partial(far_kernel, z_size, whole), out_shape=ja...  3.03 us
    ppermute x3, starting transfers between devices, per_device_ring(): k_ahead.append(lax.ppermute(k_ahead[-1], axes, ahead))  2.77 us
    dynamic_slice x2, local copies, waits for them, and re-layouts, halves(): lax.dynamic_slice_in_dim(part, own, half, 1)  1.69 us
  transfers between devices with their start and end apart: 19, of which 6 were waited for; matrix products, arithmetic and copies ran while one was open for 10% of the time, Pallas kernels for 20%

profile of v4, /device:TPU:1, one launch (start us, length us, event | category | flops | bytes accessed | tf_op | source)
XLA Modules:
  0.0 38.8 jit_solution(1453751045878668834)
XLA Ops:
  0.1 1.2 %constant_dynamic-slice_fusion.2 = bf16[64,4096]{1,0:T(8,128)(2,1)S(1)} fusion(bf16[64,8192]{1,0:T(8,128)(2,1)} %refs_0_.1, s32[]{:T(128)S(6)} %select_n.5), kind=kLoop, calls=%fused_computation.17 | loop fusion | bytes 1048580 | tf_op jit(solution)/shard_map/dynamic_slice | solution.py:331
  1.2 0.4 %collective-permute-start.1 = (bf16[64,4096]{1,0:T(8,128)(2,1)S(1)}, bf16[64,4096]{1,0:T(8,128)(2,1)S(1)}, u32[]{:S(2)}, u32[]{:S(2)}) collective-permute-start(bf16[64,4096]{1,0:T(8,128)(2,1)S(1)} %constant_dynamic-slice_fusion.2), channel_id=1, source_target_pairs={{0,1},{1,0},{2,3},{3,2},{4,5},{5,4},{6,7},{7,6},{8,9},{9,8},{10,11... | collective-permute-start | bytes 1572872 | tf_op jit(solution)/shard_map/ppermute | solution.py:332
  1.7 0.1 collective-permute-start.8
  1.8 0.7 %copy_convert_fusion = (bf16[16,2,16]{2,0,1:T(8,128)(2,1)S(1)}, s32[16,2,16]{2,0,1:T(8,128)S(1)}) fusion(s32[16,2,16]{2,1,0:T(2,128)} %param.8), kind=kLoop, calls=%fused_computation.20 | loop fusion | flops 512 | bytes 5120 | tf_op jit(solution)/shard_map/convert.11
  2.5 0.4 collective-permute-start.9
  2.9 0.8 %constant_dynamic-slice_fusion.4 = bf16[64,512]{1,0:T(8,128)(2,1)S(1)} fusion(bf16[64,1024]{1,0:T(8,128)(2,1)} %param.6, s32[]{:T(128)S(6)} %select_n.4), kind=kLoop, calls=%fused_computation.19 | loop fusion | bytes 131076 | tf_op jit(solution)/shard_map/dynamic_slice | solution.py:326
  3.7 0.8 %constant_dynamic-slice_fusion.1 = bf16[64,512]{1,0:T(8,128)(2,1)S(1)} fusion(bf16[64,1024]{1,0:T(8,128)(2,1)} %param.7, s32[]{:T(128)S(6)} %select_n.4), kind=kLoop, calls=%fused_computation.16 | loop fusion | bytes 131076 | tf_op jit(solution)/shard_map/dynamic_slice | solution.py:326
  4.6 0.1 fusion.6
  4.7 2.3 %collective-permute-start.13 = (bf16[144,512]{1,0:T(8,128)(2,1)S(1)}, bf16[144,512]{1,0:T(8,128)(2,1)S(1)}, u32[]{:S(2)}, u32[]{:S(2)}) collective-permute-start(bf16[144,512]{1,0:T(8,128)(2,1)S(1)} %pad_maximum_fusion.refs_9_), channel_id=1, source_target_pairs={{0,2},{1,3},{4,0},{5,1},{8,4},{9,5},{12,8},{13,9},{14,12},{15,13},... | collective-permute-start | bytes 442376 | tf_op jit(solution)/shard_map/ppermute | solution.py:339
  7.1 0.2 collective-permute-start.10
  7.3 1.5 %collective-permute-start.2 = (bf16[128,512]{1,0:T(8,128)(2,1)S(1)}, bf16[128,512]{1,0:T(8,128)(2,1)S(1)}, u32[]{:S(2)}, u32[]{:S(2)}) collective-permute-start(bf16[128,512]{1,0:T(8,128)(2,1)S(1)} %pad_maximum_fusion.1.refs_2_), channel_id=1, source_target_pairs={{0,4},{1,5},{4,8},{5,9},{8,12},{9,13},{12,14},{13,15},{14,10},{15,... | collective-permute-start | bytes 393224 | tf_op jit(solution)/shard_map/ppermute | solution.py:336
  8.8 2.2 %collective-permute-done.13.refs_13_ = bf16[144,512]{1,0:T(8,128)(2,1)S(1)} collective-permute-done((bf16[144,512]{1,0:T(8,128)(2,1)S(1)}, bf16[144,512]{1,0:T(8,128)(2,1)S(1)}, u32[]{:S(2)}, u32[]{:S(2)}) %collective-permute-start.13) | collective-permute-done | bytes 147488 | tf_op jit(solution)/shard_map/ppermute | solution.py:339
  11.0 1.1 %collective-permute-start.14 = (bf16[144,512]{1,0:T(8,128)(2,1)S(1)}, bf16[144,512]{1,0:T(8,128)(2,1)S(1)}, u32[]{:S(2)}, u32[]{:S(2)}) collective-permute-start(bf16[144,512]{1,0:T(8,128)(2,1)S(1)} %collective-permute-done.13.refs_13_), channel_id=1, source_target_pairs={{0,2},{1,3},{4,0},{5,1},{8,4},{9,5},{12,8},{13,9},{14,12},{15,13},... | collective-permute-start | bytes 442376 | tf_op jit(solution)/shard_map/ppermute | solution.py:339
  12.1 0.4 %collective-permute-start.11 = (bf16[144,512]{1,0:T(8,128)(2,1)S(1)}, bf16[144,512]{1,0:T(8,128)(2,1)S(1)}, u32[]{:S(2)}, u32[]{:S(2)}) collective-permute-start(bf16[144,512]{1,0:T(8,128)(2,1)S(1)} %collective-permute-done.10.refs_10_), channel_id=1, source_target_pairs={{0,4},{1,5},{4,8},{5,9},{8,12},{9,13},{12,14},{13,15},{14,10},{15,... | collective-permute-start | bytes 442376 | tf_op jit(solution)/shard_map/ppermute | solution.py:338
  12.5 2.1 %collective-permute-done.2.refs_3_ = bf16[128,512]{1,0:T(8,128)(2,1)S(1)} collective-permute-done((bf16[128,512]{1,0:T(8,128)(2,1)S(1)}, bf16[128,512]{1,0:T(8,128)(2,1)S(1)}, u32[]{:S(2)}, u32[]{:S(2)}) %collective-permute-start.2) | collective-permute-done | bytes 131104 | tf_op jit(solution)/shard_map/ppermute | solution.py:336
  14.6 0.5 %collective-permute-start.3 = (bf16[128,512]{1,0:T(8,128)(2,1)S(1)}, bf16[128,512]{1,0:T(8,128)(2,1)S(1)}, u32[]{:S(2)}, u32[]{:S(2)}) collective-permute-start(bf16[128,512]{1,0:T(8,128)(2,1)S(1)} %collective-permute-done.2.refs_3_), channel_id=1, source_target_pairs={{0,4},{1,5},{4,8},{5,9},{8,12},{9,13},{12,14},{13,15},{14,10},{15,... | collective-permute-start | bytes 393224 | tf_op jit(solution)/shard_map/ppermute | solution.py:336
  15.0 1.0 %collective-permute-start.6 = (bf16[128,512]{1,0:T(8,128)(2,1)S(1)}, bf16[128,512]{1,0:T(8,128)(2,1)S(1)}, u32[]{:S(2)}, u32[]{:S(2)}) collective-permute-start(bf16[128,512]{1,0:T(8,128)(2,1)S(1)} %collective-permute-done.5.refs_6_), channel_id=1, source_target_pairs={{0,2},{1,3},{4,0},{5,1},{8,4},{9,5},{12,8},{13,9},{14,12},{15,13},... | collective-permute-start | bytes 393224 | tf_op jit(solution)/shard_map/ppermute | solution.py:337
  16.0 0.8 %collective-permute-done.14.refs_14_ = bf16[144,512]{1,0:T(8,128)(2,1)S(1)} collective-permute-done((bf16[144,512]{1,0:T(8,128)(2,1)S(1)}, bf16[144,512]{1,0:T(8,128)(2,1)S(1)}, u32[]{:S(2)}, u32[]{:S(2)}) %collective-permute-start.14) | collective-permute-done | bytes 147488 | tf_op jit(solution)/shard_map/ppermute | solution.py:339
  16.8 0.5 %collective-permute-start.15 = (bf16[144,512]{1,0:T(8,128)(2,1)S(1)}, bf16[144,512]{1,0:T(8,128)(2,1)S(1)}, u32[]{:S(2)}, u32[]{:S(2)}) collective-permute-start(bf16[144,512]{1,0:T(8,128)(2,1)S(1)} %collective-permute-done.14.refs_14_), channel_id=1, source_target_pairs={{0,2},{1,3},{4,0},{5,1},{8,4},{9,5},{12,8},{13,9},{14,12},{15,13},... | collective-permute-start | bytes 442376 | tf_op jit(solution)/shard_map/ppermute | solution.py:339
  17.3 1.0 %collective-permute-start.12 = (bf16[144,512]{1,0:T(8,128)(2,1)S(1)}, bf16[144,512]{1,0:T(8,128)(2,1)S(1)}, u32[]{:S(2)}, u32[]{:S(2)}) collective-permute-start(bf16[144,512]{1,0:T(8,128)(2,1)S(1)} %collective-permute-done.11.refs_11_), channel_id=1, source_target_pairs={{0,4},{1,5},{4,8},{5,9},{8,12},{9,13},{12,14},{13,15},{14,10},{15,... | collective-permute-start | bytes 442376 | tf_op jit(solution)/shard_map/ppermute | solution.py:338
  18.3 1.4 %collective-permute-done.3.refs_4_ = bf16[128,512]{1,0:T(8,128)(2,1)S(1)} collective-permute-done((bf16[128,512]{1,0:T(8,128)(2,1)S(1)}, bf16[128,512]{1,0:T(8,128)(2,1)S(1)}, u32[]{:S(2)}, u32[]{:S(2)}) %collective-permute-start.3) | collective-permute-done | bytes 131104 | tf_op jit(solution)/shard_map/ppermute | solution.py:336
  19.7 0.8 %collective-permute-start.4 = (bf16[128,512]{1,0:T(8,128)(2,1)S(1)}, bf16[128,512]{1,0:T(8,128)(2,1)S(1)}, u32[]{:S(2)}, u32[]{:S(2)}) collective-permute-start(bf16[128,512]{1,0:T(8,128)(2,1)S(1)} %collective-permute-done.3.refs_4_), channel_id=1, source_target_pairs={{0,4},{1,5},{4,8},{5,9},{8,12},{9,13},{12,14},{13,15},{14,10},{15,... | collective-permute-start | bytes 393224 | tf_op jit(solution)/shard_map/ppermute | solution.py:336
  20.6 0.6 %collective-permute-start.7 = (bf16[128,512]{1,0:T(8,128)(2,1)S(1)}, bf16[128,512]{1,0:T(8,128)(2,1)S(1)}, u32[]{:S(2)}, u32[]{:S(2)}) collective-permute-start(bf16[128,512]{1,0:T(8,128)(2,1)S(1)} %collective-permute-done.6.refs_7_), channel_id=1, source_target_pairs={{0,2},{1,3},{4,0},{5,1},{8,4},{9,5},{12,8},{13,9},{14,12},{15,13},... | collective-permute-start | bytes 393224 | tf_op jit(solution)/shard_map/ppermute | solution.py:337
  21.2 0.7 %collective-permute-done.15.refs_15_ = bf16[144,512]{1,0:T(8,128)(2,1)S(1)} collective-permute-done((bf16[144,512]{1,0:T(8,128)(2,1)S(1)}, bf16[144,512]{1,0:T(8,128)(2,1)S(1)}, u32[]{:S(2)}, u32[]{:S(2)}) %collective-permute-start.15) | collective-permute-done | bytes 147488 | tf_op jit(solution)/shard_map/ppermute | solution.py:339
  21.9 0.7 %collective-permute-start.17 = (bf16[128,512]{1,0:T(8,128)(2,1)S(1)}, bf16[128,512]{1,0:T(8,128)(2,1)S(1)}, u32[]{:S(2)}, u32[]{:S(2)}) collective-permute-start(bf16[128,512]{1,0:T(8,128)(2,1)S(1)} %slice.28), channel_id=1, source_target_pairs={{0,2},{1,3},{4,0},{5,1},{8,4},{9,5},{12,8},{13,9},{14,12},{15,13},... | collective-permute-start | bytes 393224 | tf_op jit(solution)/shard_map/ppermute | solution.py:342
  22.5 2.7 %collective-permute-done.4.refs_5_ = bf16[128,512]{1,0:T(8,128)(2,1)S(1)} collective-permute-done((bf16[128,512]{1,0:T(8,128)(2,1)S(1)}, bf16[128,512]{1,0:T(8,128)(2,1)S(1)}, u32[]{:S(2)}, u32[]{:S(2)}) %collective-permute-start.4) | collective-permute-done | bytes 131104 | tf_op jit(solution)/shard_map/ppermute | solution.py:336
  25.3 0.4 %collective-permute-start.16 = (bf16[128,512]{1,0:T(8,128)(2,1)S(1)}, bf16[128,512]{1,0:T(8,128)(2,1)S(1)}, u32[]{:S(2)}, u32[]{:S(2)}) collective-permute-start(bf16[128,512]{1,0:T(8,128)(2,1)S(1)} %collective-permute-done.4.refs_5_), channel_id=1, source_target_pairs={{0,4},{1,5},{4,8},{5,9},{8,12},{9,13},{12,14},{13,15},{14,10},{15,... | collective-permute-start | bytes 393224 | tf_op jit(solution)/shard_map/ppermute | solution.py:341
  25.7 5.8 %near.1 = (bf16[4,512,256]{2,1,0:T(8,128)(2,1)S(1)}, f32[4,512,256]{2,1,0:T(8,128)S(1)}, f32[4,512,128]{2,1,0:T(8,128)S(1)}, bf16[4,512,256]{2,1,0:T(8,128)(2,1)...) custom-call(bf16[64,8192]{1,0:T(8,128)(2,1)S(1)} %copy-done, ...), custom_call_target="tpu_custom_call" | custom-call | flops 3758096384 | bytes 8388608 | tf_op jit(solution)/shard_map/near/pallas_call | solution.py:348
  31.5 1.2 %far_other.1 = bf16[64,4096]{1,0:T(8,128)(2,1)S(1)} custom-call(bf16[4,512,256]{2,1,0:T(8,128)(2,1)S(1)} %get-tuple-element.18.q_aug, f32[4,512,256]{2,1,0:T(8,128)S(1)} %get-tuple-element.19.total, f32[4,512,128]{2,1,0:T(8,128)S(1)} %get-tuple-element.20.top, bf16[128,512]{1,0:T(8,128)(2,1)S(1)} %collective-permute-done.16.k_far, ...), custom_call_target="tpu_custom_call" | custom-call | flops 268435456 | bytes 8388608 | tf_op jit(solution)/shard_map/far_other/pallas_call | solution.py:371
  32.7 3.3 %collective-permute-start.18 = (bf16[64,4096]{1,0:T(8,128)(2,1)S(1)}, bf16[64,4096]{1,0:T(8,128)(2,1)S(1)}, u32[]{:S(2)}, u32[]{:S(2)}) collective-permute-start(bf16[64,4096]{1,0:T(8,128)(2,1)S(1)} %far_other.1), channel_id=1, source_target_pairs={{0,1},{1,0},{2,3},{3,2},{4,5},{5,4},{6,7},{7,6},{8,9},{9,8},{10,11... | collective-permute-start | bytes 1572872 | tf_op jit(solution)/shard_map/ppermute | solution.py:389
  36.1 1.9 %far_own.1 = bf16[64,8192]{1,0:T(8,128)(2,1)} custom-call(bf16[4,512,256]{2,1,0:T(8,128)(2,1)S(1)} %get-tuple-element.15.q_aug, f32[4,512,256]{2,1,0:T(8,128)S(1)} %get-tuple-element.16.total, f32[4,512,128]{2,1,0:T(8,128)S(1)} %get-tuple-element.17.top, bf16[128,512]{1,0:T(8,128)(2,1)S(1)} %collective-permute-done.16.k_far, ...), custom_call_target="tpu_custom_call" | custom-call | flops 268435456 | bytes 8388608 | tf_op jit(solution)/shard_map/far_own/pallas_call | solution.py:371
  37.9 0.8 %constant_dynamic-update-slice_fusion = bf16[64,8192]{1,0:T(8,128)(2,1)} fusion(bf16[64,8192]{1,0:T(8,128)(2,1)} %far_own.1, bf16[64,4096]{1,0:T(8,128)(2,1)S(1)} %collective-permute-done.18, s32[]{:T(128)S(6)} %select_n.5), kind=kLoop, calls=%fused_computation.14 | loop fusion | bytes 1048580 | tf_op jit(solution)/shard_map/dynamic_update_slice | solution.py:390
  (25 shorter events, 0.2 us)
Async XLA Ops:
  0.0 25.7 %copy-start = (bf16[64,8192]{1,0:T(8,128)(2,1)S(1)}, bf16[64,8192]{1,0:T(8,128)(2,1)}, u32[]{:S(2)}) copy-start(bf16[64,8192]{1,0:T(8,128)(2,1)} %refs_0_.1) | copy-start | bytes 3145732
  0.0 7.2 %collective-permute-start = (bf16[64,1024]{1,0:T(8,128)(2,1)}, bf16[64,1024]{1,0:T(8,128)(2,1)S(1)}, u32[]{:S(2)}, u32[]{:S(2)}) collective-permute-start(bf16[64,1024]{1,0:T(8,128)(2,1)} %param.6), channel_id=1, source_target_pairs={{0,1},{1,0},{2,3},{3,2},{4,5},{5,4},{6,7},{7,6},{8,9},{9,8},{10,11... | collective-permute-start | bytes 393224 | tf_op jit(solution)/shard_map/ppermute | solution.py:319
  1.2 6.0 %collective-permute-start.1 = (bf16[64,4096]{1,0:T(8,128)(2,1)S(1)}, bf16[64,4096]{1,0:T(8,128)(2,1)S(1)}, u32[]{:S(2)}, u32[]{:S(2)}) collective-permute-start(bf16[64,4096]{1,0:T(8,128)(2,1)S(1)} %constant_dynamic-slice_fusion.2), channel_id=1, source_target_pairs={{0,1},{1,0},{2,3},{3,2},{4,5},{5,4},{6,7},{7,6},{8,9},{9,8},{10,11... | collective-permute-start | bytes 1572872 | tf_op jit(solution)/shard_map/ppermute | solution.py:332
  1.7 3.0 %collective-permute-start.8 = (bf16[64,1024]{1,0:T(8,128)(2,1)}, bf16[64,1024]{1,0:T(8,128)(2,1)S(1)}, u32[]{:S(2)}, u32[]{:S(2)}) collective-permute-start(bf16[64,1024]{1,0:T(8,128)(2,1)} %param.7), channel_id=1, source_target_pairs={{0,1},{1,0},{2,3},{3,2},{4,5},{5,4},{6,7},{7,6},{8,9},{9,8},{10,11... | collective-permute-start | bytes 393224 | tf_op jit(solution)/shard_map/ppermute | solution.py:320
  2.5 2.1 %collective-permute-start.9 = (s32[16,2,16]{2,0,1:T(8,128)S(1)}, s32[16,2,16]{2,0,1:T(8,128)S(1)}, u32[]{:S(2)}, u32[]{:S(2)}) collective-permute-start(s32[16,2,16]{2,0,1:T(8,128)S(1)} %get-tuple-element.22), channel_id=1, source_target_pairs={{0,1},{1,0},{2,3},{3,2},{4,5},{5,4},{6,7},{7,6},{8,9},{9,8},{10,11... | collective-permute-start | bytes 6152 | tf_op jit(solution)/shard_map/ppermute | solution.py:321
  4.7 6.3 %collective-permute-start.13 = (bf16[144,512]{1,0:T(8,128)(2,1)S(1)}, bf16[144,512]{1,0:T(8,128)(2,1)S(1)}, u32[]{:S(2)}, u32[]{:S(2)}) collective-permute-start(bf16[144,512]{1,0:T(8,128)(2,1)S(1)} %pad_maximum_fusion.refs_9_), channel_id=1, source_target_pairs={{0,2},{1,3},{4,0},{5,1},{8,4},{9,5},{12,8},{13,9},{14,12},{15,13},... | collective-permute-start | bytes 442376 | tf_op jit(solution)/shard_map/ppermute | solution.py:339
  7.1 5.0 %collective-permute-start.10 = (bf16[144,512]{1,0:T(8,128)(2,1)S(1)}, bf16[144,512]{1,0:T(8,128)(2,1)S(1)}, u32[]{:S(2)}, u32[]{:S(2)}) collective-permute-start(bf16[144,512]{1,0:T(8,128)(2,1)S(1)} %pad_maximum_fusion.refs_9_), channel_id=1, source_target_pairs={{0,4},{1,5},{4,8},{5,9},{8,12},{9,13},{12,14},{13,15},{14,10},{15,... | collective-permute-start | bytes 442376 | tf_op jit(solution)/shard_map/ppermute | solution.py:338
  7.3 7.3 %collective-permute-start.2 = (bf16[128,512]{1,0:T(8,128)(2,1)S(1)}, bf16[128,512]{1,0:T(8,128)(2,1)S(1)}, u32[]{:S(2)}, u32[]{:S(2)}) collective-permute-start(bf16[128,512]{1,0:T(8,128)(2,1)S(1)} %pad_maximum_fusion.1.refs_2_), channel_id=1, source_target_pairs={{0,4},{1,5},{4,8},{5,9},{8,12},{9,13},{12,14},{13,15},{14,10},{15,... | collective-permute-start | bytes 393224 | tf_op jit(solution)/shard_map/ppermute | solution.py:336
  8.7 6.3 %collective-permute-start.5 = (bf16[128,512]{1,0:T(8,128)(2,1)S(1)}, bf16[128,512]{1,0:T(8,128)(2,1)S(1)}, u32[]{:S(2)}, u32[]{:S(2)}) collective-permute-start(bf16[128,512]{1,0:T(8,128)(2,1)S(1)} %pad_maximum_fusion.1.refs_2_), channel_id=1, source_target_pairs={{0,2},{1,3},{4,0},{5,1},{8,4},{9,5},{12,8},{13,9},{14,12},{15,13},... | collective-permute-start | bytes 393224 | tf_op jit(solution)/shard_map/ppermute | solution.py:337
  11.0 5.8 %collective-permute-start.14 = (bf16[144,512]{1,0:T(8,128)(2,1)S(1)}, bf16[144,512]{1,0:T(8,128)(2,1)S(1)}, u32[]{:S(2)}, u32[]{:S(2)}) collective-permute-start(bf16[144,512]{1,0:T(8,128)(2,1)S(1)} %collective-permute-done.13.refs_13_), channel_id=1, source_target_pairs={{0,2},{1,3},{4,0},{5,1},{8,4},{9,5},{12,8},{13,9},{14,12},{15,13},... | collective-permute-start | bytes 442376 | tf_op jit(solution)/shard_map/ppermute | solution.py:339
  12.1 5.3 %collective-permute-start.11 = (bf16[144,512]{1,0:T(8,128)(2,1)S(1)}, bf16[144,512]{1,0:T(8,128)(2,1)S(1)}, u32[]{:S(2)}, u32[]{:S(2)}) collective-permute-start(bf16[144,512]{1,0:T(8,128)(2,1)S(1)} %collective-permute-done.10.refs_10_), channel_id=1, source_target_pairs={{0,4},{1,5},{4,8},{5,9},{8,12},{9,13},{12,14},{13,15},{14,10},{15,... | collective-permute-start | bytes 442376 | tf_op jit(solution)/shard_map/ppermute | solution.py:338
  14.6 5.2 %collective-permute-start.3 = (bf16[128,512]{1,0:T(8,128)(2,1)S(1)}, bf16[128,512]{1,0:T(8,128)(2,1)S(1)}, u32[]{:S(2)}, u32[]{:S(2)}) collective-permute-start(bf16[128,512]{1,0:T(8,128)(2,1)S(1)} %collective-permute-done.2.refs_3_), channel_id=1, source_target_pairs={{0,4},{1,5},{4,8},{5,9},{8,12},{9,13},{12,14},{13,15},{14,10},{15,... | collective-permute-start | bytes 393224 | tf_op jit(solution)/shard_map/ppermute | solution.py:336
  15.0 5.5 %collective-permute-start.6 = (bf16[128,512]{1,0:T(8,128)(2,1)S(1)}, bf16[128,512]{1,0:T(8,128)(2,1)S(1)}, u32[]{:S(2)}, u32[]{:S(2)}) collective-permute-start(bf16[128,512]{1,0:T(8,128)(2,1)S(1)} %collective-permute-done.5.refs_6_), channel_id=1, source_target_pairs={{0,2},{1,3},{4,0},{5,1},{8,4},{9,5},{12,8},{13,9},{14,12},{15,13},... | collective-permute-start | bytes 393224 | tf_op jit(solution)/shard_map/ppermute | solution.py:337
  16.8 5.0 %collective-permute-start.15 = (bf16[144,512]{1,0:T(8,128)(2,1)S(1)}, bf16[144,512]{1,0:T(8,128)(2,1)S(1)}, u32[]{:S(2)}, u32[]{:S(2)}) collective-permute-start(bf16[144,512]{1,0:T(8,128)(2,1)S(1)} %collective-permute-done.14.refs_14_), channel_id=1, source_target_pairs={{0,2},{1,3},{4,0},{5,1},{8,4},{9,5},{12,8},{13,9},{14,12},{15,13},... | collective-permute-start | bytes 442376 | tf_op jit(solution)/shard_map/ppermute | solution.py:339
  17.3 8.4 %collective-permute-start.12 = (bf16[144,512]{1,0:T(8,128)(2,1)S(1)}, bf16[144,512]{1,0:T(8,128)(2,1)S(1)}, u32[]{:S(2)}, u32[]{:S(2)}) collective-permute-start(bf16[144,512]{1,0:T(8,128)(2,1)S(1)} %collective-permute-done.11.refs_11_), channel_id=1, source_target_pairs={{0,4},{1,5},{4,8},{5,9},{8,12},{9,13},{12,14},{13,15},{14,10},{15,... | collective-permute-start | bytes 442376 | tf_op jit(solution)/shard_map/ppermute | solution.py:338
  19.7 5.5 %collective-permute-start.4 = (bf16[128,512]{1,0:T(8,128)(2,1)S(1)}, bf16[128,512]{1,0:T(8,128)(2,1)S(1)}, u32[]{:S(2)}, u32[]{:S(2)}) collective-permute-start(bf16[128,512]{1,0:T(8,128)(2,1)S(1)} %collective-permute-done.3.refs_4_), channel_id=1, source_target_pairs={{0,4},{1,5},{4,8},{5,9},{8,12},{9,13},{12,14},{13,15},{14,10},{15,... | collective-permute-start | bytes 393224 | tf_op jit(solution)/shard_map/ppermute | solution.py:336
  20.6 5.2 %collective-permute-start.7 = (bf16[128,512]{1,0:T(8,128)(2,1)S(1)}, bf16[128,512]{1,0:T(8,128)(2,1)S(1)}, u32[]{:S(2)}, u32[]{:S(2)}) collective-permute-start(bf16[128,512]{1,0:T(8,128)(2,1)S(1)} %collective-permute-done.6.refs_7_), channel_id=1, source_target_pairs={{0,2},{1,3},{4,0},{5,1},{8,4},{9,5},{12,8},{13,9},{14,12},{15,13},... | collective-permute-start | bytes 393224 | tf_op jit(solution)/shard_map/ppermute | solution.py:337
  21.9 9.6 %collective-permute-start.17 = (bf16[128,512]{1,0:T(8,128)(2,1)S(1)}, bf16[128,512]{1,0:T(8,128)(2,1)S(1)}, u32[]{:S(2)}, u32[]{:S(2)}) collective-permute-start(bf16[128,512]{1,0:T(8,128)(2,1)S(1)} %slice.28), channel_id=1, source_target_pairs={{0,2},{1,3},{4,0},{5,1},{8,4},{9,5},{12,8},{13,9},{14,12},{15,13},... | collective-permute-start | bytes 393224 | tf_op jit(solution)/shard_map/ppermute | solution.py:342
  25.3 6.3 %collective-permute-start.16 = (bf16[128,512]{1,0:T(8,128)(2,1)S(1)}, bf16[128,512]{1,0:T(8,128)(2,1)S(1)}, u32[]{:S(2)}, u32[]{:S(2)}) collective-permute-start(bf16[128,512]{1,0:T(8,128)(2,1)S(1)} %collective-permute-done.4.refs_5_), channel_id=1, source_target_pairs={{0,4},{1,5},{4,8},{5,9},{8,12},{9,13},{12,14},{13,15},{14,10},{15,... | collective-permute-start | bytes 393224 | tf_op jit(solution)/shard_map/ppermute | solution.py:341
  32.7 5.2 %collective-permute-start.18 = (bf16[64,4096]{1,0:T(8,128)(2,1)S(1)}, bf16[64,4096]{1,0:T(8,128)(2,1)S(1)}, u32[]{:S(2)}, u32[]{:S(2)}) collective-permute-start(bf16[64,4096]{1,0:T(8,128)(2,1)S(1)} %far_other.1), channel_id=1, source_target_pairs={{0,1},{1,0},{2,3},{3,2},{4,5},{5,4},{6,7},{7,6},{8,9},{9,8},{10,11... | collective-permute-start | bytes 1572872 | tf_op jit(solution)/shard_map/ppermute | solution.py:389

commit v5 on v4

--- a/solution.py
+++ b/solution.py
@@ -305,6 +305,15 @@
         copy.wait()
 
 
+def join_kernel(half_done, got, out, sem):
+    del half_done
+    span = got.shape[1]
+    start = pl.multiple_of((1 - lax.axis_index("core")) * span, span)
+    copy = pltpu.make_async_copy(got, out.at[:, pl.ds(start, span)], sem)
+    copy.start()
+    copy.wait()
+
+
 def per_device_ring(z_size, queries, keys, values, block_lists, block_counts):
     del block_counts
     rows = queries.shape[0]
@@ -334,8 +343,8 @@
     k_ahead, k_back, v_ahead, v_back = [k_unit], [k_unit], [v_unit], [v_unit]
     for _ in range(z_size - 1):
         k_ahead.append(lax.ppermute(k_ahead[-1], axes, ahead))
+        v_ahead.append(lax.ppermute(v_ahead[-1], axes, ahead))
         k_back.append(lax.ppermute(k_back[-1], axes, back))
-        v_ahead.append(lax.ppermute(v_ahead[-1], axes, ahead))
         v_back.append(lax.ppermute(v_back[-1], axes, back))
     unit_rows = 2 * rows
     k_far = lax.ppermute(k_ahead[-1], axes, ahead)
@@ -377,7 +386,7 @@
                 pltpu.VMEM((kv_heads, unit_rows, wide), jnp.bfloat16),
             ]
             + ([pltpu.VMEM((rows, q_width), jnp.bfloat16), pltpu.SemaphoreType.DMA((kv_heads,))] if whole else []),
-            compiler_params=pltpu.CompilerParams(vmem_limit_bytes=40 * 2**20),
+            compiler_params=pltpu.CompilerParams(vmem_limit_bytes=30 * 2**20),
             cost_estimate=pl.CostEstimate(
                 flops=4 * kv_heads * group_rows * unit_rows * wide,
                 bytes_accessed=8 * 2**20,
@@ -387,7 +396,16 @@
         )(*state[3 * side : 3 * side + 3], k_far, v_far)
 
     back_home = lax.ppermute(finish(1, False), "core", swap)
-    return lax.dynamic_update_slice_in_dim(finish(0, True), back_home, q_width - core * q_width, 1)
+    return pl.pallas_call(
+        join_kernel,
+        out_shape=jax.ShapeDtypeStruct((rows, 2 * q_width), jnp.bfloat16),
+        in_specs=[pl.BlockSpec(memory_space=pl.ANY)] * 2,
+        out_specs=pl.BlockSpec(memory_space=pl.ANY),
+        scratch_shapes=[pltpu.SemaphoreType.DMA],
+        input_output_aliases={0: 0},
+        compiler_params=pltpu.CompilerParams(vmem_limit_bytes=30 * 2**20),
+        name="join",
+    )(finish(0, True), back_home)
 
 
 def solution(mesh):

time: 39 us -> 39 us (level)
  local copies, waits for them, and re-layouts: 3.7 us -> 2.87 us
  Pallas kernels: 8.82 us -> 9.63 us
    dynamic_update_slice x1 -> x0, local copies, waits for them, and re-layouts: 0.83 us -> none  [per_device_ring(): lax.dynamic_update_slice_in_dim(finish(0, True), back_home, q_width - cor...]
    pallas_call x0 -> x1, Pallas kernels: none -> 0.81 us  [per_device_ring(): pl.pallas_call(join_kernel, out_shape=jax.ShapeDtypeStruct((rows, 2 * q_w...]
where the time goes in v5:
time: 39 us; the launch traced here: 38.7 us
  starting transfers between devices  15.4 us (39%)
  waiting for transfers between devices  9.95 us (26%)
  Pallas kernels  9.63 us (25%)
  local copies, waits for them, and re-layouts  2.87 us (7%)
  other arithmetic  0.83 us (2%)
    ppermute x3, waiting for transfers between devices, per_device_ring(): k_ahead.append(lax.ppermute(k_ahead[-1], axes, ahead))  6.2 us
    pallas_call x1, Pallas kernels, per_device_ring(): pl.pallas_call(functools.partial(near_kernel, z_size, heads), out_shape=(...  5.78 us
    ppermute x3, starting transfers between devices, per_device_ring(): v_back.append(lax.ppermute(v_back[-1], axes, back))  3.92 us
    ppermute x3, waiting for transfers between devices, per_device_ring(): v_back.append(lax.ppermute(v_back[-1], axes, back))  3.71 us
    ppermute x1, starting transfers between devices, per_device_ring(): back_home = lax.ppermute(finish(1, False), 'core', swap)  3.35 us
    pallas_call x2, Pallas kernels, finish(): pl.pallas_call(functools.partial(far_kernel, z_size, whole), out_shape=ja...  3.03 us
    ppermute x3, starting transfers between devices, per_device_ring(): k_ahead.append(lax.ppermute(k_ahead[-1], axes, ahead))  2.77 us
    dynamic_slice x2, local copies, waits for them, and re-layouts, halves(): lax.dynamic_slice_in_dim(part, own, half, 1)  1.69 us
  transfers between devices with their start and end apart: 19, of which 6 were waited for; matrix products, arithmetic and copies ran while one was open for 10% of the time, Pallas kernels for 20%

profile of v5, /device:TPU:1, one launch (start us, length us, event | category | flops | bytes accessed | tf_op | source)
XLA Modules:
  0.0 38.7 jit_solution(11884709732247163909)
XLA Ops:
  0.1 1.2 %constant_dynamic-slice_fusion.2 = bf16[64,4096]{1,0:T(8,128)(2,1)S(1)} fusion(bf16[64,8192]{1,0:T(8,128)(2,1)} %refs_0_.1, s32[]{:T(128)S(6)} %select_n.10), kind=kLoop, calls=%fused_computation.16 | loop fusion | bytes 1048580 | tf_op jit(solution)/shard_map/dynamic_slice | solution.py:340
  1.2 0.4 %collective-permute-start.1 = (bf16[64,4096]{1,0:T(8,128)(2,1)S(1)}, bf16[64,4096]{1,0:T(8,128)(2,1)S(1)}, u32[]{:S(2)}, u32[]{:S(2)}) collective-permute-start(bf16[64,4096]{1,0:T(8,128)(2,1)S(1)} %constant_dynamic-slice_fusion.2), channel_id=1, source_target_pairs={{0,1},{1,0},{2,3},{3,2},{4,5},{5,4},{6,7},{7,6},{8,9},{9,8},{10,11... | collective-permute-start | bytes 1572872 | tf_op jit(solution)/shard_map/ppermute | solution.py:341
  1.7 0.1 collective-permute-start.8
  1.8 0.7 %copy_convert_fusion = (bf16[16,2,16]{2,0,1:T(8,128)(2,1)S(1)}, s32[16,2,16]{2,0,1:T(8,128)S(1)}) fusion(s32[16,2,16]{2,1,0:T(2,128)} %param.8), kind=kLoop, calls=%fused_computation.19 | loop fusion | flops 512 | bytes 5120 | tf_op jit(solution)/shard_map/convert.11
  2.5 0.4 collective-permute-start.9
  2.9 0.8 %constant_dynamic-slice_fusion.4 = bf16[64,512]{1,0:T(8,128)(2,1)S(1)} fusion(bf16[64,1024]{1,0:T(8,128)(2,1)} %param.6, s32[]{:T(128)S(6)} %select_n.4), kind=kLoop, calls=%fused_computation.18 | loop fusion | bytes 131076 | tf_op jit(solution)/shard_map/dynamic_slice | solution.py:335
  3.7 0.8 %constant_dynamic-slice_fusion.1 = bf16[64,512]{1,0:T(8,128)(2,1)S(1)} fusion(bf16[64,1024]{1,0:T(8,128)(2,1)} %param.7, s32[]{:T(128)S(6)} %select_n.4), kind=kLoop, calls=%fused_computation.15 | loop fusion | bytes 131076 | tf_op jit(solution)/shard_map/dynamic_slice | solution.py:335
  4.6 0.1 fusion.6
  4.7 2.3 %collective-permute-start.13 = (bf16[144,512]{1,0:T(8,128)(2,1)S(1)}, bf16[144,512]{1,0:T(8,128)(2,1)S(1)}, u32[]{:S(2)}, u32[]{:S(2)}) collective-permute-start(bf16[144,512]{1,0:T(8,128)(2,1)S(1)} %pad_maximum_fusion.refs_9_), channel_id=1, source_target_pairs={{0,2},{1,3},{4,0},{5,1},{8,4},{9,5},{12,8},{13,9},{14,12},{15,13},... | collective-permute-start | bytes 442376 | tf_op jit(solution)/shard_map/ppermute | solution.py:348
  7.1 0.2 collective-permute-start.10
  7.3 1.5 %collective-permute-start.2 = (bf16[128,512]{1,0:T(8,128)(2,1)S(1)}, bf16[128,512]{1,0:T(8,128)(2,1)S(1)}, u32[]{:S(2)}, u32[]{:S(2)}) collective-permute-start(bf16[128,512]{1,0:T(8,128)(2,1)S(1)} %pad_maximum_fusion.1.refs_2_), channel_id=1, source_target_pairs={{0,4},{1,5},{4,8},{5,9},{8,12},{9,13},{12,14},{13,15},{14,10},{15,... | collective-permute-start | bytes 393224 | tf_op jit(solution)/shard_map/ppermute | solution.py:345
  8.8 2.2 %collective-permute-done.13.refs_13_ = bf16[144,512]{1,0:T(8,128)(2,1)S(1)} collective-permute-done((bf16[144,512]{1,0:T(8,128)(2,1)S(1)}, bf16[144,512]{1,0:T(8,128)(2,1)S(1)}, u32[]{:S(2)}, u32[]{:S(2)}) %collective-permute-start.13) | collective-permute-done | bytes 147488 | tf_op jit(solution)/shard_map/ppermute | solution.py:348
  11.0 1.1 %collective-permute-start.14 = (bf16[144,512]{1,0:T(8,128)(2,1)S(1)}, bf16[144,512]{1,0:T(8,128)(2,1)S(1)}, u32[]{:S(2)}, u32[]{:S(2)}) collective-permute-start(bf16[144,512]{1,0:T(8,128)(2,1)S(1)} %collective-permute-done.13.refs_13_), channel_id=1, source_target_pairs={{0,2},{1,3},{4,0},{5,1},{8,4},{9,5},{12,8},{13,9},{14,12},{15,13},... | collective-permute-start | bytes 442376 | tf_op jit(solution)/shard_map/ppermute | solution.py:348
  12.1 0.4 %collective-permute-start.11 = (bf16[144,512]{1,0:T(8,128)(2,1)S(1)}, bf16[144,512]{1,0:T(8,128)(2,1)S(1)}, u32[]{:S(2)}, u32[]{:S(2)}) collective-permute-start(bf16[144,512]{1,0:T(8,128)(2,1)S(1)} %collective-permute-done.10.refs_10_), channel_id=1, source_target_pairs={{0,4},{1,5},{4,8},{5,9},{8,12},{9,13},{12,14},{13,15},{14,10},{15,... | collective-permute-start | bytes 442376 | tf_op jit(solution)/shard_map/ppermute | solution.py:346
  12.5 2.1 %collective-permute-done.2.refs_3_ = bf16[128,512]{1,0:T(8,128)(2,1)S(1)} collective-permute-done((bf16[128,512]{1,0:T(8,128)(2,1)S(1)}, bf16[128,512]{1,0:T(8,128)(2,1)S(1)}, u32[]{:S(2)}, u32[]{:S(2)}) %collective-permute-start.2) | collective-permute-done | bytes 131104 | tf_op jit(solution)/shard_map/ppermute | solution.py:345
  14.6 0.5 %collective-permute-start.3 = (bf16[128,512]{1,0:T(8,128)(2,1)S(1)}, bf16[128,512]{1,0:T(8,128)(2,1)S(1)}, u32[]{:S(2)}, u32[]{:S(2)}) collective-permute-start(bf16[128,512]{1,0:T(8,128)(2,1)S(1)} %collective-permute-done.2.refs_3_), channel_id=1, source_target_pairs={{0,4},{1,5},{4,8},{5,9},{8,12},{9,13},{12,14},{13,15},{14,10},{15,... | collective-permute-start | bytes 393224 | tf_op jit(solution)/shard_map/ppermute | solution.py:345
  15.0 1.0 %collective-permute-start.6 = (bf16[128,512]{1,0:T(8,128)(2,1)S(1)}, bf16[128,512]{1,0:T(8,128)(2,1)S(1)}, u32[]{:S(2)}, u32[]{:S(2)}) collective-permute-start(bf16[128,512]{1,0:T(8,128)(2,1)S(1)} %collective-permute-done.5.refs_6_), channel_id=1, source_target_pairs={{0,2},{1,3},{4,0},{5,1},{8,4},{9,5},{12,8},{13,9},{14,12},{15,13},... | collective-permute-start | bytes 393224 | tf_op jit(solution)/shard_map/ppermute | solution.py:347
  16.0 0.8 %collective-permute-done.14.refs_14_ = bf16[144,512]{1,0:T(8,128)(2,1)S(1)} collective-permute-done((bf16[144,512]{1,0:T(8,128)(2,1)S(1)}, bf16[144,512]{1,0:T(8,128)(2,1)S(1)}, u32[]{:S(2)}, u32[]{:S(2)}) %collective-permute-start.14) | collective-permute-done | bytes 147488 | tf_op jit(solution)/shard_map/ppermute | solution.py:348
  16.8 0.5 %collective-permute-start.15 = (bf16[144,512]{1,0:T(8,128)(2,1)S(1)}, bf16[144,512]{1,0:T(8,128)(2,1)S(1)}, u32[]{:S(2)}, u32[]{:S(2)}) collective-permute-start(bf16[144,512]{1,0:T(8,128)(2,1)S(1)} %collective-permute-done.14.refs_14_), channel_id=1, source_target_pairs={{0,2},{1,3},{4,0},{5,1},{8,4},{9,5},{12,8},{13,9},{14,12},{15,13},... | collective-permute-start | bytes 442376 | tf_op jit(solution)/shard_map/ppermute | solution.py:348
  17.3 1.0 %collective-permute-start.12 = (bf16[144,512]{1,0:T(8,128)(2,1)S(1)}, bf16[144,512]{1,0:T(8,128)(2,1)S(1)}, u32[]{:S(2)}, u32[]{:S(2)}) collective-permute-start(bf16[144,512]{1,0:T(8,128)(2,1)S(1)} %collective-permute-done.11.refs_11_), channel_id=1, source_target_pairs={{0,4},{1,5},{4,8},{5,9},{8,12},{9,13},{12,14},{13,15},{14,10},{15,... | collective-permute-start | bytes 442376 | tf_op jit(solution)/shard_map/ppermute | solution.py:346
  18.3 1.4 %collective-permute-done.3.refs_4_ = bf16[128,512]{1,0:T(8,128)(2,1)S(1)} collective-permute-done((bf16[128,512]{1,0:T(8,128)(2,1)S(1)}, bf16[128,512]{1,0:T(8,128)(2,1)S(1)}, u32[]{:S(2)}, u32[]{:S(2)}) %collective-permute-start.3) | collective-permute-done | bytes 131104 | tf_op jit(solution)/shard_map/ppermute | solution.py:345
  19.7 0.8 %collective-permute-start.4 = (bf16[128,512]{1,0:T(8,128)(2,1)S(1)}, bf16[128,512]{1,0:T(8,128)(2,1)S(1)}, u32[]{:S(2)}, u32[]{:S(2)}) collective-permute-start(bf16[128,512]{1,0:T(8,128)(2,1)S(1)} %collective-permute-done.3.refs_4_), channel_id=1, source_target_pairs={{0,4},{1,5},{4,8},{5,9},{8,12},{9,13},{12,14},{13,15},{14,10},{15,... | collective-permute-start | bytes 393224 | tf_op jit(solution)/shard_map/ppermute | solution.py:345
  20.6 0.6 %collective-permute-start.7 = (bf16[128,512]{1,0:T(8,128)(2,1)S(1)}, bf16[128,512]{1,0:T(8,128)(2,1)S(1)}, u32[]{:S(2)}, u32[]{:S(2)}) collective-permute-start(bf16[128,512]{1,0:T(8,128)(2,1)S(1)} %collective-permute-done.6.refs_7_), channel_id=1, source_target_pairs={{0,2},{1,3},{4,0},{5,1},{8,4},{9,5},{12,8},{13,9},{14,12},{15,13},... | collective-permute-start | bytes 393224 | tf_op jit(solution)/shard_map/ppermute | solution.py:347
  21.2 0.7 %collective-permute-done.15.refs_15_ = bf16[144,512]{1,0:T(8,128)(2,1)S(1)} collective-permute-done((bf16[144,512]{1,0:T(8,128)(2,1)S(1)}, bf16[144,512]{1,0:T(8,128)(2,1)S(1)}, u32[]{:S(2)}, u32[]{:S(2)}) %collective-permute-start.15) | collective-permute-done | bytes 147488 | tf_op jit(solution)/shard_map/ppermute | solution.py:348
  21.9 0.7 %collective-permute-start.17 = (bf16[128,512]{1,0:T(8,128)(2,1)S(1)}, bf16[128,512]{1,0:T(8,128)(2,1)S(1)}, u32[]{:S(2)}, u32[]{:S(2)}) collective-permute-start(bf16[128,512]{1,0:T(8,128)(2,1)S(1)} %slice.28), channel_id=1, source_target_pairs={{0,2},{1,3},{4,0},{5,1},{8,4},{9,5},{12,8},{13,9},{14,12},{15,13},... | collective-permute-start | bytes 393224 | tf_op jit(solution)/shard_map/ppermute | solution.py:351
  22.5 2.7 %collective-permute-done.4.refs_5_ = bf16[128,512]{1,0:T(8,128)(2,1)S(1)} collective-permute-done((bf16[128,512]{1,0:T(8,128)(2,1)S(1)}, bf16[128,512]{1,0:T(8,128)(2,1)S(1)}, u32[]{:S(2)}, u32[]{:S(2)}) %collective-permute-start.4) | collective-permute-done | bytes 131104 | tf_op jit(solution)/shard_map/ppermute | solution.py:345
  25.3 0.4 %collective-permute-start.16 = (bf16[128,512]{1,0:T(8,128)(2,1)S(1)}, bf16[128,512]{1,0:T(8,128)(2,1)S(1)}, u32[]{:S(2)}, u32[]{:S(2)}) collective-permute-start(bf16[128,512]{1,0:T(8,128)(2,1)S(1)} %collective-permute-done.4.refs_5_), channel_id=1, source_target_pairs={{0,4},{1,5},{4,8},{5,9},{8,12},{9,13},{12,14},{13,15},{14,10},{15,... | collective-permute-start | bytes 393224 | tf_op jit(solution)/shard_map/ppermute | solution.py:350
  25.7 5.8 %near.1 = (bf16[4,512,256]{2,1,0:T(8,128)(2,1)S(1)}, f32[4,512,256]{2,1,0:T(8,128)S(1)}, f32[4,512,128]{2,1,0:T(8,128)S(1)}, bf16[4,512,256]{2,1,0:T(8,128)(2,1)...) custom-call(bf16[64,8192]{1,0:T(8,128)(2,1)S(1)} %copy-done, ...), custom_call_target="tpu_custom_call" | custom-call | flops 3758096384 | bytes 8388608 | tf_op jit(solution)/shard_map/near/pallas_call | solution.py:357
  31.5 1.2 %far_other.1 = bf16[64,4096]{1,0:T(8,128)(2,1)S(1)} custom-call(bf16[4,512,256]{2,1,0:T(8,128)(2,1)S(1)} %get-tuple-element.18.q_aug, f32[4,512,256]{2,1,0:T(8,128)S(1)} %get-tuple-element.19.total, f32[4,512,128]{2,1,0:T(8,128)S(1)} %get-tuple-element.20.top, bf16[128,512]{1,0:T(8,128)(2,1)S(1)} %collective-permute-done.16.k_far, ...), custom_call_target="tpu_custom_call" | custom-call | flops 268435456 | bytes 8388608 | tf_op jit(solution)/shard_map/far_other/pallas_call | solution.py:380
  32.7 3.3 %collective-permute-start.18 = (bf16[64,4096]{1,0:T(8,128)(2,1)S(1)}, bf16[64,4096]{1,0:T(8,128)(2,1)S(1)}, u32[]{:S(2)}, u32[]{:S(2)}) collective-permute-start(bf16[64,4096]{1,0:T(8,128)(2,1)S(1)} %far_other.1), channel_id=1, source_target_pairs={{0,1},{1,0},{2,3},{3,2},{4,5},{5,4},{6,7},{7,6},{8,9},{9,8},{10,11... | collective-permute-start | bytes 1572872 | tf_op jit(solution)/shard_map/ppermute | solution.py:398
  36.1 1.9 %far_own.1.half_done = bf16[64,8192]{1,0:T(8,128)(2,1)} custom-call(bf16[4,512,256]{2,1,0:T(8,128)(2,1)S(1)} %get-tuple-element.15.q_aug, f32[4,512,256]{2,1,0:T(8,128)S(1)} %get-tuple-element.16.total, f32[4,512,128]{2,1,0:T(8,128)S(1)} %get-tuple-element.17.top, bf16[128,512]{1,0:T(8,128)(2,1)S(1)} %collective-permute-done.16.k_far, ...), custom_call_target="tpu_custom_call" | custom-call | flops 268435456 | bytes 8388608 | tf_op jit(solution)/shard_map/far_own/pallas_call | solution.py:380
  37.9 0.8 %join.1 = bf16[64,8192]{1,0:T(8,128)(2,1)} custom-call(bf16[64,8192]{1,0:T(8,128)(2,1)} %far_own.1.half_done, bf16[64,4096]{1,0:T(8,128)(2,1)S(1)} %collective-permute-done.18.got), custom_call_target="tpu_custom_call", output_to_operand_aliasing={{}: (0, {})} | custom-call | tf_op jit(solution)/shard_map/join/pallas_call | solution.py:399
  (25 shorter events, 0.2 us)
Async XLA Ops:
  0.0 25.7 %copy-start = (bf16[64,8192]{1,0:T(8,128)(2,1)S(1)}, bf16[64,8192]{1,0:T(8,128)(2,1)}, u32[]{:S(2)}) copy-start(bf16[64,8192]{1,0:T(8,128)(2,1)} %refs_0_.1) | copy-start | bytes 3145732
  0.0 7.2 %collective-permute-start = (bf16[64,1024]{1,0:T(8,128)(2,1)}, bf16[64,1024]{1,0:T(8,128)(2,1)S(1)}, u32[]{:S(2)}, u32[]{:S(2)}) collective-permute-start(bf16[64,1024]{1,0:T(8,128)(2,1)} %param.6), channel_id=1, source_target_pairs={{0,1},{1,0},{2,3},{3,2},{4,5},{5,4},{6,7},{7,6},{8,9},{9,8},{10,11... | collective-permute-start | bytes 393224 | tf_op jit(solution)/shard_map/ppermute | solution.py:328
  1.2 6.0 %collective-permute-start.1 = (bf16[64,4096]{1,0:T(8,128)(2,1)S(1)}, bf16[64,4096]{1,0:T(8,128)(2,1)S(1)}, u32[]{:S(2)}, u32[]{:S(2)}) collective-permute-start(bf16[64,4096]{1,0:T(8,128)(2,1)S(1)} %constant_dynamic-slice_fusion.2), channel_id=1, source_target_pairs={{0,1},{1,0},{2,3},{3,2},{4,5},{5,4},{6,7},{7,6},{8,9},{9,8},{10,11... | collective-permute-start | bytes 1572872 | tf_op jit(solution)/shard_map/ppermute | solution.py:341
  1.7 3.0 %collective-permute-start.8 = (bf16[64,1024]{1,0:T(8,128)(2,1)}, bf16[64,1024]{1,0:T(8,128)(2,1)S(1)}, u32[]{:S(2)}, u32[]{:S(2)}) collective-permute-start(bf16[64,1024]{1,0:T(8,128)(2,1)} %param.7), channel_id=1, source_target_pairs={{0,1},{1,0},{2,3},{3,2},{4,5},{5,4},{6,7},{7,6},{8,9},{9,8},{10,11... | collective-permute-start | bytes 393224 | tf_op jit(solution)/shard_map/ppermute | solution.py:329
  2.5 2.1 %collective-permute-start.9 = (s32[16,2,16]{2,0,1:T(8,128)S(1)}, s32[16,2,16]{2,0,1:T(8,128)S(1)}, u32[]{:S(2)}, u32[]{:S(2)}) collective-permute-start(s32[16,2,16]{2,0,1:T(8,128)S(1)} %get-tuple-element.22), channel_id=1, source_target_pairs={{0,1},{1,0},{2,3},{3,2},{4,5},{5,4},{6,7},{7,6},{8,9},{9,8},{10,11... | collective-permute-start | bytes 6152 | tf_op jit(solution)/shard_map/ppermute | solution.py:330
  4.7 6.3 %collective-permute-start.13 = (bf16[144,512]{1,0:T(8,128)(2,1)S(1)}, bf16[144,512]{1,0:T(8,128)(2,1)S(1)}, u32[]{:S(2)}, u32[]{:S(2)}) collective-permute-start(bf16[144,512]{1,0:T(8,128)(2,1)S(1)} %pad_maximum_fusion.refs_9_), channel_id=1, source_target_pairs={{0,2},{1,3},{4,0},{5,1},{8,4},{9,5},{12,8},{13,9},{14,12},{15,13},... | collective-permute-start | bytes 442376 | tf_op jit(solution)/shard_map/ppermute | solution.py:348
  7.1 5.0 %collective-permute-start.10 = (bf16[144,512]{1,0:T(8,128)(2,1)S(1)}, bf16[144,512]{1,0:T(8,128)(2,1)S(1)}, u32[]{:S(2)}, u32[]{:S(2)}) collective-permute-start(bf16[144,512]{1,0:T(8,128)(2,1)S(1)} %pad_maximum_fusion.refs_9_), channel_id=1, source_target_pairs={{0,4},{1,5},{4,8},{5,9},{8,12},{9,13},{12,14},{13,15},{14,10},{15,... | collective-permute-start | bytes 442376 | tf_op jit(solution)/shard_map/ppermute | solution.py:346
  7.3 7.3 %collective-permute-start.2 = (bf16[128,512]{1,0:T(8,128)(2,1)S(1)}, bf16[128,512]{1,0:T(8,128)(2,1)S(1)}, u32[]{:S(2)}, u32[]{:S(2)}) collective-permute-start(bf16[128,512]{1,0:T(8,128)(2,1)S(1)} %pad_maximum_fusion.1.refs_2_), channel_id=1, source_target_pairs={{0,4},{1,5},{4,8},{5,9},{8,12},{9,13},{12,14},{13,15},{14,10},{15,... | collective-permute-start | bytes 393224 | tf_op jit(solution)/shard_map/ppermute | solution.py:345
  8.7 6.3 %collective-permute-start.5 = (bf16[128,512]{1,0:T(8,128)(2,1)S(1)}, bf16[128,512]{1,0:T(8,128)(2,1)S(1)}, u32[]{:S(2)}, u32[]{:S(2)}) collective-permute-start(bf16[128,512]{1,0:T(8,128)(2,1)S(1)} %pad_maximum_fusion.1.refs_2_), channel_id=1, source_target_pairs={{0,2},{1,3},{4,0},{5,1},{8,4},{9,5},{12,8},{13,9},{14,12},{15,13},... | collective-permute-start | bytes 393224 | tf_op jit(solution)/shard_map/ppermute | solution.py:347
  11.0 5.8 %collective-permute-start.14 = (bf16[144,512]{1,0:T(8,128)(2,1)S(1)}, bf16[144,512]{1,0:T(8,128)(2,1)S(1)}, u32[]{:S(2)}, u32[]{:S(2)}) collective-permute-start(bf16[144,512]{1,0:T(8,128)(2,1)S(1)} %collective-permute-done.13.refs_13_), channel_id=1, source_target_pairs={{0,2},{1,3},{4,0},{5,1},{8,4},{9,5},{12,8},{13,9},{14,12},{15,13},... | collective-permute-start | bytes 442376 | tf_op jit(solution)/shard_map/ppermute | solution.py:348
  12.1 5.3 %collective-permute-start.11 = (bf16[144,512]{1,0:T(8,128)(2,1)S(1)}, bf16[144,512]{1,0:T(8,128)(2,1)S(1)}, u32[]{:S(2)}, u32[]{:S(2)}) collective-permute-start(bf16[144,512]{1,0:T(8,128)(2,1)S(1)} %collective-permute-done.10.refs_10_), channel_id=1, source_target_pairs={{0,4},{1,5},{4,8},{5,9},{8,12},{9,13},{12,14},{13,15},{14,10},{15,... | collective-permute-start | bytes 442376 | tf_op jit(solution)/shard_map/ppermute | solution.py:346
  14.6 5.2 %collective-permute-start.3 = (bf16[128,512]{1,0:T(8,128)(2,1)S(1)}, bf16[128,512]{1,0:T(8,128)(2,1)S(1)}, u32[]{:S(2)}, u32[]{:S(2)}) collective-permute-start(bf16[128,512]{1,0:T(8,128)(2,1)S(1)} %collective-permute-done.2.refs_3_), channel_id=1, source_target_pairs={{0,4},{1,5},{4,8},{5,9},{8,12},{9,13},{12,14},{13,15},{14,10},{15,... | collective-permute-start | bytes 393224 | tf_op jit(solution)/shard_map/ppermute | solution.py:345
  15.0 5.5 %collective-permute-start.6 = (bf16[128,512]{1,0:T(8,128)(2,1)S(1)}, bf16[128,512]{1,0:T(8,128)(2,1)S(1)}, u32[]{:S(2)}, u32[]{:S(2)}) collective-permute-start(bf16[128,512]{1,0:T(8,128)(2,1)S(1)} %collective-permute-done.5.refs_6_), channel_id=1, source_target_pairs={{0,2},{1,3},{4,0},{5,1},{8,4},{9,5},{12,8},{13,9},{14,12},{15,13},... | collective-permute-start | bytes 393224 | tf_op jit(solution)/shard_map/ppermute | solution.py:347
  16.8 5.0 %collective-permute-start.15 = (bf16[144,512]{1,0:T(8,128)(2,1)S(1)}, bf16[144,512]{1,0:T(8,128)(2,1)S(1)}, u32[]{:S(2)}, u32[]{:S(2)}) collective-permute-start(bf16[144,512]{1,0:T(8,128)(2,1)S(1)} %collective-permute-done.14.refs_14_), channel_id=1, source_target_pairs={{0,2},{1,3},{4,0},{5,1},{8,4},{9,5},{12,8},{13,9},{14,12},{15,13},... | collective-permute-start | bytes 442376 | tf_op jit(solution)/shard_map/ppermute | solution.py:348
  17.3 8.4 %collective-permute-start.12 = (bf16[144,512]{1,0:T(8,128)(2,1)S(1)}, bf16[144,512]{1,0:T(8,128)(2,1)S(1)}, u32[]{:S(2)}, u32[]{:S(2)}) collective-permute-start(bf16[144,512]{1,0:T(8,128)(2,1)S(1)} %collective-permute-done.11.refs_11_), channel_id=1, source_target_pairs={{0,4},{1,5},{4,8},{5,9},{8,12},{9,13},{12,14},{13,15},{14,10},{15,... | collective-permute-start | bytes 442376 | tf_op jit(solution)/shard_map/ppermute | solution.py:346
  19.7 5.5 %collective-permute-start.4 = (bf16[128,512]{1,0:T(8,128)(2,1)S(1)}, bf16[128,512]{1,0:T(8,128)(2,1)S(1)}, u32[]{:S(2)}, u32[]{:S(2)}) collective-permute-start(bf16[128,512]{1,0:T(8,128)(2,1)S(1)} %collective-permute-done.3.refs_4_), channel_id=1, source_target_pairs={{0,4},{1,5},{4,8},{5,9},{8,12},{9,13},{12,14},{13,15},{14,10},{15,... | collective-permute-start | bytes 393224 | tf_op jit(solution)/shard_map/ppermute | solution.py:345
  20.6 5.2 %collective-permute-start.7 = (bf16[128,512]{1,0:T(8,128)(2,1)S(1)}, bf16[128,512]{1,0:T(8,128)(2,1)S(1)}, u32[]{:S(2)}, u32[]{:S(2)}) collective-permute-start(bf16[128,512]{1,0:T(8,128)(2,1)S(1)} %collective-permute-done.6.refs_7_), channel_id=1, source_target_pairs={{0,2},{1,3},{4,0},{5,1},{8,4},{9,5},{12,8},{13,9},{14,12},{15,13},... | collective-permute-start | bytes 393224 | tf_op jit(solution)/shard_map/ppermute | solution.py:347
  21.9 9.6 %collective-permute-start.17 = (bf16[128,512]{1,0:T(8,128)(2,1)S(1)}, bf16[128,512]{1,0:T(8,128)(2,1)S(1)}, u32[]{:S(2)}, u32[]{:S(2)}) collective-permute-start(bf16[128,512]{1,0:T(8,128)(2,1)S(1)} %slice.28), channel_id=1, source_target_pairs={{0,2},{1,3},{4,0},{5,1},{8,4},{9,5},{12,8},{13,9},{14,12},{15,13},... | collective-permute-start | bytes 393224 | tf_op jit(solution)/shard_map/ppermute | solution.py:351
  25.3 6.3 %collective-permute-start.16 = (bf16[128,512]{1,0:T(8,128)(2,1)S(1)}, bf16[128,512]{1,0:T(8,128)(2,1)S(1)}, u32[]{:S(2)}, u32[]{:S(2)}) collective-permute-start(bf16[128,512]{1,0:T(8,128)(2,1)S(1)} %collective-permute-done.4.refs_5_), channel_id=1, source_target_pairs={{0,4},{1,5},{4,8},{5,9},{8,12},{9,13},{12,14},{13,15},{14,10},{15,... | collective-permute-start | bytes 393224 | tf_op jit(solution)/shard_map/ppermute | solution.py:350
  32.7 5.2 %collective-permute-start.18 = (bf16[64,4096]{1,0:T(8,128)(2,1)S(1)}, bf16[64,4096]{1,0:T(8,128)(2,1)S(1)}, u32[]{:S(2)}, u32[]{:S(2)}) collective-permute-start(bf16[64,4096]{1,0:T(8,128)(2,1)S(1)} %far_other.1), channel_id=1, source_target_pairs={{0,1},{1,0},{2,3},{3,2},{4,5},{5,4},{6,7},{7,6},{8,9},{9,8},{10,11... | collective-permute-start | bytes 1572872 | tf_op jit(solution)/shard_map/ppermute | solution.py:398

commit v6 on v4

--- a/solution.py
+++ b/solution.py
@@ -334,8 +334,8 @@
     k_ahead, k_back, v_ahead, v_back = [k_unit], [k_unit], [v_unit], [v_unit]
     for _ in range(z_size - 1):
         k_ahead.append(lax.ppermute(k_ahead[-1], axes, ahead))
+        v_ahead.append(lax.ppermute(v_ahead[-1], axes, ahead))
         k_back.append(lax.ppermute(k_back[-1], axes, back))
-        v_ahead.append(lax.ppermute(v_ahead[-1], axes, ahead))
         v_back.append(lax.ppermute(v_back[-1], axes, back))
     unit_rows = 2 * rows
     k_far = lax.ppermute(k_ahead[-1], axes, ahead)

time: 39 us -> 39 us (level)
  no operation moved by 1% of the time
where the time goes in v6:
time: 39 us; the launch traced here: 38.8 us
  starting transfers between devices  15.4 us (39%)
  waiting for transfers between devices  9.95 us (26%)
  Pallas kernels  8.82 us (23%)
  local copies, waits for them, and re-layouts  3.7 us (9%)
  other arithmetic  0.83 us (2%)
    ppermute x3, waiting for transfers between devices, per_device_ring(): k_ahead.append(lax.ppermute(k_ahead[-1], axes, ahead))  6.2 us
    pallas_call x1, Pallas kernels, per_device_ring(): pl.pallas_call(functools.partial(near_kernel, z_size, heads), out_shape=(...  5.79 us
    ppermute x3, starting transfers between devices, per_device_ring(): v_back.append(lax.ppermute(v_back[-1], axes, back))  3.92 us
    ppermute x3, waiting for transfers between devices, per_device_ring(): v_back.append(lax.ppermute(v_back[-1], axes, back))  3.71 us
    ppermute x1, starting transfers between devices, per_device_ring(): back_home = lax.ppermute(finish(1, False), 'core', swap)  3.35 us
    pallas_call x2, Pallas kernels, finish(): pl.pallas_call(functools.partial(far_kernel, z_size, whole), out_shape=ja...  3.03 us
    ppermute x3, starting transfers between devices, per_device_ring(): k_ahead.append(lax.ppermute(k_ahead[-1], axes, ahead))  2.77 us
    dynamic_slice x2, local copies, waits for them, and re-layouts, halves(): lax.dynamic_slice_in_dim(part, own, half, 1)  1.69 us
  transfers between devices with their start and end apart: 19, of which 6 were waited for; matrix products, arithmetic and copies ran while one was open for 10% of the time, Pallas kernels for 20%

profile of v6, /device:TPU:1, one launch (start us, length us, event | category | flops | bytes accessed | tf_op | source)
XLA Modules:
  0.0 38.8 jit_solution(1453751045878668834)
XLA Ops:
  0.1 1.2 %constant_dynamic-slice_fusion.2 = bf16[64,4096]{1,0:T(8,128)(2,1)S(1)} fusion(bf16[64,8192]{1,0:T(8,128)(2,1)} %refs_0_.1, s32[]{:T(128)S(6)} %select_n.5), kind=kLoop, calls=%fused_computation.17 | loop fusion | bytes 1048580 | tf_op jit(solution)/shard_map/dynamic_slice | solution.py:331
  1.2 0.4 %collective-permute-start.1 = (bf16[64,4096]{1,0:T(8,128)(2,1)S(1)}, bf16[64,4096]{1,0:T(8,128)(2,1)S(1)}, u32[]{:S(2)}, u32[]{:S(2)}) collective-permute-start(bf16[64,4096]{1,0:T(8,128)(2,1)S(1)} %constant_dynamic-slice_fusion.2), channel_id=1, source_target_pairs={{0,1},{1,0},{2,3},{3,2},{4,5},{5,4},{6,7},{7,6},{8,9},{9,8},{10,11... | collective-permute-start | bytes 1572872 | tf_op jit(solution)/shard_map/ppermute | solution.py:332
  1.7 0.1 collective-permute-start.8
  1.8 0.7 %copy_convert_fusion = (bf16[16,2,16]{2,0,1:T(8,128)(2,1)S(1)}, s32[16,2,16]{2,0,1:T(8,128)S(1)}) fusion(s32[16,2,16]{2,1,0:T(2,128)} %param.8), kind=kLoop, calls=%fused_computation.20 | loop fusion | flops 512 | bytes 5120 | tf_op jit(solution)/shard_map/convert.11
  2.5 0.4 collective-permute-start.9
  2.9 0.8 %constant_dynamic-slice_fusion.4 = bf16[64,512]{1,0:T(8,128)(2,1)S(1)} fusion(bf16[64,1024]{1,0:T(8,128)(2,1)} %param.6, s32[]{:T(128)S(6)} %select_n.4), kind=kLoop, calls=%fused_computation.19 | loop fusion | bytes 131076 | tf_op jit(solution)/shard_map/dynamic_slice | solution.py:326
  3.7 0.8 %constant_dynamic-slice_fusion.1 = bf16[64,512]{1,0:T(8,128)(2,1)S(1)} fusion(bf16[64,1024]{1,0:T(8,128)(2,1)} %param.7, s32[]{:T(128)S(6)} %select_n.4), kind=kLoop, calls=%fused_computation.16 | loop fusion | bytes 131076 | tf_op jit(solution)/shard_map/dynamic_slice | solution.py:326
  4.6 0.1 fusion.6
  4.7 2.3 %collective-permute-start.13 = (bf16[144,512]{1,0:T(8,128)(2,1)S(1)}, bf16[144,512]{1,0:T(8,128)(2,1)S(1)}, u32[]{:S(2)}, u32[]{:S(2)}) collective-permute-start(bf16[144,512]{1,0:T(8,128)(2,1)S(1)} %pad_maximum_fusion.refs_9_), channel_id=1, source_target_pairs={{0,2},{1,3},{4,0},{5,1},{8,4},{9,5},{12,8},{13,9},{14,12},{15,13},... | collective-permute-start | bytes 442376 | tf_op jit(solution)/shard_map/ppermute | solution.py:339
  7.1 0.2 collective-permute-start.10
  7.3 1.5 %collective-permute-start.2 = (bf16[128,512]{1,0:T(8,128)(2,1)S(1)}, bf16[128,512]{1,0:T(8,128)(2,1)S(1)}, u32[]{:S(2)}, u32[]{:S(2)}) collective-permute-start(bf16[128,512]{1,0:T(8,128)(2,1)S(1)} %pad_maximum_fusion.1.refs_2_), channel_id=1, source_target_pairs={{0,4},{1,5},{4,8},{5,9},{8,12},{9,13},{12,14},{13,15},{14,10},{15,... | collective-permute-start | bytes 393224 | tf_op jit(solution)/shard_map/ppermute | solution.py:336
  8.8 2.2 %collective-permute-done.13.refs_13_ = bf16[144,512]{1,0:T(8,128)(2,1)S(1)} collective-permute-done((bf16[144,512]{1,0:T(8,128)(2,1)S(1)}, bf16[144,512]{1,0:T(8,128)(2,1)S(1)}, u32[]{:S(2)}, u32[]{:S(2)}) %collective-permute-start.13) | collective-permute-done | bytes 147488 | tf_op jit(solution)/shard_map/ppermute | solution.py:339
  11.0 1.1 %collective-permute-start.14 = (bf16[144,512]{1,0:T(8,128)(2,1)S(1)}, bf16[144,512]{1,0:T(8,128)(2,1)S(1)}, u32[]{:S(2)}, u32[]{:S(2)}) collective-permute-start(bf16[144,512]{1,0:T(8,128)(2,1)S(1)} %collective-permute-done.13.refs_13_), channel_id=1, source_target_pairs={{0,2},{1,3},{4,0},{5,1},{8,4},{9,5},{12,8},{13,9},{14,12},{15,13},... | collective-permute-start | bytes 442376 | tf_op jit(solution)/shard_map/ppermute | solution.py:339
  12.1 0.4 %collective-permute-start.11 = (bf16[144,512]{1,0:T(8,128)(2,1)S(1)}, bf16[144,512]{1,0:T(8,128)(2,1)S(1)}, u32[]{:S(2)}, u32[]{:S(2)}) collective-permute-start(bf16[144,512]{1,0:T(8,128)(2,1)S(1)} %collective-permute-done.10.refs_10_), channel_id=1, source_target_pairs={{0,4},{1,5},{4,8},{5,9},{8,12},{9,13},{12,14},{13,15},{14,10},{15,... | collective-permute-start | bytes 442376 | tf_op jit(solution)/shard_map/ppermute | solution.py:337
  12.5 2.1 %collective-permute-done.2.refs_3_ = bf16[128,512]{1,0:T(8,128)(2,1)S(1)} collective-permute-done((bf16[128,512]{1,0:T(8,128)(2,1)S(1)}, bf16[128,512]{1,0:T(8,128)(2,1)S(1)}, u32[]{:S(2)}, u32[]{:S(2)}) %collective-permute-start.2) | collective-permute-done | bytes 131104 | tf_op jit(solution)/shard_map/ppermute | solution.py:336
  14.6 0.5 %collective-permute-start.3 = (bf16[128,512]{1,0:T(8,128)(2,1)S(1)}, bf16[128,512]{1,0:T(8,128)(2,1)S(1)}, u32[]{:S(2)}, u32[]{:S(2)}) collective-permute-start(bf16[128,512]{1,0:T(8,128)(2,1)S(1)} %collective-permute-done.2.refs_3_), channel_id=1, source_target_pairs={{0,4},{1,5},{4,8},{5,9},{8,12},{9,13},{12,14},{13,15},{14,10},{15,... | collective-permute-start | bytes 393224 | tf_op jit(solution)/shard_map/ppermute | solution.py:336
  15.0 1.0 %collective-permute-start.6 = (bf16[128,512]{1,0:T(8,128)(2,1)S(1)}, bf16[128,512]{1,0:T(8,128)(2,1)S(1)}, u32[]{:S(2)}, u32[]{:S(2)}) collective-permute-start(bf16[128,512]{1,0:T(8,128)(2,1)S(1)} %collective-permute-done.5.refs_6_), channel_id=1, source_target_pairs={{0,2},{1,3},{4,0},{5,1},{8,4},{9,5},{12,8},{13,9},{14,12},{15,13},... | collective-permute-start | bytes 393224 | tf_op jit(solution)/shard_map/ppermute | solution.py:338
  16.0 0.8 %collective-permute-done.14.refs_14_ = bf16[144,512]{1,0:T(8,128)(2,1)S(1)} collective-permute-done((bf16[144,512]{1,0:T(8,128)(2,1)S(1)}, bf16[144,512]{1,0:T(8,128)(2,1)S(1)}, u32[]{:S(2)}, u32[]{:S(2)}) %collective-permute-start.14) | collective-permute-done | bytes 147488 | tf_op jit(solution)/shard_map/ppermute | solution.py:339
  16.8 0.5 %collective-permute-start.15 = (bf16[144,512]{1,0:T(8,128)(2,1)S(1)}, bf16[144,512]{1,0:T(8,128)(2,1)S(1)}, u32[]{:S(2)}, u32[]{:S(2)}) collective-permute-start(bf16[144,512]{1,0:T(8,128)(2,1)S(1)} %collective-permute-done.14.refs_14_), channel_id=1, source_target_pairs={{0,2},{1,3},{4,0},{5,1},{8,4},{9,5},{12,8},{13,9},{14,12},{15,13},... | collective-permute-start | bytes 442376 | tf_op jit(solution)/shard_map/ppermute | solution.py:339
  17.3 1.0 %collective-permute-start.12 = (bf16[144,512]{1,0:T(8,128)(2,1)S(1)}, bf16[144,512]{1,0:T(8,128)(2,1)S(1)}, u32[]{:S(2)}, u32[]{:S(2)}) collective-permute-start(bf16[144,512]{1,0:T(8,128)(2,1)S(1)} %collective-permute-done.11.refs_11_), channel_id=1, source_target_pairs={{0,4},{1,5},{4,8},{5,9},{8,12},{9,13},{12,14},{13,15},{14,10},{15,... | collective-permute-start | bytes 442376 | tf_op jit(solution)/shard_map/ppermute | solution.py:337
  18.3 1.4 %collective-permute-done.3.refs_4_ = bf16[128,512]{1,0:T(8,128)(2,1)S(1)} collective-permute-done((bf16[128,512]{1,0:T(8,128)(2,1)S(1)}, bf16[128,512]{1,0:T(8,128)(2,1)S(1)}, u32[]{:S(2)}, u32[]{:S(2)}) %collective-permute-start.3) | collective-permute-done | bytes 131104 | tf_op jit(solution)/shard_map/ppermute | solution.py:336
  19.7 0.8 %collective-permute-start.4 = (bf16[128,512]{1,0:T(8,128)(2,1)S(1)}, bf16[128,512]{1,0:T(8,128)(2,1)S(1)}, u32[]{:S(2)}, u32[]{:S(2)}) collective-permute-start(bf16[128,512]{1,0:T(8,128)(2,1)S(1)} %collective-permute-done.3.refs_4_), channel_id=1, source_target_pairs={{0,4},{1,5},{4,8},{5,9},{8,12},{9,13},{12,14},{13,15},{14,10},{15,... | collective-permute-start | bytes 393224 | tf_op jit(solution)/shard_map/ppermute | solution.py:336
  20.6 0.6 %collective-permute-start.7 = (bf16[128,512]{1,0:T(8,128)(2,1)S(1)}, bf16[128,512]{1,0:T(8,128)(2,1)S(1)}, u32[]{:S(2)}, u32[]{:S(2)}) collective-permute-start(bf16[128,512]{1,0:T(8,128)(2,1)S(1)} %collective-permute-done.6.refs_7_), channel_id=1, source_target_pairs={{0,2},{1,3},{4,0},{5,1},{8,4},{9,5},{12,8},{13,9},{14,12},{15,13},... | collective-permute-start | bytes 393224 | tf_op jit(solution)/shard_map/ppermute | solution.py:338
  21.2 0.7 %collective-permute-done.15.refs_15_ = bf16[144,512]{1,0:T(8,128)(2,1)S(1)} collective-permute-done((bf16[144,512]{1,0:T(8,128)(2,1)S(1)}, bf16[144,512]{1,0:T(8,128)(2,1)S(1)}, u32[]{:S(2)}, u32[]{:S(2)}) %collective-permute-start.15) | collective-permute-done | bytes 147488 | tf_op jit(solution)/shard_map/ppermute | solution.py:339
  21.9 0.7 %collective-permute-start.17 = (bf16[128,512]{1,0:T(8,128)(2,1)S(1)}, bf16[128,512]{1,0:T(8,128)(2,1)S(1)}, u32[]{:S(2)}, u32[]{:S(2)}) collective-permute-start(bf16[128,512]{1,0:T(8,128)(2,1)S(1)} %slice.28), channel_id=1, source_target_pairs={{0,2},{1,3},{4,0},{5,1},{8,4},{9,5},{12,8},{13,9},{14,12},{15,13},... | collective-permute-start | bytes 393224 | tf_op jit(solution)/shard_map/ppermute | solution.py:342
  22.5 2.7 %collective-permute-done.4.refs_5_ = bf16[128,512]{1,0:T(8,128)(2,1)S(1)} collective-permute-done((bf16[128,512]{1,0:T(8,128)(2,1)S(1)}, bf16[128,512]{1,0:T(8,128)(2,1)S(1)}, u32[]{:S(2)}, u32[]{:S(2)}) %collective-permute-start.4) | collective-permute-done | bytes 131104 | tf_op jit(solution)/shard_map/ppermute | solution.py:336
  25.3 0.4 %collective-permute-start.16 = (bf16[128,512]{1,0:T(8,128)(2,1)S(1)}, bf16[128,512]{1,0:T(8,128)(2,1)S(1)}, u32[]{:S(2)}, u32[]{:S(2)}) collective-permute-start(bf16[128,512]{1,0:T(8,128)(2,1)S(1)} %collective-permute-done.4.refs_5_), channel_id=1, source_target_pairs={{0,4},{1,5},{4,8},{5,9},{8,12},{9,13},{12,14},{13,15},{14,10},{15,... | collective-permute-start | bytes 393224 | tf_op jit(solution)/shard_map/ppermute | solution.py:341
  25.7 5.8 %near.1 = (bf16[4,512,256]{2,1,0:T(8,128)(2,1)S(1)}, f32[4,512,256]{2,1,0:T(8,128)S(1)}, f32[4,512,128]{2,1,0:T(8,128)S(1)}, bf16[4,512,256]{2,1,0:T(8,128)(2,1)...) custom-call(bf16[64,8192]{1,0:T(8,128)(2,1)S(1)} %copy-done, ...), custom_call_target="tpu_custom_call" | custom-call | flops 3758096384 | bytes 8388608 | tf_op jit(solution)/shard_map/near/pallas_call | solution.py:348
  31.5 1.2 %far_other.1 = bf16[64,4096]{1,0:T(8,128)(2,1)S(1)} custom-call(bf16[4,512,256]{2,1,0:T(8,128)(2,1)S(1)} %get-tuple-element.18.q_aug, f32[4,512,256]{2,1,0:T(8,128)S(1)} %get-tuple-element.19.total, f32[4,512,128]{2,1,0:T(8,128)S(1)} %get-tuple-element.20.top, bf16[128,512]{1,0:T(8,128)(2,1)S(1)} %collective-permute-done.16.k_far, ...), custom_call_target="tpu_custom_call" | custom-call | flops 268435456 | bytes 8388608 | tf_op jit(solution)/shard_map/far_other/pallas_call | solution.py:371
  32.7 3.3 %collective-permute-start.18 = (bf16[64,4096]{1,0:T(8,128)(2,1)S(1)}, bf16[64,4096]{1,0:T(8,128)(2,1)S(1)}, u32[]{:S(2)}, u32[]{:S(2)}) collective-permute-start(bf16[64,4096]{1,0:T(8,128)(2,1)S(1)} %far_other.1), channel_id=1, source_target_pairs={{0,1},{1,0},{2,3},{3,2},{4,5},{5,4},{6,7},{7,6},{8,9},{9,8},{10,11... | collective-permute-start | bytes 1572872 | tf_op jit(solution)/shard_map/ppermute | solution.py:389
  36.1 1.9 %far_own.1 = bf16[64,8192]{1,0:T(8,128)(2,1)} custom-call(bf16[4,512,256]{2,1,0:T(8,128)(2,1)S(1)} %get-tuple-element.15.q_aug, f32[4,512,256]{2,1,0:T(8,128)S(1)} %get-tuple-element.16.total, f32[4,512,128]{2,1,0:T(8,128)S(1)} %get-tuple-element.17.top, bf16[128,512]{1,0:T(8,128)(2,1)S(1)} %collective-permute-done.16.k_far, ...), custom_call_target="tpu_custom_call" | custom-call | flops 268435456 | bytes 8388608 | tf_op jit(solution)/shard_map/far_own/pallas_call | solution.py:371
  37.9 0.8 %constant_dynamic-update-slice_fusion = bf16[64,8192]{1,0:T(8,128)(2,1)} fusion(bf16[64,8192]{1,0:T(8,128)(2,1)} %far_own.1, bf16[64,4096]{1,0:T(8,128)(2,1)S(1)} %collective-permute-done.18, s32[]{:T(128)S(6)} %select_n.5), kind=kLoop, calls=%fused_computation.14 | loop fusion | bytes 1048580 | tf_op jit(solution)/shard_map/dynamic_update_slice | solution.py:390
  (25 shorter events, 0.2 us)
Async XLA Ops:
  0.0 25.7 %copy-start = (bf16[64,8192]{1,0:T(8,128)(2,1)S(1)}, bf16[64,8192]{1,0:T(8,128)(2,1)}, u32[]{:S(2)}) copy-start(bf16[64,8192]{1,0:T(8,128)(2,1)} %refs_0_.1) | copy-start | bytes 3145732
  0.0 7.2 %collective-permute-start = (bf16[64,1024]{1,0:T(8,128)(2,1)}, bf16[64,1024]{1,0:T(8,128)(2,1)S(1)}, u32[]{:S(2)}, u32[]{:S(2)}) collective-permute-start(bf16[64,1024]{1,0:T(8,128)(2,1)} %param.6), channel_id=1, source_target_pairs={{0,1},{1,0},{2,3},{3,2},{4,5},{5,4},{6,7},{7,6},{8,9},{9,8},{10,11... | collective-permute-start | bytes 393224 | tf_op jit(solution)/shard_map/ppermute | solution.py:319
  1.2 6.0 %collective-permute-start.1 = (bf16[64,4096]{1,0:T(8,128)(2,1)S(1)}, bf16[64,4096]{1,0:T(8,128)(2,1)S(1)}, u32[]{:S(2)}, u32[]{:S(2)}) collective-permute-start(bf16[64,4096]{1,0:T(8,128)(2,1)S(1)} %constant_dynamic-slice_fusion.2), channel_id=1, source_target_pairs={{0,1},{1,0},{2,3},{3,2},{4,5},{5,4},{6,7},{7,6},{8,9},{9,8},{10,11... | collective-permute-start | bytes 1572872 | tf_op jit(solution)/shard_map/ppermute | solution.py:332
  1.7 3.0 %collective-permute-start.8 = (bf16[64,1024]{1,0:T(8,128)(2,1)}, bf16[64,1024]{1,0:T(8,128)(2,1)S(1)}, u32[]{:S(2)}, u32[]{:S(2)}) collective-permute-start(bf16[64,1024]{1,0:T(8,128)(2,1)} %param.7), channel_id=1, source_target_pairs={{0,1},{1,0},{2,3},{3,2},{4,5},{5,4},{6,7},{7,6},{8,9},{9,8},{10,11... | collective-permute-start | bytes 393224 | tf_op jit(solution)/shard_map/ppermute | solution.py:320
  2.5 2.1 %collective-permute-start.9 = (s32[16,2,16]{2,0,1:T(8,128)S(1)}, s32[16,2,16]{2,0,1:T(8,128)S(1)}, u32[]{:S(2)}, u32[]{:S(2)}) collective-permute-start(s32[16,2,16]{2,0,1:T(8,128)S(1)} %get-tuple-element.22), channel_id=1, source_target_pairs={{0,1},{1,0},{2,3},{3,2},{4,5},{5,4},{6,7},{7,6},{8,9},{9,8},{10,11... | collective-permute-start | bytes 6152 | tf_op jit(solution)/shard_map/ppermute | solution.py:321
  4.7 6.3 %collective-permute-start.13 = (bf16[144,512]{1,0:T(8,128)(2,1)S(1)}, bf16[144,512]{1,0:T(8,128)(2,1)S(1)}, u32[]{:S(2)}, u32[]{:S(2)}) collective-permute-start(bf16[144,512]{1,0:T(8,128)(2,1)S(1)} %pad_maximum_fusion.refs_9_), channel_id=1, source_target_pairs={{0,2},{1,3},{4,0},{5,1},{8,4},{9,5},{12,8},{13,9},{14,12},{15,13},... | collective-permute-start | bytes 442376 | tf_op jit(solution)/shard_map/ppermute | solution.py:339
  7.1 5.0 %collective-permute-start.10 = (bf16[144,512]{1,0:T(8,128)(2,1)S(1)}, bf16[144,512]{1,0:T(8,128)(2,1)S(1)}, u32[]{:S(2)}, u32[]{:S(2)}) collective-permute-start(bf16[144,512]{1,0:T(8,128)(2,1)S(1)} %pad_maximum_fusion.refs_9_), channel_id=1, source_target_pairs={{0,4},{1,5},{4,8},{5,9},{8,12},{9,13},{12,14},{13,15},{14,10},{15,... | collective-permute-start | bytes 442376 | tf_op jit(solution)/shard_map/ppermute | solution.py:337
  7.3 7.3 %collective-permute-start.2 = (bf16[128,512]{1,0:T(8,128)(2,1)S(1)}, bf16[128,512]{1,0:T(8,128)(2,1)S(1)}, u32[]{:S(2)}, u32[]{:S(2)}) collective-permute-start(bf16[128,512]{1,0:T(8,128)(2,1)S(1)} %pad_maximum_fusion.1.refs_2_), channel_id=1, source_target_pairs={{0,4},{1,5},{4,8},{5,9},{8,12},{9,13},{12,14},{13,15},{14,10},{15,... | collective-permute-start | bytes 393224 | tf_op jit(solution)/shard_map/ppermute | solution.py:336
  8.7 6.3 %collective-permute-start.5 = (bf16[128,512]{1,0:T(8,128)(2,1)S(1)}, bf16[128,512]{1,0:T(8,128)(2,1)S(1)}, u32[]{:S(2)}, u32[]{:S(2)}) collective-permute-start(bf16[128,512]{1,0:T(8,128)(2,1)S(1)} %pad_maximum_fusion.1.refs_2_), channel_id=1, source_target_pairs={{0,2},{1,3},{4,0},{5,1},{8,4},{9,5},{12,8},{13,9},{14,12},{15,13},... | collective-permute-start | bytes 393224 | tf_op jit(solution)/shard_map/ppermute | solution.py:338
  11.0 5.8 %collective-permute-start.14 = (bf16[144,512]{1,0:T(8,128)(2,1)S(1)}, bf16[144,512]{1,0:T(8,128)(2,1)S(1)}, u32[]{:S(2)}, u32[]{:S(2)}) collective-permute-start(bf16[144,512]{1,0:T(8,128)(2,1)S(1)} %collective-permute-done.13.refs_13_), channel_id=1, source_target_pairs={{0,2},{1,3},{4,0},{5,1},{8,4},{9,5},{12,8},{13,9},{14,12},{15,13},... | collective-permute-start | bytes 442376 | tf_op jit(solution)/shard_map/ppermute | solution.py:339
  12.1 5.3 %collective-permute-start.11 = (bf16[144,512]{1,0:T(8,128)(2,1)S(1)}, bf16[144,512]{1,0:T(8,128)(2,1)S(1)}, u32[]{:S(2)}, u32[]{:S(2)}) collective-permute-start(bf16[144,512]{1,0:T(8,128)(2,1)S(1)} %collective-permute-done.10.refs_10_), channel_id=1, source_target_pairs={{0,4},{1,5},{4,8},{5,9},{8,12},{9,13},{12,14},{13,15},{14,10},{15,... | collective-permute-start | bytes 442376 | tf_op jit(solution)/shard_map/ppermute | solution.py:337
  14.6 5.2 %collective-permute-start.3 = (bf16[128,512]{1,0:T(8,128)(2,1)S(1)}, bf16[128,512]{1,0:T(8,128)(2,1)S(1)}, u32[]{:S(2)}, u32[]{:S(2)}) collective-permute-start(bf16[128,512]{1,0:T(8,128)(2,1)S(1)} %collective-permute-done.2.refs_3_), channel_id=1, source_target_pairs={{0,4},{1,5},{4,8},{5,9},{8,12},{9,13},{12,14},{13,15},{14,10},{15,... | collective-permute-start | bytes 393224 | tf_op jit(solution)/shard_map/ppermute | solution.py:336
  15.0 5.5 %collective-permute-start.6 = (bf16[128,512]{1,0:T(8,128)(2,1)S(1)}, bf16[128,512]{1,0:T(8,128)(2,1)S(1)}, u32[]{:S(2)}, u32[]{:S(2)}) collective-permute-start(bf16[128,512]{1,0:T(8,128)(2,1)S(1)} %collective-permute-done.5.refs_6_), channel_id=1, source_target_pairs={{0,2},{1,3},{4,0},{5,1},{8,4},{9,5},{12,8},{13,9},{14,12},{15,13},... | collective-permute-start | bytes 393224 | tf_op jit(solution)/shard_map/ppermute | solution.py:338
  16.8 5.0 %collective-permute-start.15 = (bf16[144,512]{1,0:T(8,128)(2,1)S(1)}, bf16[144,512]{1,0:T(8,128)(2,1)S(1)}, u32[]{:S(2)}, u32[]{:S(2)}) collective-permute-start(bf16[144,512]{1,0:T(8,128)(2,1)S(1)} %collective-permute-done.14.refs_14_), channel_id=1, source_target_pairs={{0,2},{1,3},{4,0},{5,1},{8,4},{9,5},{12,8},{13,9},{14,12},{15,13},... | collective-permute-start | bytes 442376 | tf_op jit(solution)/shard_map/ppermute | solution.py:339
  17.3 8.4 %collective-permute-start.12 = (bf16[144,512]{1,0:T(8,128)(2,1)S(1)}, bf16[144,512]{1,0:T(8,128)(2,1)S(1)}, u32[]{:S(2)}, u32[]{:S(2)}) collective-permute-start(bf16[144,512]{1,0:T(8,128)(2,1)S(1)} %collective-permute-done.11.refs_11_), channel_id=1, source_target_pairs={{0,4},{1,5},{4,8},{5,9},{8,12},{9,13},{12,14},{13,15},{14,10},{15,... | collective-permute-start | bytes 442376 | tf_op jit(solution)/shard_map/ppermute | solution.py:337
  19.7 5.5 %collective-permute-start.4 = (bf16[128,512]{1,0:T(8,128)(2,1)S(1)}, bf16[128,512]{1,0:T(8,128)(2,1)S(1)}, u32[]{:S(2)}, u32[]{:S(2)}) collective-permute-start(bf16[128,512]{1,0:T(8,128)(2,1)S(1)} %collective-permute-done.3.refs_4_), channel_id=1, source_target_pairs={{0,4},{1,5},{4,8},{5,9},{8,12},{9,13},{12,14},{13,15},{14,10},{15,... | collective-permute-start | bytes 393224 | tf_op jit(solution)/shard_map/ppermute | solution.py:336
  20.6 5.2 %collective-permute-start.7 = (bf16[128,512]{1,0:T(8,128)(2,1)S(1)}, bf16[128,512]{1,0:T(8,128)(2,1)S(1)}, u32[]{:S(2)}, u32[]{:S(2)}) collective-permute-start(bf16[128,512]{1,0:T(8,128)(2,1)S(1)} %collective-permute-done.6.refs_7_), channel_id=1, source_target_pairs={{0,2},{1,3},{4,0},{5,1},{8,4},{9,5},{12,8},{13,9},{14,12},{15,13},... | collective-permute-start | bytes 393224 | tf_op jit(solution)/shard_map/ppermute | solution.py:338
  21.9 9.6 %collective-permute-start.17 = (bf16[128,512]{1,0:T(8,128)(2,1)S(1)}, bf16[128,512]{1,0:T(8,128)(2,1)S(1)}, u32[]{:S(2)}, u32[]{:S(2)}) collective-permute-start(bf16[128,512]{1,0:T(8,128)(2,1)S(1)} %slice.28), channel_id=1, source_target_pairs={{0,2},{1,3},{4,0},{5,1},{8,4},{9,5},{12,8},{13,9},{14,12},{15,13},... | collective-permute-start | bytes 393224 | tf_op jit(solution)/shard_map/ppermute | solution.py:342
  25.3 6.3 %collective-permute-start.16 = (bf16[128,512]{1,0:T(8,128)(2,1)S(1)}, bf16[128,512]{1,0:T(8,128)(2,1)S(1)}, u32[]{:S(2)}, u32[]{:S(2)}) collective-permute-start(bf16[128,512]{1,0:T(8,128)(2,1)S(1)} %collective-permute-done.4.refs_5_), channel_id=1, source_target_pairs={{0,4},{1,5},{4,8},{5,9},{8,12},{9,13},{12,14},{13,15},{14,10},{15,... | collective-permute-start | bytes 393224 | tf_op jit(solution)/shard_map/ppermute | solution.py:341
  32.7 5.2 %collective-permute-start.18 = (bf16[64,4096]{1,0:T(8,128)(2,1)S(1)}, bf16[64,4096]{1,0:T(8,128)(2,1)S(1)}, u32[]{:S(2)}, u32[]{:S(2)}) collective-permute-start(bf16[64,4096]{1,0:T(8,128)(2,1)S(1)} %far_other.1), channel_id=1, source_target_pairs={{0,1},{1,0},{2,3},{3,2},{4,5},{5,4},{6,7},{7,6},{8,9},{9,8},{10,11... | collective-permute-start | bytes 1572872 | tf_op jit(solution)/shard_map/ppermute | solution.py:389
